TPU v7x, 256 devices: a whole 4x4x8 slice. The times are simulated.
256 devices in a mesh: layer: 4 (over z_hi, core), grid: 64 (over z_lo, y, x).
Axes of the slice: x: 4, y: 4, z: 8 (z_hi: 2, z_lo: 4; z = z_hi * 4 + z_lo), core: 2. Of those that a mesh axis runs over, the one named last changes fastest.
Arguments:
- band_blocks: bfloat16 [640, 9, 128, 128], P('grid'), may hold values from -7 to 7, as said below
- retained: int32 [640, 9], P('grid'), may hold values from 0 to 1, as said below
Outputs:
- purified: bfloat16 [640, 9, 128, 128], P('grid', None, 'layer')
Inputs may be any that keep to these rules, and one draw needn't show every extreme that they name: `band_blocks`: the matrix is symmetric: block slot w of block row i equals the transpose of block slot 8 - w of block row (i + w - 4) mod 640. retained[i, w] = 1 exactly when retained[(i + w - 4) mod 640, 8 - w] = 1; the middle slot w = 4 is 1 in every block row.
All inputs are finite; a program needn't handle non-finite values.
Results may differ from a plain program's by a relative error of at most 0.005.
Values may be sent and summed in bfloat16 or wider, within the bound.
No kernel may reach another device: no remote copies, remote signals or barrier semaphores. Data moves between devices by JAX's collectives and lax.ppermute only.
A program may use at most 64 MiB of HBM per device.

v0:
```python
import jax
import jax.numpy as jnp
from jax import lax
from jax.sharding import PartitionSpec as P

STEPS = 2


def extended(block, sides, width):
    for axis, dim in sides:
        count = lax.axis_size(axis)
        forward = [(i, i + 1) for i in range(count - 1)]
        forward.append((count - 1, 0))
        backward = [(target, source) for source, target in forward]
        low = lax.ppermute(
            lax.slice_in_dim(block, block.shape[dim] - width, None, axis=dim), axis, forward
        )
        high = lax.ppermute(lax.slice_in_dim(block, 0, width, axis=dim), axis, backward)
        block = jnp.concatenate([low, block, high], axis=dim)
    return block


def strip_product(left_rows, halo_rows, reach):
    row_count = left_rows.shape[0]
    band_width = left_rows.shape[1]
    padded = jnp.pad(halo_rows, ((0, 0), (reach, reach), (0, 0), (0, 0)))
    running = jnp.zeros(
        (row_count, band_width, left_rows.shape[2], halo_rows.shape[3]), jnp.float32
    )
    for offset in range(band_width):
        source = padded[
            offset : offset + row_count, 2 * reach - offset : 2 * reach - offset + band_width
        ]
        running = running + jnp.einsum(
            "rab,rwbc->rwac", left_rows[:, offset], source, preferred_element_type=jnp.float32
        )
    return running


def per_device(band_blocks, retained):
    layer_count = lax.axis_size("layer")
    share = lax.axis_index("layer")
    band_width = band_blocks.shape[1]
    block_width = band_blocks.shape[2]
    reach = (band_width - 1) // 2
    piece = block_width // layer_count
    kept = (retained != 0)[:, :, None, None]
    whole_rows = jnp.where(kept, band_blocks, jnp.zeros_like(band_blocks))
    quarter = lax.dynamic_slice_in_dim(whole_rows, share * piece, piece, 2)
    for repeat in range(STEPS):
        if repeat > 0:
            whole_rows = lax.all_gather(quarter, "layer", axis=2, tiled=True)
        halo_rows = extended(whole_rows, (("grid", 0),), reach)
        square = jnp.where(kept, strip_product(quarter, halo_rows, reach), 0.0).astype(jnp.bfloat16)
        cube = jnp.where(kept, strip_product(square, halo_rows, reach), 0.0)
        quarter = (
            (3.0 * quarter.astype(jnp.float32) - cube / (4.0 * band_width * block_width)) * 0.5
        ).astype(jnp.bfloat16)
    return quarter


def solution(mesh):
    return jax.shard_map(
        per_device,
        mesh=mesh,
        in_specs=(P("grid", None, None, None), P("grid", None)),
        out_specs=P("grid", None, "layer", None),
        check_vma=False,
    )
```

profile of v0, /device:TPU:1, one launch (start us, length us, event | category | flops | bytes accessed | tf_op | source)
XLA Modules:
  0.0 176.5 jit_solution(6591009244091471911)
XLA Ops:
  6.5 0.7 broadcast_compare_fusion
  7.3 2.1 %copy_select_fusion = bf16[10,9,128,128]{3,2,0,1:T(8,128)(2,1)S(1)} fusion(bf16[10,9,128,128]{3,2,1,0:T(8,128)(2,1)} %param.2, pred[10,9]{0,1:T(8,128)(4,1)S(1)} %copy.3), kind=kLoop, calls=%fused_computation.8 | loop fusion | flops 1474560 | bytes 5898330 | tf_op jit(solution)/shard_map/jit(_where)/select_n | solution.py:48
  9.5 1.6 fusion.94
  11.0 2.0 %collective-permute-start = (bf16[4,9,128,128]{3,2,0,1:T(8,128)(2,1)}, bf16[4,9,128,128]{3,2,0,1:T(8,128)(2,1)}, u32[]{:S(2)}, u32[]{:S(2)}) collective-permute-start(bf16[4,9,128,128]{3,2,0,1:T(8,128)(2,1)} %get-tuple-element.7), channel_id=1, source_target_pairs={{0,1},{1,2},{2,3},{3,4},{4,5},{5,6},{6,7},{7,8},{8,9},{9,10},{10,1... | collective-permute-start | bytes 3538952 | tf_op jit(solution)/shard_map/ppermute | solution.py:15
  13.1 7.8 %collective-permute-start.1 = (bf16[4,9,128,128]{3,2,0,1:T(8,128)(2,1)}, bf16[4,9,128,128]{3,2,0,1:T(8,128)(2,1)}, u32[]{:S(2)}, u32[]{:S(2)}) collective-permute-start(bf16[4,9,128,128]{3,2,0,1:T(8,128)(2,1)} %get-tuple-element.8), channel_id=1, source_target_pairs={{1,0},{2,1},{3,2},{4,3},{5,4},{6,5},{7,6},{8,7},{9,8},{10,9},{11,1... | collective-permute-start | bytes 3538952 | tf_op jit(solution)/shard_map/ppermute | solution.py:18
  20.8 0.6 fusion.83
  21.4 24.9 %collective-permute-done = bf16[4,9,128,128]{3,2,0,1:T(8,128)(2,1)} collective-permute-done((bf16[4,9,128,128]{3,2,0,1:T(8,128)(2,1)}, bf16[4,9,128,128]{3,2,0,1:T(8,128)(2,1)}, u32[]{:S(2)}, u32[]{:S(2)}) %collective-permute-start) | collective-permute-done | bytes 1179680 | tf_op jit(solution)/shard_map/ppermute | solution.py:15
  46.3 4.1 %select_maximum_fusion.2 = bf16[18,17,128,128]{3,2,0,1:T(8,128)(2,1)S(1)} fusion(bf16[4,9,128,128]{3,2,0,1:T(8,128)(2,1)} %collective-permute-done.1, bf16[10,9,128,128]{3,2,0,1:T(8,128)(2,1)S(1)} %copy_select_fusion, bf16[4,9,128,128]{3,2,0,1:T(8,128)(2,1)} %collective-permute-done), kind=kLoop, calls=%fused_computation.5 | loop fusion | flops 60162048 | bytes 15335424 | tf_op jit(solution)/shard_map/concatenate | solution.py:19
  50.4 0.6 fusion.62
  51.0 0.6 fusion.58
  51.5 0.6 fusion.54
  52.1 0.6 fusion.50
  52.7 0.6 fusion.46
  53.2 0.6 fusion.42
  53.8 0.6 fusion.38
  54.4 1.0 fusion.70
  55.9 0.6 fusion.44
  56.5 0.6 fusion.48
  57.0 0.6 fusion.80
  57.6 0.6 fusion.52
  58.1 0.6 fusion.56
  58.7 0.6 fusion.60
  59.3 0.6 fusion.64
  59.8 2.0 %fusion.69 = bf16[10,9,32,128]{3,2,0,1:T(8,128)(2,1)} fusion(f32[10,9,128,32]{2,3,0,1:T(8,128)S(1)} %fusion.40, f32[10,9,128,32]{2,3,0,1:T(8,128)S(1)} %fusion.44, f32[10,9,128,32]{2,3,0,1:T(8,128)S(1)} %fusion.48, f32[10,9,128,32]{2,3,0,1:T(8,128)S(1)} %fusion.80, f32[10,9,128,32]{2,3,0,1:T(8,128)S(1)} %fusion.52, f32[10,9,128,32]{2,3,0,1:T(8,128)S(1)} %fusion.56, ...), kind=kOutput, calls=%fused_computation.78 | convolution fusion | flops 99901440 | bytes 16304132 | tf_op jit(solution)/shard_map/rab,rwbc->rwac/dot_general | solution.py:34
  61.8 55.3 %all-gather.2.cloned.1.call-done = bf16[10,9,128,128]{3,2,0,1:T(8,128)(2,1)} async-done(((bf16[10,9,32,128]{3,2,0,1:T(8,128)(2,1)}), bf16[10,9,128,128]{3,2,0,1:T(8,128)(2,1)}) %all-gather.2.cloned.1.call-update) | async-done | bytes 2949136 | tf_op jit(solution)/shard_map/all_gather | solution.py:52
  117.1 1.9 %fusion.93 = (bf16[4,9,128,128]{3,2,0,1:T(8,128)(2,1)S(1)}, bf16[4,9,128,128]{3,2,0,1:T(8,128)(2,1)S(1)}) fusion(bf16[10,9,128,128]{3,2,0,1:T(8,128)(2,1)} %all-gather.2.cloned.1.call-done), kind=kLoop, calls=%fused_computation.133 | loop fusion | bytes 4718592 | tf_op jit(solution)/shard_map/slice | solution.py:16
  119.1 1.3 collective-permute-start.2
  120.3 6.3 %collective-permute-start.3 = (bf16[4,9,128,128]{3,2,0,1:T(8,128)(2,1)S(1)}, bf16[4,9,128,128]{3,2,0,1:T(8,128)(2,1)S(1)}, u32[]{:S(2)}, u32[]{:S(2)}) collective-permute-start(bf16[4,9,128,128]{3,2,0,1:T(8,128)(2,1)S(1)} %get-tuple-element.6), channel_id=1, source_target_pairs={{1,0},{2,1},{3,2},{4,3},{5,4},{6,5},{7,6},{8,7},{9,8},{10,9},{11,1... | collective-permute-start | bytes 3538952 | tf_op jit(solution)/shard_map/ppermute | solution.py:18
  126.6 0.6 fusion.77
  127.2 25.3 %collective-permute-done.2 = bf16[4,9,128,128]{3,2,0,1:T(8,128)(2,1)S(1)} collective-permute-done((bf16[4,9,128,128]{3,2,0,1:T(8,128)(2,1)S(1)}, bf16[4,9,128,128]{3,2,0,1:T(8,128)(2,1)S(1)}, u32[]{:S(2)}, u32[]{:S(2)}) %collective-permute-start.2) | collective-permute-done | bytes 1179680 | tf_op jit(solution)/shard_map/ppermute | solution.py:15
  152.5 5.6 %select_maximum_fusion = bf16[18,17,128,128]{3,2,0,1:T(8,128)(2,1)S(1)} fusion(bf16[4,9,128,128]{3,2,0,1:T(8,128)(2,1)S(1)} %collective-permute-done.3, bf16[10,9,128,128]{3,2,0,1:T(8,128)(2,1)S(1)} %copy-done, bf16[4,9,128,128]{3,2,0,1:T(8,128)(2,1)S(1)} %collective-permute-done.2), kind=kLoop, calls=%fused_computation.3 | loop fusion | flops 60162048 | bytes 15335424 | tf_op jit(solution)/shard_map/concatenate | solution.py:19
  158.0 0.6 fusion.30
  158.6 0.6 fusion.26
  159.2 0.6 fusion.22
  159.7 0.6 fusion.18
  160.3 0.6 fusion.14
  160.9 0.6 fusion.10
  161.4 0.6 fusion.6
  162.0 1.0 fusion.71
  163.5 0.6 fusion.12
  164.1 0.6 fusion.16
  164.6 0.6 fusion.20
  165.2 0.6 fusion.24
  165.8 0.6 fusion.28
  166.3 0.6 fusion.32
  166.9 0.6 fusion.74
  167.5 1.2 fusion.67
  168.7 0.9 copy.78
  (11 shorter events, 1.3 us)
Async XLA Ops:
  6.5 110.6 %all-gather.2.cloned.1.call-start = ((), (), s32[]{:S(2)}) async-start(), calls=%async_computation | async-start | bytes 3686400 | tf_op jit(solution)/shard_map/all_gather | solution.py:52
  11.0 35.2 %collective-permute-start = (bf16[4,9,128,128]{3,2,0,1:T(8,128)(2,1)}, bf16[4,9,128,128]{3,2,0,1:T(8,128)(2,1)}, u32[]{:S(2)}, u32[]{:S(2)}) collective-permute-start(bf16[4,9,128,128]{3,2,0,1:T(8,128)(2,1)} %get-tuple-element.7), channel_id=1, source_target_pairs={{0,1},{1,2},{2,3},{3,4},{4,5},{5,6},{6,7},{7,8},{8,9},{9,10},{10,1... | collective-permute-start | bytes 3538952 | tf_op jit(solution)/shard_map/ppermute | solution.py:15
  13.1 33.2 %collective-permute-start.1 = (bf16[4,9,128,128]{3,2,0,1:T(8,128)(2,1)}, bf16[4,9,128,128]{3,2,0,1:T(8,128)(2,1)}, u32[]{:S(2)}, u32[]{:S(2)}) collective-permute-start(bf16[4,9,128,128]{3,2,0,1:T(8,128)(2,1)} %get-tuple-element.8), channel_id=1, source_target_pairs={{1,0},{2,1},{3,2},{4,3},{5,4},{6,5},{7,6},{8,7},{9,8},{10,9},{11,1... | collective-permute-start | bytes 3538952 | tf_op jit(solution)/shard_map/ppermute | solution.py:18
  61.8 64.9 %copy-start.1 = (bf16[10,9,32,128]{3,2,0,1:T(8,128)(2,1)S(1)}, bf16[10,9,32,128]{3,2,0,1:T(8,128)(2,1)}, u32[]{:S(2)}) copy-start(bf16[10,9,32,128]{3,2,0,1:T(8,128)(2,1)} %fusion.69) | copy-start | bytes 2211844
  117.1 9.5 %copy-start = (bf16[10,9,128,128]{3,2,0,1:T(8,128)(2,1)S(1)}, bf16[10,9,128,128]{3,2,0,1:T(8,128)(2,1)}, u32[]{:S(2)}) copy-start(bf16[10,9,128,128]{3,2,0,1:T(8,128)(2,1)} %all-gather.2.cloned.1.call-done) | copy-start | bytes 8847364
  119.1 33.4 %collective-permute-start.2 = (bf16[4,9,128,128]{3,2,0,1:T(8,128)(2,1)S(1)}, bf16[4,9,128,128]{3,2,0,1:T(8,128)(2,1)S(1)}, u32[]{:S(2)}, u32[]{:S(2)}) collective-permute-start(bf16[4,9,128,128]{3,2,0,1:T(8,128)(2,1)S(1)} %get-tuple-element.5), channel_id=1, source_target_pairs={{0,1},{1,2},{2,3},{3,4},{4,5},{5,6},{6,7},{7,8},{8,9},{9,10},{10,1... | collective-permute-start | bytes 3538952 | tf_op jit(solution)/shard_map/ppermute | solution.py:15
  120.3 32.1 %collective-permute-start.3 = (bf16[4,9,128,128]{3,2,0,1:T(8,128)(2,1)S(1)}, bf16[4,9,128,128]{3,2,0,1:T(8,128)(2,1)S(1)}, u32[]{:S(2)}, u32[]{:S(2)}) collective-permute-start(bf16[4,9,128,128]{3,2,0,1:T(8,128)(2,1)S(1)} %get-tuple-element.6), channel_id=1, source_target_pairs={{1,0},{2,1},{3,2},{4,3},{5,4},{6,5},{7,6},{8,7},{9,8},{10,9},{11,1... | collective-permute-start | bytes 3538952 | tf_op jit(solution)/shard_map/ppermute | solution.py:18
Sparse Core Ops, SparseCore 0:
  61.9 55.1 all-gather.1
where the time goes:
time: 177 us; the launch traced here: 176 us
  waiting for transfers between devices  105 us (59%)
  matrix products  23.1 us (13%)
  starting transfers between devices  17.4 us (10%)
  between operations  13.5 us (8%)
  other arithmetic  12.5 us (7%)
  local copies, waits for them, and re-layouts  4.53 us (3%)
    all_gather x1, waiting for transfers between devices, per_device(): whole_rows = lax.all_gather(quarter, 'layer', axis=2, tiled=True)  55.3 us
    ppermute x2, waiting for transfers between devices, extended(): lax.ppermute(lax.slice_in_dim(block, block.shape[dim] - width, None, axis...  50.1 us
    dot_general x36, matrix products, strip_product(): jnp.einsum('rab,rwbc->rwac', left_rows[:, offset], source, preferred_elem...  23.1 us
    ppermute x2, starting transfers between devices, extended(): lax.ppermute(lax.slice_in_dim(block, 0, width, axis=dim), axis, backward)  14.1 us
    concatenate x2, other arithmetic, extended(): block = jnp.concatenate([low, block, high], axis=dim)  9.7 us
  transfers between devices with their start and end apart: 5, of which 3 were waited for; matrix products, arithmetic and copies ran while one was open for 1% of the time, Pallas kernels for 0%

commit v1 on v0

v1 whole, which is shorter than its diff:
```python
import jax
import jax.numpy as jnp
from jax import lax
from jax.experimental import pallas as pl
from jax.experimental.pallas import tpu as pltpu
from jax.sharding import PartitionSpec as P

B = 128
T = 256
R = 10
W = 9
SHARE = 32
SCALE = 1.0 / (4.0 * W * B)
BF = jnp.bfloat16
F32 = jnp.float32

HALO = [(h, c) for h in range(8) for c in range(max(0, h - 4), h + 1)]
HALO_AT = {hc: n for n, hc in enumerate(HALO)}
NH = len(HALO)

ANY = pl.BlockSpec(memory_space=pl.ANY)
VM = pl.BlockSpec(memory_space=pltpu.VMEM)
SM = pl.BlockSpec(memory_space=pltpu.SMEM)


def nt(a, b):
    return lax.dot_general(a, b, (((1,), (1,)), ((), ())), preferred_element_type=F32)


def nn(a, b):
    return lax.dot_general(a, b, (((1,), (0,)), ((), ())), preferred_element_type=F32)


def flip_core():
    return lax.rem(lax.axis_index("layer"), 2)


def own_mask(ret, flip, i, j):
    if not 0 <= i < R:
        i, j = j, i
    w = j - i + 4
    row = jnp.where(flip == 1, R - 1 - i, i)
    slot = jnp.where(flip == 1, W - 1 - w, w)
    return (ret[row, slot] != 0).astype(F32)


def eye():
    r = lax.broadcasted_iota(jnp.int32, (T, T), 0)
    c = lax.broadcasted_iota(jnp.int32, (T, T), 1)
    return (r == c).astype(F32).astype(BF)


def quads(tile, I, J, mask):
    for a in range(2):
        for b in range(2):
            i, j = 2 * I + a, 2 * J + b
            q = tile[a * B : (a + 1) * B, b * B : (b + 1) * B]
            yield a, b, (q * mask(i, j) if abs(i - j) <= 4 else None)


def put_masked(store, tile, I, J, mask):
    for a, b, q in quads(tile, I, J, mask):
        store(a, b, jnp.zeros((B, B), BF) if q is None else q.astype(BF))


def put_step(store, x, cube, I, J, mask):
    for a, b, q in quads(cube, I, J, mask):
        if q is None:
            store(a, b, jnp.zeros((B, B), BF))
        else:
            xq = x[a * B : (a + 1) * B, b * B : (b + 1) * B].astype(F32)
            store(a, b, ((3.0 * xq - q * SCALE) * 0.5).astype(BF))


def at(ref, *lead):
    def store(a, b, v):
        ref[(*lead, pl.ds(a * B, B), pl.ds(b * B, B))] = v

    return store


def payload_kernel(x, ret, out, buf, sem):
    flip = flip_core()
    copies = []
    for n, (h, c) in enumerate(HALO):
        i, w = h + 2, c - h + 4
        row = jnp.where(flip == 1, R - 1 - i, i)
        slot = jnp.where(flip == 1, W - 1 - w, w)
        cp = pltpu.make_async_copy(x.at[row, slot], buf.at[n], sem.at[n])
        cp.start()
        copies.append(cp)
    for n, (h, c) in enumerate(HALO):
        m = own_mask(ret, flip, h + 2, c + 2)
        out[NH, pl.ds(n, 1), :] = jnp.full((1, B), m, F32).astype(BF)
    out[NH, pl.ds(NH, B - NH), :] = jnp.zeros((B - NH, B), BF)
    for n, (h, c) in enumerate(HALO):
        copies[n].wait()
        m = own_mask(ret, flip, h + 2, c + 2)
        out[n] = (buf[n].astype(F32) * m).astype(BF)


def payload(x, ret):
    return pl.pallas_call(
        payload_kernel,
        out_shape=jax.ShapeDtypeStruct((NH + 1, B, B), BF),
        in_specs=[ANY, SM],
        out_specs=VM,
        scratch_shapes=[pltpu.VMEM((NH, B, B), BF), pltpu.SemaphoreType.DMA((NH,))],
        name="payload",
    )(x, ret)


D1_EARLY = [(0, 2), (2, 0), (1, 2), (2, 1), (2, 2), (1, 3), (3, 1), (2, 3), (3, 2), (2, 4), (4, 2)]
D1_CORNER = [(0, 0), (0, 1), (1, 0), (1, 1)]


def early_kernel(x, ret, xb01, xt, s4, acc, d1, xb, sb):
    flip = flip_core()

    def mask(i, j):
        return own_mask(ret, flip, i, j)

    for I in range(5):
        xb[I, pl.ds(0, B), pl.ds(9 * B, B)] = jnp.zeros((B, B), BF)
        xb[I, pl.ds(B, B), pl.ds(0, B)] = jnp.zeros((B, B), BF)
        for a in range(2):
            for w in range(W):
                i = 2 * I + a
                row = jnp.where(flip == 1, R - 1 - i, i)
                slot = jnp.where(flip == 1, W - 1 - w, w)
                v = x[row, slot].astype(F32) * mask(i, i + w - 4)
                xb[I, pl.ds(a * B, B), pl.ds((a + w) * B, B)] = v.astype(BF)

    def xs(I, lo, hi):
        return xb[I, :, pl.ds((lo - I + 2) * T, (hi - lo + 1) * T)]

    def ss(I, lo, hi):
        return sb[I, :, pl.ds((lo - I + 2) * T, (hi - lo + 1) * T)]

    one = eye()
    xb01[...] = xb[pl.ds(0, 2)]
    for n, (I, K) in enumerate([(0, -2), (0, -1), (1, -1)]):
        xt[n] = nt(one, xs(I, K, K)).astype(BF)

    for I in range(5):
        for J in range(I, min(I + 3, 5)):
            lo, hi = J - 2, I + 2
            s = nt(xs(I, lo, hi), xs(J, lo, hi))

            def store(a, b, v, I=I, J=J):
                sb[I, pl.ds(a * B, B), pl.ds((J - I + 2) * T + b * B, B)] = v

            put_masked(store, s, I, J, mask)
            if J > I:
                sb[J, :, pl.ds((I - J + 2) * T, T)] = nt(one, ss(I, J, J)).astype(BF)

    for n, (I, J) in enumerate(D1_CORNER):
        s4[n] = ss(I, J, J)
        lo, hi = max(0, I - 2, J - 2), min(I, J) + 2
        acc[n] = nt(ss(I, lo, hi), xs(J, lo, hi))

    for I, J in D1_EARLY:
        lo, hi = max(I, J) - 2, min(I, J) + 2
        cube = nt(ss(I, lo, hi), xs(J, lo, hi))

        def store(a, b, v, I=I, J=J):
            d1[J + 2, pl.ds((I - J + 2) * T + a * B, B), pl.ds(b * B, B)] = v

        put_step(store, xs(I, J, J), cube, I, J, mask)


def early(x, ret):
    return pl.pallas_call(
        early_kernel,
        out_shape=[
            jax.ShapeDtypeStruct((2, T, 5 * T), BF),
            jax.ShapeDtypeStruct((3, T, T), BF),
            jax.ShapeDtypeStruct((4, T, T), BF),
            jax.ShapeDtypeStruct((4, T, T), F32),
            jax.ShapeDtypeStruct((7, 5 * T, T), BF),
        ],
        in_specs=[VM, SM],
        out_specs=[VM] * 5,
        scratch_shapes=[pltpu.VMEM((5, T, 5 * T), BF), pltpu.VMEM((5, T, 5 * T), BF)],
        compiler_params=pltpu.CompilerParams(vmem_limit_bytes=40 * 2**20),
        cost_estimate=pl.CostEstimate(flops=2 * 110 * T * T * T, bytes_accessed=12 * 2**20, transcendentals=0),
        name="early",
    )(x, ret)


def halo_mask(ret, flip, hal):
    def mask(i, j):
        if 0 <= i < R or 0 <= j < R:
            return own_mask(ret, flip, i, j)
        h, c = max(i, j) + 8, min(i, j) + 8
        return hal[NH, pl.ds(HALO_AT[h, c], 1), :].astype(F32)

    return mask


def unpack(hal, xh, lowest, one):
    for I in range(lowest, 0):
        for J in range(max(I - 2, lowest), I + 1):
            for a in range(2):
                for b in range(2):
                    h, c = 2 * I + a + 8, 2 * J + b + 8
                    dst = (I + 4, pl.ds(a * B, B), pl.ds((J - I + 2) * T + b * B, B))
                    if abs(h - c) > 4:
                        xh[dst] = jnp.zeros((B, B), BF)
                    elif c <= h:
                        xh[dst] = hal[HALO_AT[h, c]]
                    else:
                        xh[dst] = nt(one[:B, :B], hal[HALO_AT[c, h]]).astype(BF)
            if J < I:
                tile = xh[I + 4, :, pl.ds((J - I + 2) * T, T)]
                xh[J + 4, :, pl.ds((I - J + 2) * T, T)] = nt(one, tile).astype(BF)


def put_cross(xh, xt):
    xh[2, :, pl.ds(4 * T, T)] = xt[0]
    xh[3, :, pl.ds(3 * T, T)] = xt[1]
    xh[3, :, pl.ds(4 * T, T)] = xt[2]


S_CROSS = [(0, -2), (0, -1), (1, -1)]


def corner_kernel(hal, xb01, xt, acc, ret, s3, x1c, xh):
    flip = flip_core()
    mask = halo_mask(ret, flip, hal)
    one = eye()
    unpack(hal, xh, -2, one)
    put_cross(xh, xt)

    def xs(I, lo, hi):
        if I >= 0:
            return xb01[I, :, pl.ds((lo - I + 2) * T, (hi - lo + 1) * T)]
        return xh[I + 4, :, pl.ds((lo - I + 2) * T, (hi - lo + 1) * T)]

    for n, (I, J) in enumerate(S_CROSS):
        lo, hi = I - 2, J + 2
        put_masked(at(s3, n), nt(xs(I, lo, hi), xs(J, lo, hi)), I, J, mask)
    terms = {
        (0, 0): [(0, -2), (1, -1)],
        (0, 1): [(1, -1)],
        (1, 0): [(2, -1)],
        (1, 1): [(2, -1)],
    }
    for n, (I, J) in enumerate(D1_CORNER):
        cube = acc[n]
        for k, m in terms[I, J]:
            cube = cube + nt(s3[k], xs(J, m, m))
        put_step(at(x1c, n), xs(I, J, J), cube, I, J, mask)


def corner(hal, xb01, xt, acc, ret):
    return pl.pallas_call(
        corner_kernel,
        out_shape=[jax.ShapeDtypeStruct((3, T, T), BF), jax.ShapeDtypeStruct((4, T, T), BF)],
        in_specs=[VM, VM, VM, VM, SM],
        out_specs=[VM, VM],
        scratch_shapes=[pltpu.VMEM((4, T, 5 * T), BF)],
        compiler_params=pltpu.CompilerParams(vmem_limit_bytes=24 * 2**20),
        cost_estimate=pl.CostEstimate(flops=2 * 20 * T * T * T, bytes_accessed=4 * 2**20, transcendentals=0),
        name="corner",
    )(hal, xb01, xt, acc, ret)


D1_HALO = [(-2, -2), (-2, -1), (-1, -2), (-1, -1), (-2, 0), (0, -2), (-1, 0), (0, -1), (-1, 1), (1, -1)]


def halo_kernel(hal, xb01, xt, s4, s3, ret, d1_in, d1, xh, sb):
    del d1_in
    flip = flip_core()
    mask = halo_mask(ret, flip, hal)
    one = eye()
    unpack(hal, xh, -4, one)
    put_cross(xh, xt)

    def xs(I, lo, hi):
        if I >= 0:
            return xb01[I, :, pl.ds((lo - I + 2) * T, (hi - lo + 1) * T)]
        return xh[I + 4, :, pl.ds((lo - I + 2) * T, (hi - lo + 1) * T)]

    def spos(I, J):
        return (I + 2, slice(None), pl.ds((J - I + 2) * T, T))

    def ss(I, lo, hi):
        return sb[I + 2, :, pl.ds((lo - I + 2) * T, (hi - lo + 1) * T)]

    for n, (I, J) in enumerate(D1_CORNER):
        sb[spos(I, J)] = s4[n]
    for n, (I, J) in enumerate(S_CROSS):
        sb[spos(I, J)] = s3[n]
        sb[spos(J, I)] = nt(one, s3[n]).astype(BF)
    for I, J in [(-1, -1), (-2, -2), (-1, -2), (-1, -3), (-2, -3), (-2, -4)]:
        lo, hi = I - 2, J + 2
        if I == -2:
            lo = -4
        if J < -2:
            hi = J + 2

        def store(a, b, v, I=I, J=J):
            sb[I + 2, pl.ds(a * B, B), pl.ds((J - I + 2) * T + b * B, B)] = v

        put_masked(store, nt(xs(I, lo, hi), xs(J, lo, hi)), I, J, mask)
    sb[spos(-2, -1)] = nt(one, ss(-1, -2, -2)).astype(BF)

    for I, J in D1_HALO:
        lo, hi = max(I, J) - 2, min(I, J) + 2
        cube = nt(ss(I, lo, hi), xs(J, lo, hi))

        def store(a, b, v, I=I, J=J):
            d1[J + 2, pl.ds((I - J + 2) * T + a * B, B), pl.ds(b * B, B)] = v

        put_step(store, xs(I, J, J), cube, I, J, mask)


def halo(hal, xb01, xt, s4, s3, ret, d1):
    return pl.pallas_call(
        halo_kernel,
        out_shape=jax.ShapeDtypeStruct((7, 5 * T, T), BF),
        in_specs=[VM, VM, VM, VM, VM, SM, VM],
        out_specs=VM,
        scratch_shapes=[pltpu.VMEM((4, T, 5 * T), BF), pltpu.VMEM((4, T, 5 * T), BF)],
        input_output_aliases={6: 0},
        compiler_params=pltpu.CompilerParams(vmem_limit_bytes=32 * 2**20),
        cost_estimate=pl.CostEstimate(flops=2 * 80 * T * T * T, bytes_accessed=9 * 2**20, transcendentals=0),
        name="halo",
    )(hal, xb01, xt, s4, s3, ret, d1)


H = R // 2
Q = 2 * SHARE


def second_kernel(d1_in, x1c, x1p, ret, full, send, d1, left, s1):
    layer = lax.axis_index("layer")
    flip = lax.rem(layer, 2)
    chip_rows = pl.multiple_of(lax.div(layer, 2) * Q, Q)

    for J in range(-2, 5):
        for K in range(max(J - 2, -2), min(J + 2, 4) + 1):
            dst = (J + 2, pl.ds((K - J + 2) * T, T))
            if (K, J) in D1_CORNER:
                d1[dst] = x1c[D1_CORNER.index((K, J))]
            elif (4 - K, 4 - J) in D1_CORNER:
                n = D1_CORNER.index((4 - K, 4 - J))
                for a in range(2):
                    for b in range(2):
                        d1[J + 2, pl.ds((K - J + 2) * T + a * B, B), pl.ds(b * B, B)] = x1p[
                            n, pl.ds((1 - a) * B, B), pl.ds((1 - b) * B, B)
                        ]
            else:
                d1[dst] = d1_in[dst]

    for i in range(H):
        I, a = i // 2, i % 2
        for J in range(-2, 5):
            dst = (pl.ds(i * Q, Q), pl.ds((J + 2) * T, T))
            if abs(I - J) <= 2:
                left[dst] = d1[J + 2, pl.ds((I - J + 2) * T + a * B + chip_rows, Q), :]
            else:
                left[dst] = jnp.zeros((Q, T), BF)

    def mask(i, j):
        return own_mask(ret, flip, i, j)

    def product(lhs, J):
        i0, i1 = max(0, 2 * J - 4), min(H - 1, 2 * J + 5)
        k0, k1 = max(J - 2, -2), min(J + 2, 4)
        a = lhs[pl.ds(i0 * Q, (i1 - i0 + 1) * Q), pl.ds((k0 + 2) * T, (k1 - k0 + 1) * T)]
        return i0, i1, nn(a, d1[J + 2, pl.ds((k0 - J + 2) * T, (k1 - k0 + 1) * T), :])

    for J in range(-2, 5):
        i0, i1, s = product(left, J)
        for i in range(H):
            for b in range(2):
                j = 2 * J + b
                dst = (pl.ds(i * Q, Q), pl.ds((J + 2) * T + b * B, B))
                if abs(i - j) <= 4 and i0 <= i <= i1:
                    q = s[(i - i0) * Q : (i - i0 + 1) * Q, b * B : (b + 1) * B]
                    s1[dst] = (q * mask(i, j)).astype(BF)
                else:
                    s1[dst] = jnp.zeros((Q, B), BF)

    for J in range(-2, 5):
        i0, i1, cube = product(s1, J)
        for i in range(i0, i1 + 1):
            for b in range(2):
                j = 2 * J + b
                if abs(i - j) > 4:
                    continue
                q = cube[(i - i0) * Q : (i - i0 + 1) * Q, b * B : (b + 1) * B] * mask(i, j)
                x = left[pl.ds(i * Q, Q), pl.ds((J + 2) * T + b * B, B)].astype(F32)
                v = ((3.0 * x - q * SCALE) * 0.5).astype(BF)
                w = j - i + 4
                row = jnp.where(flip == 1, R - 1 - i, i)
                near = jnp.where(flip == 1, H - 1 - i, i)
                slot = jnp.where(flip == 1, W - 1 - w, w)
                lo, hi = v[:SHARE], v[SHARE:]
                full[row, slot] = jnp.where(flip == 1, hi, lo)
                send[near, slot] = jnp.where(flip == 1, lo, hi)


def second(d1, x1c, x1p, ret):
    return pl.pallas_call(
        second_kernel,
        out_shape=[
            jax.ShapeDtypeStruct((R, W, SHARE, B), BF),
            jax.ShapeDtypeStruct((H, W, SHARE, B), BF),
        ],
        in_specs=[VM, VM, VM, SM],
        out_specs=[VM, VM],
        scratch_shapes=[
            pltpu.VMEM((7, 5 * T, T), BF),
            pltpu.VMEM((H * Q, 7 * T), BF),
            pltpu.VMEM((H * Q, 7 * T), BF),
        ],
        compiler_params=pltpu.CompilerParams(vmem_limit_bytes=32 * 2**20),
        cost_estimate=pl.CostEstimate(flops=2 * 58 * T * T * T, bytes_accessed=7 * 2**20, transcendentals=0),
        name="second",
    )(d1, x1c, x1p, ret)


def chain(layers, grid):
    pairs = []
    for l in range(layers):
        for g in range(grid):
            t = g + 1 if l % 2 == 0 else g - 1
            k = l if 0 <= t < grid else (l + 2) % layers
            pairs.append((l * grid + g, k * grid + t % grid))
    return pairs


def per_device(x, ret):
    layers, grid = lax.axis_size("layer"), lax.axis_size("grid")
    cores = [(l, l ^ 1) for l in range(layers)]
    flip = lax.rem(lax.axis_index("layer"), 2)
    hal = lax.ppermute(payload(x, ret), ("layer", "grid"), chain(layers, grid))
    xb01, xt, s4, acc, d1 = early(x, ret)
    s3, x1c = corner(hal, xb01, xt, acc, ret)
    x1p = lax.ppermute(x1c, "layer", cores)
    d1 = halo(hal, xb01, xt, s4, s3, ret, d1)
    full, send = second(d1, x1c, x1p, ret)
    other = lax.ppermute(send, "layer", cores)
    return lax.dynamic_update_slice(full, other, (jnp.where(flip == 1, 0, H), 0, 0, 0))


def solution(mesh):
    return jax.shard_map(
        per_device,
        mesh=mesh,
        in_specs=(P("grid", None, None, None), P("grid", None)),
        out_specs=P("grid", None, "layer", None),
        check_vma=False,
    )
```

time: 177 us -> 40.2 us (0.23)
  waiting for transfers between devices: 105 us -> 5.56 us
  matrix products: 23.1 us -> 0 us
  Pallas kernels: 0 us -> 17.8 us
  between operations: 13.5 us -> 0.04 us
  other arithmetic: 12.5 us -> 0 us
  starting transfers between devices: 17.4 us -> 13.1 us
    all_gather x1 -> x0, waiting for transfers between devices: 55.3 us -> none  [per_device(): whole_rows = lax.all_gather(quarter, 'layer', axis=2, tiled=True)]
    ppermute x4 -> x3, waiting for transfers between devices: 50.1 us -> 5.56 us  [the longest x1 3.89 us: per_device(): hal = lax.ppermute(payload(x, ret), ('layer', 'grid'), chain(layers, grid))]
    dot_general x36 -> x0, matrix products: 23.1 us -> none  [strip_product(): jnp.einsum('rab,rwbc->rwac', left_rows[:, offset], source, preferred_elem...]
    pallas_call x0 -> x5, Pallas kernels: none -> 17.8 us  [the longest x1 5.28 us: early(): pl.pallas_call(early_kernel, out_shape=[jax.ShapeDtypeStruct((2, T, 5 * T...]
    concatenate x2 -> x0, other arithmetic: 9.7 us -> none  [extended(): block = jnp.concatenate([low, block, high], axis=dim)]
    ppermute x4 -> x3, starting transfers between devices: 17.4 us -> 13.1 us  [the longest x1 11.1 us: per_device(): hal = lax.ppermute(payload(x, ret), ('layer', 'grid'), chain(layers, grid))]
    slice x2 -> x0, local copies, waits for them, and re-layouts: 3.5 us -> none  [extended(): lax.slice_in_dim(block, block.shape[dim] - width, None, axis=dim)]
    unnamed x4, local copies, waits for them, and re-layouts: 0.01 us -> 2.53 us
  transfers between devices with their start and end apart: 5 -> 3, of which waited for: 3 -> 2; matrix products, arithmetic and copies ran while one was open for 1% -> 0% of each run, Pallas kernels for 0% -> 22%
where the time goes in v1:
time: 40.2 us; the launch traced here: 39.9 us
  Pallas kernels  17.8 us (44%)
  starting transfers between devices  13.1 us (33%)
  waiting for transfers between devices  5.56 us (14%)
  local copies, waits for them, and re-layouts  3.29 us (8%)
    ppermute x1, starting transfers between devices, per_device(): hal = lax.ppermute(payload(x, ret), ('layer', 'grid'), chain(layers, grid))  11.1 us
    pallas_call x1, Pallas kernels, early(): pl.pallas_call(early_kernel, out_shape=[jax.ShapeDtypeStruct((2, T, 5 * T...  5.28 us
    pallas_call x1, Pallas kernels, second(): pl.pallas_call(second_kernel, out_shape=[jax.ShapeDtypeStruct((R, W, SHAR...  4.01 us
    ppermute x1, waiting for transfers between devices, per_device(): hal = lax.ppermute(payload(x, ret), ('layer', 'grid'), chain(layers, grid))  3.89 us
    pallas_call x1, Pallas kernels, halo(): pl.pallas_call(halo_kernel, out_shape=jax.ShapeDtypeStruct((7, 5 * T, T),...  3.61 us
    pallas_call x1, Pallas kernels, payload(): pl.pallas_call(payload_kernel, out_shape=jax.ShapeDtypeStruct((NH + 1, B,...  3.26 us
    unnamed x4, local copies, waits for them, and re-layouts  2.53 us
    ppermute x1, starting transfers between devices, per_device(): x1p = lax.ppermute(x1c, 'layer', cores)  1.97 us
  transfers between devices with their start and end apart: 3, of which 2 were waited for; matrix products, arithmetic and copies ran while one was open for 0% of the time, Pallas kernels for 22%

profile of v1, /device:TPU:1, one launch (start us, length us, event | category | flops | bytes accessed | tf_op | source)
XLA Modules:
  0.0 39.9 jit_solution(9492428818314200657)
XLA Ops:
  0.0 3.3 %payload.1 = bf16[31,128,128]{2,1,0:T(8,128)(2,1)} custom-call(bf16[10,9,128,128]{3,2,1,0:T(8,128)(2,1)} %x.3, s32[10,9]{1,0:T(8,128)} %ret.9), custom_call_target="tpu_custom_call" | custom-call | tf_op jit(solution)/shard_map/payload/pallas_call | solution.py:103
  3.3 11.1 %collective-permute-start = (bf16[31,128,128]{2,1,0:T(8,128)(2,1)}, bf16[31,128,128]{2,1,0:T(8,128)(2,1)S(1)}, u32[]{:S(2)}, u32[]{:S(2)}) collective-permute-start(bf16[31,128,128]{2,1,0:T(8,128)(2,1)} %payload.1), channel_id=1, source_target_pairs={{0,1},{1,2},{2,3},{3,4},{4,5},{5,6},{6,7},{7,8},{8,9},{9,10},{10,1... | collective-permute-start | bytes 3047432 | tf_op jit(solution)/shard_map/ppermute | solution.py:440
  14.4 0.0 copy-start
  14.4 1.8 %copy-done = bf16[10,9,128,128]{3,2,1,0:T(8,128)(2,1)S(1)} copy-done((bf16[10,9,128,128]{3,2,1,0:T(8,128)(2,1)S(1)}, bf16[10,9,128,128]{3,2,1,0:T(8,128)(2,1)}, u32[]{:S(2)}) %copy-start) | copy-done | bytes 2949144
  16.2 0.0 copy-start.1
  16.2 0.7 %copy-done.1 = s32[10,9]{1,0:T(8,128)S(1)} copy-done((s32[10,9]{1,0:T(8,128)S(1)}, s32[10,9]{1,0:T(8,128)}, u32[]{:S(2)}) %copy-start.1) | copy-done | bytes 384
  16.9 5.3 %early.1 = (bf16[2,256,1280]{2,1,0:T(8,128)(2,1)S(1)}, bf16[3,256,256]{2,1,0:T(8,128)(2,1)S(1)}, bf16[4,256,256]{2,1,0:T(8,128)(2,1)S(1)}, f32[4,256,256]{2,1,0:T(8,128)S(1)}, bf16[7,1280,256]{2,1,0:T(8,128)(2,1)S(1)}) custom-call(bf16[10,9,128,128]{3,2,1,0:T(8,128)(2,1)S(1)} %copy-done, s32[10,9]{1,0:T(8,128)S(1)} %copy-done.1), custom_call_target="tpu_custom_call" | custom-call | flops 3690987520 | bytes 12582912 | tf_op jit(solution)/shard_map/early/pallas_call | solution.py:173
  22.2 3.9 %collective-permute-done.hal = bf16[31,128,128]{2,1,0:T(8,128)(2,1)S(1)} collective-permute-done((bf16[31,128,128]{2,1,0:T(8,128)(2,1)}, bf16[31,128,128]{2,1,0:T(8,128)(2,1)S(1)}, u32[]{:S(2)}, u32[]{:S(2)}) %collective-permute-start) | collective-permute-done | bytes 1015840 | tf_op jit(solution)/shard_map/ppermute | solution.py:440
  26.1 1.7 %corner.1 = (bf16[3,256,256]{2,1,0:T(8,128)(2,1)S(1)}, bf16[4,256,256]{2,1,0:T(8,128)(2,1)S(1)}) custom-call(bf16[31,128,128]{2,1,0:T(8,128)(2,1)S(1)} %collective-permute-done.hal, bf16[2,256,1280]{2,1,0:T(8,128)(2,1)S(1)} %get-tuple-element.14.xb01, bf16[3,256,256]{2,1,0:T(8,128)(2,1)S(1)} %get-tuple-element.15.xt, ...), custom_call_target="tpu_custom_call" | custom-call | flops 671088640 | bytes 4194304 | tf_op jit(solution)/shard_map/corner/pallas_call | solution.py:257
  27.8 2.0 %collective-permute-start.1 = (bf16[4,256,256]{2,1,0:T(8,128)(2,1)S(1)}, bf16[4,256,256]{2,1,0:T(8,128)(2,1)S(1)}, u32[]{:S(2)}, u32[]{:S(2)}) collective-permute-start(bf16[4,256,256]{2,1,0:T(8,128)(2,1)S(1)} %get-tuple-element.20.x1c), channel_id=1, source_target_pairs={{0,64},{64,0},{128,192},{192,128},{1,65},{65,1},{129,193},{193,129... | collective-permute-start | bytes 1572872 | tf_op jit(solution)/shard_map/ppermute | solution.py:443
  29.8 3.6 %halo.1.d1_in = bf16[7,1280,256]{2,1,0:T(8,128)(2,1)S(1)} custom-call(bf16[31,128,128]{2,1,0:T(8,128)(2,1)S(1)} %collective-permute-done.hal, bf16[2,256,1280]{2,1,0:T(8,128)(2,1)S(1)} %get-tuple-element.14.xb01, bf16[3,256,256]{2,1,0:T(8,128)(2,1)S(1)} %get-tuple-element.15.xt, ...), custom_call_target="tpu_custom_call", output_to_operand_aliasing={{}: (6, {})} | custom-call | flops 2684354560 | bytes 9437184 | tf_op jit(solution)/shard_map/halo/pallas_call | solution.py:320
  33.4 0.0 collective-permute-done.1.x1p
  33.4 4.0 %second.1 = (bf16[10,9,32,128]{3,2,1,0:T(8,128)(2,1)}, bf16[5,9,32,128]{3,2,1,0:T(8,128)(2,1)S(1)}) custom-call(bf16[7,1280,256]{2,1,0:T(8,128)(2,1)S(1)} %halo.1.d1_in, bf16[4,256,256]{2,1,0:T(8,128)(2,1)S(1)} %get-tuple-element.20.x1c, bf16[4,256,256]{2,1,0:T(8,128)(2,1)S(1)} %collective-permute-done.1.x1p, s32[10,9]{1,0:T(8,128)S(1)} %copy-done.1), custom_call_target="tpu_custom_call" | custom-call | flops 1946157056 | bytes 7340032 | tf_op jit(solution)/shard_map/second/pallas_call | solution.py:407
  37.4 0.0 collective-permute-start.2
  37.4 1.7 %collective-permute-done.2 = bf16[5,9,32,128]{3,2,1,0:T(8,128)(2,1)S(1)} collective-permute-done((bf16[5,9,32,128]{3,2,1,0:T(8,128)(2,1)S(1)}, bf16[5,9,32,128]{3,2,1,0:T(8,128)(2,1)S(1)}, u32[]{:S(2)}, u32[]{:S(2)}) %collective-permute-start.2) | collective-permute-done | bytes 368672 | tf_op jit(solution)/shard_map/ppermute | solution.py:446
  39.1 0.8 %constant_dynamic-update-slice_fusion = bf16[10,9,32,128]{3,2,1,0:T(8,128)(2,1)} fusion(bf16[10,9,32,128]{3,2,1,0:T(8,128)(2,1)} %get-tuple-element.21, bf16[5,9,32,128]{3,2,1,0:T(8,128)(2,1)S(1)} %collective-permute-done.2, s32[]{:T(128)S(6)} %select_n.5), kind=kLoop, calls=%fused_computation | loop fusion | bytes 737284 | tf_op jit(solution)/shard_map/dynamic_update_slice | solution.py:447
Async XLA Ops:
  3.3 22.8 %collective-permute-start = (bf16[31,128,128]{2,1,0:T(8,128)(2,1)}, bf16[31,128,128]{2,1,0:T(8,128)(2,1)S(1)}, u32[]{:S(2)}, u32[]{:S(2)}) collective-permute-start(bf16[31,128,128]{2,1,0:T(8,128)(2,1)} %payload.1), channel_id=1, source_target_pairs={{0,1},{1,2},{2,3},{3,4},{4,5},{5,6},{6,7},{7,8},{8,9},{9,10},{10,1... | collective-permute-start | bytes 3047432 | tf_op jit(solution)/shard_map/ppermute | solution.py:440
  14.4 1.8 %copy-start = (bf16[10,9,128,128]{3,2,1,0:T(8,128)(2,1)S(1)}, bf16[10,9,128,128]{3,2,1,0:T(8,128)(2,1)}, u32[]{:S(2)}) copy-start(bf16[10,9,128,128]{3,2,1,0:T(8,128)(2,1)} %x.3) | copy-start | bytes 8847364
  16.2 0.7 %copy-start.1 = (s32[10,9]{1,0:T(8,128)S(1)}, s32[10,9]{1,0:T(8,128)}, u32[]{:S(2)}) copy-start(s32[10,9]{1,0:T(8,128)} %ret.9) | copy-start | bytes 1084
  27.8 5.6 %collective-permute-start.1 = (bf16[4,256,256]{2,1,0:T(8,128)(2,1)S(1)}, bf16[4,256,256]{2,1,0:T(8,128)(2,1)S(1)}, u32[]{:S(2)}, u32[]{:S(2)}) collective-permute-start(bf16[4,256,256]{2,1,0:T(8,128)(2,1)S(1)} %get-tuple-element.20.x1c), channel_id=1, source_target_pairs={{0,64},{64,0},{128,192},{192,128},{1,65},{65,1},{129,193},{193,129... | collective-permute-start | bytes 1572872 | tf_op jit(solution)/shard_map/ppermute | solution.py:443
  37.4 1.7 %collective-permute-start.2 = (bf16[5,9,32,128]{3,2,1,0:T(8,128)(2,1)S(1)}, bf16[5,9,32,128]{3,2,1,0:T(8,128)(2,1)S(1)}, u32[]{:S(2)}, u32[]{:S(2)}) collective-permute-start(bf16[5,9,32,128]{3,2,1,0:T(8,128)(2,1)S(1)} %get-tuple-element.22), channel_id=1, source_target_pairs={{0,64},{64,0},{128,192},{192,128},{1,65},{65,1},{129,193},{193,129... | collective-permute-start | bytes 1105928 | tf_op jit(solution)/shard_map/ppermute | solution.py:446

commit v2 on v1

v2 whole, which is shorter than its diff:
```python
import jax
import jax.numpy as jnp
from jax import lax
from jax.experimental import pallas as pl
from jax.experimental.pallas import tpu as pltpu
from jax.sharding import PartitionSpec as P

B = 128
T = 256
R = 10
W = 9
SHARE = 32
SCALE = 1.0 / (4.0 * W * B)
BF = jnp.bfloat16
F32 = jnp.float32
MIB = 2**20

A_OFF = [(5, 4), (6, 4), (7, 4), (6, 5), (7, 5), (7, 6)]
A_PACK = [(4, 5), (6, 7)]
A_PAIRS = [(h, c) for h in range(4, 8) for c in range(4, h + 1)]
B_OFF = [(h, c) for h in range(4, 8) for c in range(h - 4, 4)]
C_OFF = [(h - 4, c - 4) for h, c in A_OFF]
C_PACK = [(h - 4, c - 4) for h, c in A_PACK]
MASKS = A_PAIRS + B_OFF
NA = len(A_OFF) + 2
NB = len(B_OFF) + len(C_OFF) + 2
A_ROWS = NA * B + 32
B_ROWS = NB * B + 16

HBM = pl.BlockSpec(memory_space=pltpu.HBM)
VM = pl.BlockSpec(memory_space=pltpu.VMEM)


def nt(a, b):
    return lax.dot_general(a, b, (((1,), (1,)), ((), ())), preferred_element_type=F32)


def nn(a, b):
    return lax.dot_general(a, b, (((1,), (0,)), ((), ())), preferred_element_type=F32)


def flip_core():
    return lax.rem(lax.axis_index("layer"), 2)


def place(flip, i, w):
    return jnp.where(flip == 1, R - 1 - i, i), jnp.where(flip == 1, W - 1 - w, w)


def own_slot(i, j):
    if not 0 <= i < R:
        i, j = j, i
    return i, j - i + 4


def smem_mask(ret, flip, i, j):
    row, slot = place(flip, *own_slot(i, j))
    return (ret[row, slot] != 0).astype(F32)


def iotas(n):
    return lax.broadcasted_iota(jnp.int32, (n, n), 0), lax.broadcasted_iota(jnp.int32, (n, n), 1)


def eye():
    r, c = iotas(T)
    return (r == c).astype(F32).astype(BF)


def whole(row16):
    return jnp.concatenate([row16] * (B // 16), axis=0)


def put_masked(store, tile, I, J, mask):
    for a in range(2):
        for b in range(2):
            i, j = 2 * I + a, 2 * J + b
            if abs(i - j) > 4:
                store(a, b, jnp.zeros((B, B), BF))
            else:
                store(a, b, (tile[a * B : (a + 1) * B, b * B : (b + 1) * B] * mask(i, j)).astype(BF))


def put_step(store, x, cube, I, J, mask):
    for a in range(2):
        for b in range(2):
            i, j = 2 * I + a, 2 * J + b
            if abs(i - j) > 4:
                store(a, b, jnp.zeros((B, B), BF))
            else:
                q = cube[a * B : (a + 1) * B, b * B : (b + 1) * B] * mask(i, j)
                xq = x[a * B : (a + 1) * B, b * B : (b + 1) * B].astype(F32)
                store(a, b, ((3.0 * xq - q * SCALE) * 0.5).astype(BF))


def at(ref, *lead):
    def store(a, b, v):
        ref[(*lead, pl.ds(a * B, B), pl.ds(b * B, B))] = v

    return store


def d1_store(d1, I, J):
    def store(a, b, v):
        d1[J + 2, pl.ds((I - J + 2) * T + a * B, B), pl.ds(b * B, B)] = v

    return store


def pack_kernel(off, packs, masks, x, ret, out, buf, smem, sem, ret_sem):
    flip = flip_core()
    blocks = off + [(h, h) for pair in packs for h in pair]
    load = pltpu.make_async_copy(ret, smem, ret_sem)
    load.start()
    copies = []
    for n, (h, c) in enumerate(blocks):
        row, slot = place(flip, h + 2, c - h + 4)
        cp = pltpu.make_async_copy(x.at[row, slot], buf.at[n], sem.at[n])
        cp.start()
        copies.append(cp)
    load.wait()
    aux = (len(off) + len(packs)) * B
    if masks:
        rows = [jnp.full((1, B), smem_mask(smem, flip, h + 2, c + 2), F32) for h, c in masks]
    else:
        rows = []
    r, c_ = iotas(B)

    def masked(n):
        h, c = blocks[n]
        copies[n].wait()
        m = jnp.full((16, B), smem_mask(smem, flip, h + 2, c + 2), F32).astype(BF)
        return buf[n] * whole(m)

    for n in range(len(off)):
        out[pl.ds(n * B, B), :] = masked(n)
    for k in range(len(packs)):
        n = len(off) + 2 * k
        first, second = masked(n).astype(F32), masked(n + 1).astype(F32)
        out[pl.ds((len(off) + k) * B, B), :] = jnp.where(r <= c_, first, second).astype(BF)
        rows.append(jnp.sum(jnp.where(r == c_, second, 0.0), axis=0, keepdims=True))
    n_rows = out.shape[0] - aux
    rows.append(jnp.zeros((n_rows - len(rows), B), F32))
    out[pl.ds(aux, n_rows), :] = jnp.concatenate(rows, axis=0).astype(BF)


def pack(x, ret, off, packs, masks, rows, name):
    def kernel(*refs):
        pack_kernel(off, packs, masks, *refs)

    n = len(off) + 2 * len(packs)
    return pl.pallas_call(
        kernel,
        out_shape=jax.ShapeDtypeStruct((rows, B), BF),
        in_specs=[HBM, HBM],
        out_specs=VM,
        scratch_shapes=[
            pltpu.VMEM((n, B, B), BF),
            pltpu.SMEM((R, W), jnp.int32),
            pltpu.SemaphoreType.DMA((n,)),
            pltpu.SemaphoreType.DMA,
        ],
        compiler_params=pltpu.CompilerParams(vmem_limit_bytes=4 * MIB),
        cost_estimate=pl.CostEstimate(flops=1000, bytes_accessed=2 * rows * B * 2, transcendentals=0),
        name=name,
    )(x, ret)


D1_EARLY = [(0, 2), (2, 0), (1, 2), (2, 1), (2, 2), (1, 3), (3, 1), (2, 3), (3, 2), (2, 4), (4, 2)]
D1_CORNER = [(0, 0), (0, 1), (1, 0), (1, 1)]
MK = R * W + 6


def early_kernel(x, ret, xb01, xt, s4, acc, d1, mk, xin, xb, sb, smem, sem, ret_sem):
    flip = flip_core()
    load = pltpu.make_async_copy(ret, smem, ret_sem)
    load.start()
    copies = []
    for i in range(R):
        row, _ = place(flip, i, 0)
        cp = pltpu.make_async_copy(x.at[row], xin.at[i], sem.at[i])
        cp.start()
        copies.append(cp)
    load.wait()
    masks = {(i, w): smem_mask(smem, flip, i, i + w - 4) for i in range(R) for w in range(W)}
    for (i, w), m in masks.items():
        mk[pl.ds(i * W + w, 1), :] = jnp.full((1, B), m, F32)
    mk[pl.ds(R * W, MK - R * W), :] = jnp.zeros((MK - R * W, B), F32)

    def mask(i, j):
        return masks[own_slot(i, j)]

    for I in range(5):
        xb[I, pl.ds(0, B), pl.ds(9 * B, B)] = jnp.zeros((B, B), BF)
        xb[I, pl.ds(B, B), pl.ds(0, B)] = jnp.zeros((B, B), BF)
        for a in range(2):
            i = 2 * I + a
            copies[i].wait()
            for w in range(W):
                _, slot = place(flip, i, w)
                m = jnp.full((16, B), masks[i, w], F32).astype(BF)
                xb[I, pl.ds(a * B, B), pl.ds((a + w) * B, B)] = xin[i, slot] * whole(m)

    def xs(I, lo, hi):
        return xb[I, :, pl.ds((lo - I + 2) * T, (hi - lo + 1) * T)]

    def ss(I, lo, hi):
        return sb[I, :, pl.ds((lo - I + 2) * T, (hi - lo + 1) * T)]

    one = eye()
    xb01[...] = xb[pl.ds(0, 2)]
    for n, (I, K) in enumerate([(0, -2), (0, -1), (1, -1)]):
        xt[n] = nt(one, xs(I, K, K)).astype(BF)

    for I in range(5):
        for J in range(I, min(I + 3, 5)):
            lo, hi = J - 2, I + 2
            s = nt(xs(I, lo, hi), xs(J, lo, hi))

            def store(a, b, v, I=I, J=J):
                sb[I, pl.ds(a * B, B), pl.ds((J - I + 2) * T + b * B, B)] = v

            put_masked(store, s, I, J, mask)
            if J > I:
                sb[J, :, pl.ds((I - J + 2) * T, T)] = nt(one, ss(I, J, J)).astype(BF)

    for n, (I, J) in enumerate(D1_CORNER):
        s4[n] = ss(I, J, J)
        lo, hi = max(0, I - 2, J - 2), min(I, J) + 2
        acc[n] = nt(ss(I, lo, hi), xs(J, lo, hi))

    for I, J in D1_EARLY:
        lo, hi = max(I, J) - 2, min(I, J) + 2
        put_step(d1_store(d1, I, J), xs(I, J, J), nt(ss(I, lo, hi), xs(J, lo, hi)), I, J, mask)


def early(x, ret):
    return pl.pallas_call(
        early_kernel,
        out_shape=[
            jax.ShapeDtypeStruct((2, T, 5 * T), BF),
            jax.ShapeDtypeStruct((3, T, T), BF),
            jax.ShapeDtypeStruct((4, T, T), BF),
            jax.ShapeDtypeStruct((4, T, T), F32),
            jax.ShapeDtypeStruct((7, 5 * T, T), BF),
            jax.ShapeDtypeStruct((MK, B), F32),
        ],
        in_specs=[HBM, HBM],
        out_specs=[VM] * 6,
        scratch_shapes=[
            pltpu.VMEM((R, W, B, B), BF),
            pltpu.VMEM((5, T, 5 * T), BF),
            pltpu.VMEM((5, T, 5 * T), BF),
            pltpu.SMEM((R, W), jnp.int32),
            pltpu.SemaphoreType.DMA((R,)),
            pltpu.SemaphoreType.DMA,
        ],
        compiler_params=pltpu.CompilerParams(vmem_limit_bytes=36 * MIB),
        cost_estimate=pl.CostEstimate(flops=2 * 110 * T * T * T, bytes_accessed=12 * MIB, transcendentals=0),
        name="early",
    )(x, ret)


def halo_mask(mk, pa):
    def mask(i, j):
        if 0 <= i < R or 0 <= j < R:
            i, w = own_slot(i, j)
            return mk[pl.ds(i * W + w, 1), :]
        n = MASKS.index((max(i, j) + 8, min(i, j) + 8))
        return pa[pl.ds(NA * B + n, 1), :].astype(F32)

    return mask


def block_of(pa, pb):
    where, packed = {}, {}
    for n, hc in enumerate(A_OFF):
        where[hc] = (pa, n)
    for k, pair in enumerate(A_PACK):
        packed[pair] = (pa, len(A_OFF) + k, NA * B + len(MASKS) + k)
    if pb is not None:
        for n, hc in enumerate(B_OFF + C_OFF):
            where[hc] = (pb, n)
        for k, pair in enumerate(C_PACK):
            packed[pair] = (pb, NB - 2 + k, NB * B + k)
    return where, packed


def unpack(pa, pb, xh, one):
    lowest = -2 if pb is None else -4
    where, packed = block_of(pa, pb)
    r, c_ = iotas(B)

    def dst(h, c):
        I, J = h // 2 - 4, c // 2 - 4
        return (I + 4, pl.ds((h % 2) * B, B), pl.ds((J - I + 2) * T + (c % 2) * B, B))

    for (h, g), (ref, n, row) in packed.items():
        both = ref[pl.ds(n * B, B), :]
        turned = nt(one[:B, :B], both)
        both = both.astype(F32)
        xh[dst(h, h)] = jnp.where(r <= c_, both, turned).astype(BF)
        other = jnp.where(r < c_, turned, both)
        xh[dst(g, g)] = jnp.where(r == c_, ref[pl.ds(row, 1), :].astype(F32), other).astype(BF)
    for I in range(lowest, 0):
        for J in range(max(I - 2, lowest), I + 1):
            for a in range(2):
                for b in range(2):
                    h, c = 2 * I + a + 8, 2 * J + b + 8
                    if h == c:
                        continue
                    if abs(h - c) > 4:
                        xh[dst(h, c)] = jnp.zeros((B, B), BF)
                    elif c < h:
                        ref, n = where[h, c]
                        xh[dst(h, c)] = ref[pl.ds(n * B, B), :]
                    else:
                        ref, n = where[c, h]
                        xh[dst(h, c)] = nt(one[:B, :B], ref[pl.ds(n * B, B), :]).astype(BF)
            if J < I:
                tile = xh[I + 4, :, pl.ds((J - I + 2) * T, T)]
                xh[J + 4, :, pl.ds((I - J + 2) * T, T)] = nt(one, tile).astype(BF)


def put_cross(xh, xt):
    xh[2, :, pl.ds(4 * T, T)] = xt[0]
    xh[3, :, pl.ds(3 * T, T)] = xt[1]
    xh[3, :, pl.ds(4 * T, T)] = xt[2]


def rows_of(xb01, xh):
    def xs(I, lo, hi):
        cols = pl.ds((lo - I + 2) * T, (hi - lo + 1) * T)
        return xb01[I, :, cols] if I >= 0 else xh[I + 4, :, cols]

    return xs


S_CROSS = [(0, -2), (0, -1), (1, -1)]


def corner_kernel(pa, xb01, xt, s4, acc, mk, d1_in, s3, d1, swap, xh):
    del d1_in
    mask = halo_mask(mk, pa)
    one = eye()
    unpack(pa, None, xh, one)
    put_cross(xh, xt)
    xs = rows_of(xb01, xh)

    for n, (I, J) in enumerate(S_CROSS):
        lo, hi = I - 2, J + 2
        put_masked(at(s3, n), nt(xs(I, lo, hi), xs(J, lo, hi)), I, J, mask)
    terms = {
        (0, 0): [(0, -2), (1, -1)],
        (0, 1): [(1, -1)],
        (1, 0): [(2, -1)],
        (1, 1): [(2, -1)],
    }
    for n, (I, J) in enumerate(D1_CORNER):
        cube = acc[n]
        for k, m in terms[I, J]:
            cube = cube + nt(s3[k], xs(J, m, m))
        near = d1_store(d1, I, J)

        def store(a, b, v, I=I, J=J, near=near):
            near(a, b, v)
            r, c = 3 - (2 * I + a), 3 - (2 * J + b)
            swap[c // 2, pl.ds(r * B, B), pl.ds((c % 2) * B, B)] = v

        put_step(store, xs(I, J, J), cube, I, J, mask)

    known = {hc: s4[n] for n, hc in enumerate(D1_CORNER)}
    known.update({hc: s3[n] for n, hc in enumerate(S_CROSS)})
    for I, J in S_CROSS:
        lo, hi = I - 2, J + 2
        cube = sum(nt(known[I, m], xs(J, m, m)) for m in range(lo, hi + 1))
        put_step(d1_store(d1, I, J), xs(I, J, J), cube, I, J, mask)


def corner(pa, xb01, xt, s4, acc, mk, d1):
    return pl.pallas_call(
        corner_kernel,
        out_shape=[
            jax.ShapeDtypeStruct((3, T, T), BF),
            jax.ShapeDtypeStruct((7, 5 * T, T), BF),
            jax.ShapeDtypeStruct((2, 2 * T, T), BF),
        ],
        in_specs=[VM] * 7,
        out_specs=[VM] * 3,
        scratch_shapes=[pltpu.VMEM((4, T, 5 * T), BF)],
        input_output_aliases={6: 1},
        compiler_params=pltpu.CompilerParams(vmem_limit_bytes=24 * MIB),
        cost_estimate=pl.CostEstimate(flops=2 * 30 * T * T * T, bytes_accessed=4 * MIB, transcendentals=0),
        name="corner",
    )(pa, xb01, xt, s4, acc, mk, d1)


D1_HALO = [(-2, 0), (-1, 0), (-1, 1), (-1, -1), (-1, -2), (-2, -1), (-2, -2)]
H = R // 2
Q = 2 * SHARE


def finish_kernel(pa, pb, xb01, xt, s4, s3, mk, swapped, d1_in, d1, keep, send, xh, sb, left, s1):
    del d1_in
    layer = lax.axis_index("layer")
    flip = lax.rem(layer, 2)
    chip_rows = pl.multiple_of(lax.div(layer, 2) * Q, Q)
    mask = halo_mask(mk, pa)
    one = eye()
    unpack(pa, pb, xh, one)
    put_cross(xh, xt)
    xs = rows_of(xb01, xh)

    def spos(I, J):
        return (I + 2, slice(None), pl.ds((J - I + 2) * T, T))

    def ss(I, lo, hi):
        return sb[I + 2, :, pl.ds((lo - I + 2) * T, (hi - lo + 1) * T)]

    for n, (I, J) in enumerate(D1_CORNER):
        sb[spos(I, J)] = s4[n]
    for n, (I, J) in enumerate(S_CROSS):
        sb[spos(I, J)] = s3[n]
        sb[spos(J, I)] = nt(one, s3[n]).astype(BF)
    for I, J in [(-1, -1), (-2, -2), (-1, -2), (-1, -3), (-2, -3), (-2, -4)]:
        lo, hi = I - 2, J + 2

        def store(a, b, v, I=I, J=J):
            sb[I + 2, pl.ds(a * B, B), pl.ds((J - I + 2) * T + b * B, B)] = v

        put_masked(store, nt(xs(I, lo, hi), xs(J, lo, hi)), I, J, mask)
    sb[spos(-2, -1)] = nt(one, ss(-1, -2, -2)).astype(BF)

    for I, J in D1_HALO:
        lo, hi = max(I, J) - 2, min(I, J) + 2
        put_step(d1_store(d1, I, J), xs(I, J, J), nt(ss(I, lo, hi), xs(J, lo, hi)), I, J, mask)

    for i in range(H):
        I, a = i // 2, i % 2
        for J in range(-2, 5):
            dst = (pl.ds(i * Q, Q), pl.ds((J + 2) * T, T))
            if abs(I - J) <= 2:
                left[dst] = d1[J + 2, pl.ds((I - J + 2) * T + a * B + chip_rows, Q), :]
            else:
                left[dst] = jnp.zeros((Q, T), BF)

    def product(lhs, J):
        i0, i1 = max(0, 2 * J - 4), min(H - 1, 2 * J + 5)
        k0, k1 = max(J - 2, -2), min(J + 2, 4)
        rows = pl.ds(i0 * Q, (i1 - i0 + 1) * Q)
        if J < 3:
            a = lhs[rows, pl.ds((k0 + 2) * T, (k1 - k0 + 1) * T)]
            return i0, i1, nn(a, d1[J + 2, pl.ds((k0 - J + 2) * T, (k1 - k0 + 1) * T), :])
        a, b = lhs[rows, pl.ds((k0 + 2) * T, (3 - k0) * T)], lhs[rows, pl.ds(5 * T, 2 * T)]
        return i0, i1, nn(a, d1[J + 2, pl.ds((k0 - J + 2) * T, (3 - k0) * T), :]) + nn(b, swapped[J - 3])

    for J in range(4, -3, -1):
        i0, i1, s = product(left, J)
        for i in range(H):
            for b in range(2):
                j = 2 * J + b
                dst = (pl.ds(i * Q, Q), pl.ds((J + 2) * T + b * B, B))
                if abs(i - j) <= 4 and i0 <= i <= i1:
                    q = s[(i - i0) * Q : (i - i0 + 1) * Q, b * B : (b + 1) * B]
                    s1[dst] = (q * mask(i, j)).astype(BF)
                else:
                    s1[dst] = jnp.zeros((Q, B), BF)

    for J in range(4, -3, -1):
        i0, i1, cube = product(s1, J)
        for i in range(i0, i1 + 1):
            for b in range(2):
                j = 2 * J + b
                if abs(i - j) > 4:
                    continue
                q = cube[(i - i0) * Q : (i - i0 + 1) * Q, b * B : (b + 1) * B] * mask(i, j)
                x = left[pl.ds(i * Q, Q), pl.ds((J + 2) * T + b * B, B)].astype(F32)
                v = (3.0 * x - q * SCALE) * 0.5
                w = j - i + 4
                near = jnp.where(flip == 1, H - 1 - i, i)
                slot = jnp.where(flip == 1, W - 1 - w, w)
                lo, hi = v[:SHARE].astype(BF), v[SHARE:].astype(BF)
                keep[near, slot] = jnp.where(flip == 1, hi, lo)
                send[near, slot] = jnp.where(flip == 1, lo, hi)


def finish(pa, pb, xb01, xt, s4, s3, mk, swapped, d1):
    return pl.pallas_call(
        finish_kernel,
        out_shape=[
            jax.ShapeDtypeStruct((7, 5 * T, T), BF),
            jax.ShapeDtypeStruct((H, W, SHARE, B), BF),
            jax.ShapeDtypeStruct((H, W, SHARE, B), BF),
        ],
        in_specs=[VM] * 9,
        out_specs=[VM] * 3,
        scratch_shapes=[
            pltpu.VMEM((4, T, 5 * T), BF),
            pltpu.VMEM((4, T, 5 * T), BF),
            pltpu.VMEM((H * Q, 7 * T), BF),
            pltpu.VMEM((H * Q, 7 * T), BF),
        ],
        input_output_aliases={8: 0},
        compiler_params=pltpu.CompilerParams(vmem_limit_bytes=36 * MIB),
        cost_estimate=pl.CostEstimate(flops=2 * 120 * T * T * T, bytes_accessed=8 * MIB, transcendentals=0),
        name="finish",
    )(pa, pb, xb01, xt, s4, s3, mk, swapped, d1)


def join_kernel(keep, other, out, sem):
    flip = flip_core()
    a = pltpu.make_async_copy(keep, out.at[pl.ds(jnp.where(flip == 1, H, 0), H)], sem.at[0])
    b = pltpu.make_async_copy(other, out.at[pl.ds(jnp.where(flip == 1, 0, H), H)], sem.at[1])
    a.start()
    b.start()
    a.wait()
    b.wait()


def join(keep, other):
    return pl.pallas_call(
        join_kernel,
        out_shape=jax.ShapeDtypeStruct((R, W, SHARE, B), BF),
        in_specs=[VM, VM],
        out_specs=HBM,
        scratch_shapes=[pltpu.SemaphoreType.DMA((2,))],
        compiler_params=pltpu.CompilerParams(vmem_limit_bytes=2 * MIB),
        name="join",
    )(keep, other)


def chain(layers, grid):
    pairs = []
    for l in range(layers):
        for g in range(grid):
            pairs.append((l * grid + g, l * grid + (g + 1 if l % 2 == 0 else g - 1) % grid))
    return pairs


def per_device(x, ret):
    layers, grid = lax.axis_size("layer"), lax.axis_size("grid")
    cores = [(l, l ^ 1) for l in range(layers)]
    pairs = chain(layers, grid)
    x = pltpu.with_memory_space_constraint(x, pltpu.HBM)
    ret = pltpu.with_memory_space_constraint(ret, pltpu.HBM)
    pa = pack(x, ret, A_OFF, A_PACK, MASKS, A_ROWS, "pack_corner")
    pa = lax.ppermute(pa, ("layer", "grid"), pairs)
    pb = pack(x, ret, B_OFF + C_OFF, C_PACK, [], B_ROWS, "pack_deep")
    pb = lax.ppermute(pb, ("layer", "grid"), pairs)
    xb01, xt, s4, acc, d1, mk = early(x, ret)
    s3, d1, swap = corner(pa, xb01, xt, s4, acc, mk, d1)
    swapped = lax.ppermute(swap, "layer", cores)
    _, keep, send = finish(pa, pb, xb01, xt, s4, s3, mk, swapped, d1)
    other = lax.ppermute(send, "layer", cores)
    return join(keep, other)


def solution(mesh):
    return jax.shard_map(
        per_device,
        mesh=mesh,
        in_specs=(P("grid", None, None, None), P("grid", None)),
        out_specs=P("grid", None, "layer", None),
        check_vma=False,
    )
```

time: 40.2 us -> 31.1 us (0.77)
  local copies, waits for them, and re-layouts: 3.29 us -> 0 us
  waiting for transfers between devices: 5.56 us -> 3.34 us
  starting transfers between devices: 13.1 us -> 11.1 us
  Pallas kernels: 17.8 us -> 16.2 us
    unnamed x4 -> x0, local copies, waits for them, and re-layouts: 2.53 us -> none
    pallas_call x3 -> x4, Pallas kernels: 10.9 us -> 8.38 us  [the longest x1 5.02 us: finish(): pl.pallas_call(finish_kernel, out_shape=[jax.ShapeDtypeStruct((7, 5 * T,...]
    ppermute x2 -> x3, starting transfers between devices: 13.1 us -> 10.8 us  [the longest x1 9.9 us: per_device(): pa = lax.ppermute(pa, ('layer', 'grid'), pairs)]
    ppermute x2 -> x3, waiting for transfers between devices: 3.89 us -> 1.9 us  [the longest x1 1.46 us: per_device(): swapped = lax.ppermute(swap, 'layer', cores)]
    pallas_call x1, Pallas kernels: 5.28 us -> 6.26 us  [early(): pl.pallas_call(early_kernel, out_shape=[jax.ShapeDtypeStruct((2, T, 5 * T...]
    dynamic_update_slice x1 -> x0, local copies, waits for them, and re-layouts: 0.76 us -> none  [per_device(): lax.dynamic_update_slice(full, other, (jnp.where(flip == 1, 0, H), 0, 0, 0))]
  transfers between devices with their start and end apart: 3 -> 4, of which waited for: 2 -> 3; matrix products, arithmetic and copies ran while one was open for 0% -> 0% of each run, Pallas kernels for 22% -> 30%
where the time goes in v2:
time: 31.1 us; the launch traced here: 30.8 us
  Pallas kernels  16.2 us (52%)
  starting transfers between devices  11.1 us (36%)
  waiting for transfers between devices  3.34 us (11%)
    ppermute x1, starting transfers between devices, per_device(): pa = lax.ppermute(pa, ('layer', 'grid'), pairs)  9.9 us
    pallas_call x1, Pallas kernels, early(): pl.pallas_call(early_kernel, out_shape=[jax.ShapeDtypeStruct((2, T, 5 * T...  6.26 us
    pallas_call x1, Pallas kernels, finish(): pl.pallas_call(finish_kernel, out_shape=[jax.ShapeDtypeStruct((7, 5 * T,...  5.02 us
    pallas_call x2, Pallas kernels, pack(): pl.pallas_call(kernel, out_shape=jax.ShapeDtypeStruct((rows, B), BF), in_...  2.48 us
    pallas_call x1, Pallas kernels, corner(): pl.pallas_call(corner_kernel, out_shape=[jax.ShapeDtypeStruct((3, T, T),...  1.52 us
    ppermute x1, waiting for transfers between devices, per_device(): swapped = lax.ppermute(swap, 'layer', cores)  1.46 us
    ppermute x1, waiting for transfers between devices, per_device(): other = lax.ppermute(send, 'layer', cores)  1.44 us
    pallas_call x1, Pallas kernels, join(): pl.pallas_call(join_kernel, out_shape=jax.ShapeDtypeStruct((R, W, SHARE,...  0.88 us
  transfers between devices with their start and end apart: 4, of which 3 were waited for; matrix products, arithmetic and copies ran while one was open for 0% of the time, Pallas kernels for 30%

profile of v2, /device:TPU:1, one launch (start us, length us, event | category | flops | bytes accessed | tf_op | source)
XLA Modules:
  0.0 30.8 jit_solution(14119621246993437421)
XLA Ops:
  0.0 1.1 %pack_corner.1 = bf16[1056,128]{1,0:T(8,128)(2,1)S(1)} custom-call(bf16[10,9,128,128]{3,2,1,0:T(8,128)(2,1)} %x.1, s32[10,9]{1,0:T(8,128)} %ret.1), custom_call_target="tpu_custom_call" | custom-call | flops 1000 | bytes 540672 | tf_op jit(solution)/shard_map/pack_corner/pallas_call | solution.py:152
  1.1 9.9 %collective-permute-start = (bf16[1056,128]{1,0:T(8,128)(2,1)S(1)}, bf16[1056,128]{1,0:T(8,128)(2,1)S(1)}, u32[]{:S(2)}, u32[]{:S(2)}) collective-permute-start(bf16[1056,128]{1,0:T(8,128)(2,1)S(1)} %pack_corner.1), channel_id=1, source_target_pairs={{0,1},{1,2},{2,3},{3,4},{4,5},{5,6},{6,7},{7,8},{8,9},{9,10},{10,1... | collective-permute-start | bytes 811016 | tf_op jit(solution)/shard_map/ppermute | solution.py:547
  11.0 1.4 %pack_deep.1 = bf16[2320,128]{1,0:T(8,128)(2,1)S(1)} custom-call(bf16[10,9,128,128]{3,2,1,0:T(8,128)(2,1)} %x.1, s32[10,9]{1,0:T(8,128)} %ret.1), custom_call_target="tpu_custom_call" | custom-call | flops 1000 | bytes 1187840 | tf_op jit(solution)/shard_map/pack_deep/pallas_call | solution.py:152
  12.4 0.6 %collective-permute-start.1 = (bf16[2320,128]{1,0:T(8,128)(2,1)S(1)}, bf16[2320,128]{1,0:T(8,128)(2,1)S(1)}, u32[]{:S(2)}, u32[]{:S(2)}) collective-permute-start(bf16[2320,128]{1,0:T(8,128)(2,1)S(1)} %pack_deep.1), channel_id=1, source_target_pairs={{0,1},{1,2},{2,3},{3,4},{4,5},{5,6},{6,7},{7,8},{8,9},{9,10},{10,1... | collective-permute-start | bytes 1781768 | tf_op jit(solution)/shard_map/ppermute | solution.py:549
  13.0 6.3 %early.1 = (bf16[2,256,1280]{2,1,0:T(8,128)(2,1)S(1)}, bf16[3,256,256]{2,1,0:T(8,128)(2,1)S(1)}, bf16[4,256,256]{2,1,0:T(8,128)(2,1)S(1)}, f32[4,256,256]{2,1,0:...) custom-call(bf16[10,9,128,128]{3,2,1,0:T(8,128)(2,1)} %x.1, s32[10,9]{1,0:T(8,128)} %ret.1), custom_call_target="tpu_custom_call" | custom-call | flops 3690987520 | bytes 12582912 | tf_op jit(solution)/shard_map/early/pallas_call | solution.py:238
  19.3 0.0 collective-permute-done.pa
  19.3 1.5 %corner.1 = (bf16[3,256,256]{2,1,0:T(8,128)(2,1)S(1)}, bf16[7,1280,256]{2,1,0:T(8,128)(2,1)S(1)}, bf16[2,512,256]{2,1,0:T(8,128)(2,1)S(1)}) custom-call(bf16[1056,128]{1,0:T(8,128)(2,1)S(1)} %collective-permute-done.pa, bf16[2,256,1280]{2,1,0:T(8,128)(2,1)S(1)} %get-tuple-element.16.xb01, ...), custom_call_target="tpu_custom_call", output_to_operand_aliasing={{1}: (6, {})} | custom-call | flops 1006632960 | bytes 4194304 | tf_op jit(solution)/shard_map/corner/pallas_call | solution.py:381
  20.8 0.3 collective-permute-start.2
  21.1 0.4 %collective-permute-done.1.pb = bf16[2320,128]{1,0:T(8,128)(2,1)S(1)} collective-permute-done((bf16[2320,128]{1,0:T(8,128)(2,1)S(1)}, bf16[2320,128]{1,0:T(8,128)(2,1)S(1)}, u32[]{:S(2)}, u32[]{:S(2)}) %collective-permute-start.1) | collective-permute-done | bytes 593952 | tf_op jit(solution)/shard_map/ppermute | solution.py:549
  21.5 1.5 %collective-permute-done.2.swapped = bf16[2,512,256]{2,1,0:T(8,128)(2,1)S(1)} collective-permute-done((bf16[2,512,256]{2,1,0:T(8,128)(2,1)S(1)}, bf16[2,512,256]{2,1,0:T(8,128)(2,1)S(1)}, u32[]{:S(2)}, u32[]{:S(2)}) %collective-permute-start.2) | collective-permute-done | bytes 524320 | tf_op jit(solution)/shard_map/ppermute | solution.py:552
  23.0 5.0 %finish.1 = (bf16[7,1280,256]{2,1,0:T(8,128)(2,1)S(1)}, bf16[5,9,32,128]{3,2,1,0:T(8,128)(2,1)S(1)}, bf16[5,9,32,128]{3,2,1,0:T(8,128)(2,1)S(1)}) custom-call(bf16[1056,128]{1,0:T(8,128)(2,1)S(1)} %collective-permute-done.pa, bf16[2320,128]{1,0:T(8,128)(2,1)S(1)} %collective-permute-done.1.pb, ...), custom_call_target="tpu_custom_call", output_to_operand_aliasing={{0}: (8, {})} | custom-call | flops 4026531840 | bytes 8388608 | tf_op jit(solution)/shard_map/finish/pallas_call | solution.py:488
  28.0 0.3 %collective-permute-start.3 = (bf16[5,9,32,128]{3,2,1,0:T(8,128)(2,1)S(1)}, bf16[5,9,32,128]{3,2,1,0:T(8,128)(2,1)S(1)}, u32[]{:S(2)}, u32[]{:S(2)}) collective-permute-start(bf16[5,9,32,128]{3,2,1,0:T(8,128)(2,1)S(1)} %get-tuple-element.26), channel_id=1, source_target_pairs={{0,64},{64,0},{128,192},{192,128},{1,65},{65,1},{129,193},{193,129... | collective-permute-start | bytes 1105928 | tf_op jit(solution)/shard_map/ppermute | solution.py:554
  28.4 1.4 %collective-permute-done.3.other = bf16[5,9,32,128]{3,2,1,0:T(8,128)(2,1)S(1)} collective-permute-done((bf16[5,9,32,128]{3,2,1,0:T(8,128)(2,1)S(1)}, bf16[5,9,32,128]{3,2,1,0:T(8,128)(2,1)S(1)}, u32[]{:S(2)}, u32[]{:S(2)}) %collective-permute-start.3) | collective-permute-done | bytes 368672 | tf_op jit(solution)/shard_map/ppermute | solution.py:554
  29.8 0.9 %join.1 = bf16[10,9,32,128]{3,2,1,0:T(8,128)(2,1)} custom-call(bf16[5,9,32,128]{3,2,1,0:T(8,128)(2,1)S(1)} %get-tuple-element.25.keep, bf16[5,9,32,128]{3,2,1,0:T(8,128)(2,1)S(1)} %collective-permute-done.3.other), custom_call_target="tpu_custom_call" | custom-call | tf_op jit(solution)/shard_map/join/pallas_call | solution.py:521
Async XLA Ops:
  1.1 18.2 %collective-permute-start = (bf16[1056,128]{1,0:T(8,128)(2,1)S(1)}, bf16[1056,128]{1,0:T(8,128)(2,1)S(1)}, u32[]{:S(2)}, u32[]{:S(2)}) collective-permute-start(bf16[1056,128]{1,0:T(8,128)(2,1)S(1)} %pack_corner.1), channel_id=1, source_target_pairs={{0,1},{1,2},{2,3},{3,4},{4,5},{5,6},{6,7},{7,8},{8,9},{9,10},{10,1... | collective-permute-start | bytes 811016 | tf_op jit(solution)/shard_map/ppermute | solution.py:547
  12.4 9.2 %collective-permute-start.1 = (bf16[2320,128]{1,0:T(8,128)(2,1)S(1)}, bf16[2320,128]{1,0:T(8,128)(2,1)S(1)}, u32[]{:S(2)}, u32[]{:S(2)}) collective-permute-start(bf16[2320,128]{1,0:T(8,128)(2,1)S(1)} %pack_deep.1), channel_id=1, source_target_pairs={{0,1},{1,2},{2,3},{3,4},{4,5},{5,6},{6,7},{7,8},{8,9},{9,10},{10,1... | collective-permute-start | bytes 1781768 | tf_op jit(solution)/shard_map/ppermute | solution.py:549
  20.8 2.2 %collective-permute-start.2 = (bf16[2,512,256]{2,1,0:T(8,128)(2,1)S(1)}, bf16[2,512,256]{2,1,0:T(8,128)(2,1)S(1)}, u32[]{:S(2)}, u32[]{:S(2)}) collective-permute-start(bf16[2,512,256]{2,1,0:T(8,128)(2,1)S(1)} %get-tuple-element.23), channel_id=1, source_target_pairs={{0,64},{64,0},{128,192},{192,128},{1,65},{65,1},{129,193},{193,129... | collective-permute-start | bytes 1572872 | tf_op jit(solution)/shard_map/ppermute | solution.py:552
  28.0 1.8 %collective-permute-start.3 = (bf16[5,9,32,128]{3,2,1,0:T(8,128)(2,1)S(1)}, bf16[5,9,32,128]{3,2,1,0:T(8,128)(2,1)S(1)}, u32[]{:S(2)}, u32[]{:S(2)}) collective-permute-start(bf16[5,9,32,128]{3,2,1,0:T(8,128)(2,1)S(1)} %get-tuple-element.26), channel_id=1, source_target_pairs={{0,64},{64,0},{128,192},{192,128},{1,65},{65,1},{129,193},{193,129... | collective-permute-start | bytes 1105928 | tf_op jit(solution)/shard_map/ppermute | solution.py:554

commit v3 on v0

v3 whole, which is shorter than its diff:
```python
import jax
import jax.numpy as jnp
from jax import lax
from jax.experimental import pallas as pl
from jax.experimental.pallas import tpu as pltpu
from jax.sharding import PartitionSpec as P

B = 128
T = 256
R = 10
W = 9
SHARE = 32
SCALE = 1.0 / (4.0 * W * B)
BF = jnp.bfloat16
F32 = jnp.float32
MIB = 2**20

A_OFF = [(5, 4), (6, 4), (7, 4), (6, 5), (7, 5), (7, 6)]
A_PACK = [(4, 5), (6, 7)]
A_PAIRS = [(h, c) for h in range(4, 8) for c in range(4, h + 1)]
B_OFF = [(h, c) for h in range(4, 8) for c in range(h - 4, 4)]
C_OFF = [(h - 4, c - 4) for h, c in A_OFF]
C_PACK = [(h - 4, c - 4) for h, c in A_PACK]
MASKS = A_PAIRS + B_OFF
NA = len(A_OFF) + 2
NB = len(B_OFF) + len(C_OFF) + 2
A_ROWS = NA * B + 32
B_ROWS = NB * B + 16

HBM = pl.BlockSpec(memory_space=pltpu.HBM)
VM = pl.BlockSpec(memory_space=pltpu.VMEM)


def nt(a, b):
    return lax.dot_general(a, b, (((1,), (1,)), ((), ())), preferred_element_type=F32)


def nn(a, b):
    return lax.dot_general(a, b, (((1,), (0,)), ((), ())), preferred_element_type=F32)


def flip_core():
    return lax.rem(lax.axis_index("layer"), 2)


def place(flip, i, w):
    return jnp.where(flip == 1, R - 1 - i, i), jnp.where(flip == 1, W - 1 - w, w)


def own_slot(i, j):
    if not 0 <= i < R:
        i, j = j, i
    return i, j - i + 4


def smem_mask(ret, flip, i, j):
    row, slot = place(flip, *own_slot(i, j))
    return (ret[row, slot] != 0).astype(F32)


def iotas(n):
    return lax.broadcasted_iota(jnp.int32, (n, n), 0), lax.broadcasted_iota(jnp.int32, (n, n), 1)


def eye():
    r, c = iotas(T)
    return (r == c).astype(F32).astype(BF)


def whole(row16):
    return jnp.concatenate([row16] * (B // 16), axis=0)


def put_masked(store, tile, I, J, mask):
    for a in range(2):
        for b in range(2):
            i, j = 2 * I + a, 2 * J + b
            if abs(i - j) > 4:
                store(a, b, jnp.zeros((B, B), BF))
            else:
                store(a, b, (tile[a * B : (a + 1) * B, b * B : (b + 1) * B] * mask(i, j)).astype(BF))


def put_step(store, x, cube, I, J, mask):
    for a in range(2):
        for b in range(2):
            i, j = 2 * I + a, 2 * J + b
            if abs(i - j) > 4:
                store(a, b, jnp.zeros((B, B), BF))
            else:
                q = cube[a * B : (a + 1) * B, b * B : (b + 1) * B] * mask(i, j)
                xq = x[a * B : (a + 1) * B, b * B : (b + 1) * B].astype(F32)
                store(a, b, ((3.0 * xq - q * SCALE) * 0.5).astype(BF))


def at(ref, *lead):
    def store(a, b, v):
        ref[(*lead, pl.ds(a * B, B), pl.ds(b * B, B))] = v

    return store


def d1_store(d1, I, J):
    def store(a, b, v):
        d1[J + 2, pl.ds((I - J + 2) * T + a * B, B), pl.ds(b * B, B)] = v

    return store


def send_rows(out, off, packs, masks, get, mask_of):
    r, c = iotas(B)
    aux = (len(off) + len(packs)) * B
    for n, (h, g) in enumerate(off):
        out[pl.ds(n * B, B), :] = get(h, g)
    rows = [mask_of(h, g) for h, g in masks]
    for k, (h, g) in enumerate(packs):
        first, second = get(h, h).astype(F32), get(g, g).astype(F32)
        out[pl.ds((len(off) + k) * B, B), :] = jnp.where(r <= c, first, second).astype(BF)
        rows.append(jnp.sum(jnp.where(r == c, second, 0.0), axis=0, keepdims=True))
    n_rows = out.shape[0] - aux
    rows.append(jnp.zeros((n_rows - len(rows), B), F32))
    out[pl.ds(aux, n_rows), :] = jnp.concatenate(rows, axis=0).astype(BF)


def pack_corner_kernel(x, ret, out, buf, smem, sem, ret_sem):
    flip = flip_core()
    load = pltpu.make_async_copy(ret, smem, ret_sem)
    load.start()
    blocks = A_OFF + [(h, h) for pair in A_PACK for h in pair]
    copies = {}
    for n, (h, g) in enumerate(blocks):
        row, slot = place(flip, h + 2, g - h + 4)
        copies[h, g] = (pltpu.make_async_copy(x.at[row, slot], buf.at[n], sem.at[n]), n)
        copies[h, g][0].start()
    load.wait()

    def get(h, g):
        copy, n = copies[h, g]
        copy.wait()
        m = jnp.full((16, B), smem_mask(smem, flip, h + 2, g + 2), F32).astype(BF)
        return buf[n] * whole(m)

    def mask_of(h, g):
        return jnp.full((1, B), smem_mask(smem, flip, h + 2, g + 2), F32)

    send_rows(out, A_OFF, A_PACK, MASKS, get, mask_of)


def pack_corner(x, ret):
    n = len(A_OFF) + 2 * len(A_PACK)
    return pl.pallas_call(
        pack_corner_kernel,
        out_shape=jax.ShapeDtypeStruct((A_ROWS, B), BF),
        in_specs=[HBM, HBM],
        out_specs=VM,
        scratch_shapes=[
            pltpu.VMEM((n, B, B), BF),
            pltpu.SMEM((R, W), jnp.int32),
            pltpu.SemaphoreType.DMA((n,)),
            pltpu.SemaphoreType.DMA,
        ],
        compiler_params=pltpu.CompilerParams(vmem_limit_bytes=4 * MIB),
        cost_estimate=pl.CostEstimate(flops=1000, bytes_accessed=MIB, transcendentals=0),
        name="pack_corner",
    )(x, ret)


MK = R * W + 6


def pack_deep_kernel(x, ret, first, out, xin, mk, smem, sem, ret_sem):
    del first
    flip = flip_core()
    load = pltpu.make_async_copy(ret, smem, ret_sem)
    load.start()
    copies = {}
    for i in [*range(2, R), 0, 1]:
        row, _ = place(flip, i, 0)
        copies[i] = pltpu.make_async_copy(x.at[row], xin.at[i], sem.at[i])
        copies[i].start()
    load.wait()
    for i in range(R):
        for w in range(W):
            mk[pl.ds(i * W + w, 1), :] = jnp.full((1, B), smem_mask(smem, flip, i, i + w - 4), F32)
    mk[pl.ds(R * W, MK - R * W), :] = jnp.zeros((MK - R * W, B), F32)
    for i in range(2, R):
        copies[i].wait()

    def get(h, g):
        _, slot = place(flip, h + 2, g - h + 4)
        m = jnp.full((16, B), smem_mask(smem, flip, h + 2, g + 2), F32).astype(BF)
        return xin[h + 2, slot] * whole(m)

    send_rows(out, B_OFF + C_OFF, C_PACK, [], get, None)
    copies[0].wait()
    copies[1].wait()


def pack_deep(x, ret, first):
    return pl.pallas_call(
        pack_deep_kernel,
        out_shape=[
            jax.ShapeDtypeStruct((B_ROWS, B), BF),
            jax.ShapeDtypeStruct((R, W, B, B), BF),
            jax.ShapeDtypeStruct((MK, B), F32),
        ],
        in_specs=[HBM, HBM, VM],
        out_specs=[VM] * 3,
        scratch_shapes=[
            pltpu.SMEM((R, W), jnp.int32),
            pltpu.SemaphoreType.DMA((R,)),
            pltpu.SemaphoreType.DMA,
        ],
        compiler_params=pltpu.CompilerParams(vmem_limit_bytes=8 * MIB),
        cost_estimate=pl.CostEstimate(flops=1000, bytes_accessed=4 * MIB, transcendentals=0),
        name="pack_deep",
    )(x, ret, first)


D1_EARLY = [(0, 2), (2, 0), (1, 2), (2, 1), (2, 2), (1, 3)]
D1_CORNER = [(0, 0), (0, 1), (1, 0), (1, 1)]
S_EARLY = [(0, 0), (0, 1), (0, 2), (1, 1), (1, 2), (1, 3), (2, 2), (2, 3), (2, 4)]
S_TURNED = [(0, 1), (0, 2), (1, 2)]
D1 = jax.ShapeDtypeStruct((7, 5 * T, T), BF)
HROWS = jax.ShapeDtypeStruct((4, T, 5 * T), BF)


def xh_at(I, J):
    return (I + 4, slice(None), pl.ds((J - I + 2) * T, T))


def sb_at(I, J):
    return (I + 2, slice(None), pl.ds((J - I + 2) * T, T))


def sb_store(sb, I, J):
    def store(a, b, v):
        sb[I + 2, pl.ds(a * B, B), pl.ds((J - I + 2) * T + b * B, B)] = v

    return store


def rows_of(xb01, xh):
    def xs(I, lo, hi):
        cols = pl.ds((lo - I + 2) * T, (hi - lo + 1) * T)
        return xb01[I, :, cols] if I >= 0 else xh[I + 4, :, cols]

    return xs


def square_rows(sb):
    def ss(I, lo, hi):
        return sb[I + 2, :, pl.ds((lo - I + 2) * T, (hi - lo + 1) * T)]

    return ss


def own_masks(mk):
    def mask(i, j):
        i, w = own_slot(i, j)
        return mk[pl.ds(i * W + w, 1), :]

    return mask


def early_kernel(xin, mk, xb01, xh, sb, acc, d1, centre, xb, s):
    flip = flip_core()
    mask = own_masks(mk)

    for I in range(5):
        xb[I, pl.ds(0, B), pl.ds(9 * B, B)] = jnp.zeros((B, B), BF)
        xb[I, pl.ds(B, B), pl.ds(0, B)] = jnp.zeros((B, B), BF)
        for a in range(2):
            i = 2 * I + a
            for w in range(W):
                _, slot = place(flip, i, w)
                m = jnp.broadcast_to(mask(i, i + w - 4), (16, B)).astype(BF)
                v = xin[i, slot] * whole(m)
                xb[I, pl.ds(a * B, B), pl.ds((a + w) * B, B)] = v
                if I < 2:
                    xb01[I, pl.ds(a * B, B), pl.ds((a + w) * B, B)] = v
        if I < 2:
            xb01[I, pl.ds(0, B), pl.ds(9 * B, B)] = jnp.zeros((B, B), BF)
            xb01[I, pl.ds(B, B), pl.ds(0, B)] = jnp.zeros((B, B), BF)

    def xs(I, lo, hi):
        return xb[I, :, pl.ds((lo - I + 2) * T, (hi - lo + 1) * T)]

    def ss(I, lo, hi):
        return s[I, :, pl.ds((lo - I + 2) * T, (hi - lo + 1) * T)]

    one = eye()
    for I, K in S_CROSS:
        xh[xh_at(K, I)] = nt(one, xs(I, K, K)).astype(BF)

    for I, J in S_EARLY:
        def store(a, b, v, I=I, J=J):
            s[I, pl.ds(a * B, B), pl.ds((J - I + 2) * T + b * B, B)] = v

        put_masked(store, nt(xs(I, J - 2, I + 2), xs(J, J - 2, I + 2)), I, J, mask)
        if (I, J) in S_TURNED:
            s[J, :, pl.ds((I - J + 2) * T, T)] = nt(one, ss(I, J, J)).astype(BF)

    for n, (I, J) in enumerate(D1_CORNER):
        sb[sb_at(I, J)] = ss(I, J, J)
        lo, hi = max(0, I - 2, J - 2), min(I, J) + 2
        acc[n] = nt(ss(I, lo, hi), xs(J, lo, hi))

    for I, J in D1_EARLY:
        lo, hi = max(I, J) - 2, min(I, J) + 2
        store = put_swap(d1_store(d1, I, J), centre, CENTRE, I, J)
        put_step(store, xs(I, J, J), nt(ss(I, lo, hi), xs(J, lo, hi)), I, J, mask)


def early(xin, mk):
    return pl.pallas_call(
        early_kernel,
        out_shape=[
            jax.ShapeDtypeStruct((2, T, 5 * T), BF),
            HROWS,
            HROWS,
            jax.ShapeDtypeStruct((4, T, T), F32),
            D1,
            jax.ShapeDtypeStruct((len(CENTRE), B, B), BF),
        ],
        in_specs=[VM] * 2,
        out_specs=[VM] * 6,
        scratch_shapes=[pltpu.VMEM((5, T, 5 * T), BF), pltpu.VMEM((3, T, 5 * T), BF)],
        compiler_params=pltpu.CompilerParams(vmem_limit_bytes=24 * MIB),
        cost_estimate=pl.CostEstimate(flops=2 * T * T * T, bytes_accessed=1000, transcendentals=0),
        name="early",
    )(xin, mk)


def halo_mask(mk, pa):
    own = own_masks(mk)

    def mask(i, j):
        if 0 <= i < R or 0 <= j < R:
            return own(i, j)
        n = MASKS.index((max(i, j) + 8, min(i, j) + 8))
        return pa[pl.ds(NA * B + n, 1), :].astype(F32)

    return mask


def unpack(ref, off, packs, base, aux, xh, one):
    r, c_ = iotas(B)
    n_off = len(off)

    def dst(h, c):
        I, J = h // 2 - 4, c // 2 - 4
        return (I + 4, pl.ds((h % 2) * B, B), pl.ds((J - I + 2) * T + (c % 2) * B, B))

    tiles = set()
    for n, (h, c) in enumerate(off):
        xh[dst(h, c)] = ref[pl.ds(n * B, B), :]
        if h // 2 == c // 2:
            xh[dst(c, h)] = nt(one[:B, :B], ref[pl.ds(n * B, B), :]).astype(BF)
        else:
            tiles.add((h // 2 - 4, c // 2 - 4))
    for k, (h, g) in enumerate(packs):
        both = ref[pl.ds((base + k) * B, B), :]
        turned = nt(one[:B, :B], both)
        both = both.astype(F32)
        xh[dst(h, h)] = jnp.where(r <= c_, both, turned).astype(BF)
        other = jnp.where(r < c_, turned, both)
        diagonal = ref[pl.ds(aux + k, 1), :].astype(F32)
        xh[dst(g, g)] = jnp.where(r == c_, diagonal, other).astype(BF)
    for I, J in sorted(tiles):
        for a in range(2):
            for b in range(2):
                if abs(2 * I + a - 2 * J - b) > 4:
                    xh[dst(2 * I + a + 8, 2 * J + b + 8)] = jnp.zeros((B, B), BF)
        xh[xh_at(J, I)] = nt(one, xh[xh_at(I, J)]).astype(BF)


S_CROSS = [(0, -2), (0, -1), (1, -1)]
CENTRE = [(r, c) for r in range(4, 9) for c in range(2, 9) if abs(r - c) <= 4 and not (r < 6 and c < 6) and (r < 6 or c < 6)]
CORNER = [(r, c) for r in range(6, 9) for c in range(6, 9)]


def put_swap(store, swap, blocks, I, J):
    def both(a, b, v):
        store(a, b, v)
        at = (R - 1 - 2 * I - a, R - 1 - 2 * J - b)
        if at in blocks:
            swap[blocks.index(at)] = v

    return both


def corner_kernel(pa, xb01, acc, mk, xh_in, sb_in, d1_in, xh, sb, d1, swap):
    del xh_in, sb_in, d1_in
    mask = halo_mask(mk, pa)
    one = eye()
    unpack(pa, A_OFF, A_PACK, len(A_OFF), NA * B + len(MASKS), xh, one)
    xs = rows_of(xb01, xh)
    ss = square_rows(sb)

    for I, J in S_CROSS:
        put_masked(sb_store(sb, I, J), nt(xs(I, I - 2, J + 2), xs(J, I - 2, J + 2)), I, J, mask)
    terms = {(0, 0): -2, (0, 1): -1, (1, 0): -1, (1, 1): -1}
    for n, (I, J) in enumerate(D1_CORNER):
        lo = terms[I, J]
        cube = acc[n] + nt(ss(I, lo, -1), xs(J, lo, -1))
        store = put_swap(d1_store(d1, I, J), swap, CORNER, I, J)
        put_step(store, xs(I, J, J), cube, I, J, mask)
    for I, J in S_CROSS:
        cube = nt(ss(I, I - 2, J + 2), xs(J, I - 2, J + 2))
        put_step(d1_store(d1, I, J), xs(I, J, J), cube, I, J, mask)


def corner(pa, xb01, acc, mk, xh, sb, d1):
    return pl.pallas_call(
        corner_kernel,
        out_shape=[HROWS, HROWS, D1, jax.ShapeDtypeStruct((len(CORNER), B, B), BF)],
        in_specs=[VM] * 7,
        out_specs=[VM] * 4,
        input_output_aliases={4: 0, 5: 1, 6: 2},
        compiler_params=pltpu.CompilerParams(vmem_limit_bytes=16 * MIB),
        cost_estimate=pl.CostEstimate(flops=2 * 32 * T * T * T, bytes_accessed=1000, transcendentals=0),
        name="corner",
    )(pa, xb01, acc, mk, xh, sb, d1)


H = R // 2
Q = 2 * SHARE
M = H * Q
S_PART = [(-1, -1), (-2, -2), (-1, -2)]
D1_HALO = [(-2, 0), (-1, 0), (-1, 1), (-1, -1), (-1, -2), (-2, -1), (-2, -2)]
LEFT = jax.ShapeDtypeStruct((M, 7 * T), BF)


def chip_share():
    layer = lax.axis_index("layer")
    return lax.rem(layer, 2), pl.multiple_of(lax.div(layer, 2) * Q, Q)


def in_rows(J):
    return max(0, 2 * J - 4), min(H - 1, 2 * J + 5)


def put_left(left, d1, i, J, chip_rows):
    I, a = i // 2, i % 2
    dst = (pl.ds(i * Q, Q), pl.ds((J + 2) * T, T))
    if abs(I - J) <= 2:
        left[dst] = d1[J + 2, pl.ds((I - J + 2) * T + a * B + chip_rows, Q), :]
    else:
        left[dst] = jnp.zeros((Q, T), BF)


def product(lhs, d1, J, i0, i1, k0, k1):
    a = lhs[pl.ds(i0 * Q, (i1 - i0 + 1) * Q), pl.ds((k0 + 2) * T, (k1 - k0 + 1) * T)]
    return nn(a, d1[J + 2, pl.ds((k0 - J + 2) * T, (k1 - k0 + 1) * T), :])


def beside_kernel(xb01, mk, xh, sb, d1_in, d1, left, sp, xp, s1p):
    del mk, d1_in
    _, chip_rows = chip_share()
    one = eye()
    xs = rows_of(xb01, xh)

    def ss(I, m):
        return nt(one, sb[sb_at(m, I)]).astype(BF)

    turned = {(-2, 0): ss(-2, 0), (-1, 0): ss(-1, 0), (-1, 1): ss(-1, 1)}
    for n, (I, J) in enumerate(S_PART):
        sp[n] = nt(xs(I, -2, J + 2 if I >= J else I + 2), xs(J, -2, J + 2 if I >= J else I + 2))
    for n, (I, J) in enumerate(D1_HALO):
        total = None
        for m in range(min(I, J) + 3):
            term = nt(turned[I, m], xs(J, m, m))
            total = term if total is None else total + term
        xp[n] = total
    for i in range(H):
        for J in range(-2, 5):
            if not (i == 4 and J >= 3):
                put_left(left, d1, i, J, chip_rows)
    for J, k1 in [(-2, 0), (-1, 1), (0, 2)]:
        i0, i1 = in_rows(J)
        s1p[pl.ds(i0 * Q, (i1 - i0 + 1) * Q), pl.ds((J + 2) * T, T)] = product(left, d1, J, i0, i1, 0, k1)


def beside(xb01, mk, xh, sb, d1):
    return pl.pallas_call(
        beside_kernel,
        out_shape=[
            D1,
            LEFT,
            jax.ShapeDtypeStruct((len(S_PART), T, T), F32),
            jax.ShapeDtypeStruct((len(D1_HALO), T, T), F32),
            jax.ShapeDtypeStruct((M, 3 * T), F32),
        ],
        in_specs=[VM] * 5,
        out_specs=[VM] * 5,
        input_output_aliases={4: 0},
        compiler_params=pltpu.CompilerParams(vmem_limit_bytes=16 * MIB),
        cost_estimate=pl.CostEstimate(flops=1000, bytes_accessed=1000, transcendentals=0),
        name="beside",
    )(xb01, mk, xh, sb, d1)


def put_square(s1, s, J, i0, mask):
    i1 = i0 + s.shape[0] // Q - 1
    for i in range(H):
        for b in range(2):
            j = 2 * J + b
            dst = (pl.ds(i * Q, Q), pl.ds((J + 2) * T + b * B, B))
            if abs(i - j) <= 4:
                assert i0 <= i <= i1
                q = s[(i - i0) * Q : (i - i0 + 1) * Q, b * B : (b + 1) * B]
                s1[dst] = (q * mask(i, j)).astype(BF)
            else:
                s1[dst] = jnp.zeros((Q, B), BF)


def swapped_kernel(centre, swapped, mk, left_in, d1_in, left, d1, s1, s1q, x2p):
    del left_in, d1_in
    _, chip_rows = chip_share()
    mask = own_masks(mk)

    def put(r, c, v):
        d1_store(d1, r // 2, c // 2)(r % 2, c % 2, v)

    for ref, blocks in ((centre, CENTRE), (swapped, CORNER)):
        for n, (r, c) in enumerate(blocks):
            put(r, c, ref[n])
    for k in range(4, R):
        put(k, R - 1, jnp.zeros((B, B), BF))
        if k < R - 1:
            put(R - 1, k, jnp.zeros((B, B), BF))
    put(7, 2, jnp.zeros((B, B), BF))
    for J in (3, 4):
        put_left(left, d1, 4, J, chip_rows)
    for J in (2, 3, 4):
        i0, i1 = in_rows(J)
        put_square(s1, product(left, d1, J, i0, i1, max(J - 2, 0), 4), J, i0, mask)
    s1q[...] = product(left, d1, 1, 0, H - 1, 0, 3)
    for J in range(5):
        i0, i1 = in_rows(J)
        part = product(s1, d1, J, i0, i1, 2, min(J + 2, 4))
        x2p[pl.ds(i0 * Q, (i1 - i0 + 1) * Q), pl.ds(J * T, T)] = part


def use_swapped(centre, swapped, mk, left, d1):
    return pl.pallas_call(
        swapped_kernel,
        out_shape=[
            LEFT,
            D1,
            LEFT,
            jax.ShapeDtypeStruct((M, T), F32),
            jax.ShapeDtypeStruct((M, 5 * T), F32),
        ],
        in_specs=[VM] * 5,
        out_specs=[VM] * 5,
        input_output_aliases={3: 0, 4: 1},
        compiler_params=pltpu.CompilerParams(vmem_limit_bytes=16 * MIB),
        cost_estimate=pl.CostEstimate(flops=1000, bytes_accessed=1000, transcendentals=0),
        name="use_swapped",
    )(centre, swapped, mk, left, d1)


def finish_kernel(pa, pb, xb01, mk, left, sp, xp, s1p, s1q, x2p, xh_in, sb_in, d1_in, s1_in, xh, sb, d1, s1, keep, send):
    del xh_in, sb_in, d1_in, s1_in
    flip, _ = chip_share()
    mask = halo_mask(mk, pa)
    one = eye()
    unpack(pb, B_OFF + C_OFF, C_PACK, NB - 2, NB * B, xh, one)
    xs = rows_of(xb01, xh)
    ss = square_rows(sb)

    for n, (I, J) in enumerate(S_PART):
        lo = max(I, J) - 2
        put_masked(sb_store(sb, I, J), sp[n] + nt(xs(I, lo, -3), xs(J, lo, -3)), I, J, mask)
    sb[sb_at(-2, -1)] = nt(one, ss(-1, -2, -2)).astype(BF)
    for I, J in [(-1, -3), (-2, -3), (-2, -4)]:
        put_masked(sb_store(sb, I, J), nt(xs(I, I - 2, J + 2), xs(J, I - 2, J + 2)), I, J, mask)

    for n, (I, J) in enumerate(D1_HALO):
        lo = max(I, J) - 2
        put_step(d1_store(d1, I, J), xs(I, J, J), xp[n] + nt(ss(I, lo, -1), xs(J, lo, -1)), I, J, mask)

    for J in (1, 0, -1, -2):
        i0, i1 = in_rows(J)
        near = min(i1, 3)
        part = product(left, d1, J, i0, near, max(J - 2, -2), -1)
        rows = pl.ds(i0 * Q, (near - i0 + 1) * Q)
        rest = s1q if J == 1 else s1p
        cols = pl.ds(0, T) if J == 1 else pl.ds((J + 2) * T, T)
        total = part + rest[rows, cols]
        if i1 > near:
            total = jnp.concatenate([total, rest[pl.ds((near + 1) * Q, (i1 - near) * Q), cols]], axis=0)
        put_square(s1, total, J, i0, mask)

    for J in range(4, -3, -1):
        i0, i1 = in_rows(J)
        rows = pl.ds(i0 * Q, (i1 - i0 + 1) * Q)
        k0 = max(J - 2, -2)
        if J == 4:
            cube = x2p[rows, pl.ds(J * T, T)]
        else:
            cube = product(s1, d1, J, i0, i1, k0, min(J + 2, 1))
            if J >= 0:
                cube = cube + x2p[rows, pl.ds(J * T, T)]
        for i in range(i0, i1 + 1):
            for b in range(2):
                j = 2 * J + b
                if abs(i - j) > 4:
                    continue
                q = cube[(i - i0) * Q : (i - i0 + 1) * Q, b * B : (b + 1) * B] * mask(i, j)
                x = left[pl.ds(i * Q, Q), pl.ds((J + 2) * T + b * B, B)].astype(F32)
                v = (3.0 * x - q * SCALE) * 0.5
                w = j - i + 4
                near = jnp.where(flip == 1, H - 1 - i, i)
                slot = jnp.where(flip == 1, W - 1 - w, w)
                lo, hi = v[:SHARE].astype(BF), v[SHARE:].astype(BF)
                keep[near, slot] = jnp.where(flip == 1, hi, lo)
                send[near, slot] = jnp.where(flip == 1, lo, hi)


def finish(pa, pb, xb01, mk, left, sp, xp, s1p, s1q, x2p, xh, sb, d1, s1):
    half = jax.ShapeDtypeStruct((H, W, SHARE, B), BF)
    return pl.pallas_call(
        finish_kernel,
        out_shape=[HROWS, HROWS, D1, LEFT, half, half],
        in_specs=[VM] * 14,
        out_specs=[VM] * 6,
        input_output_aliases={10: 0, 11: 1, 12: 2, 13: 3},
        compiler_params=pltpu.CompilerParams(vmem_limit_bytes=16 * MIB),
        cost_estimate=pl.CostEstimate(flops=2 * 70 * T * T * T, bytes_accessed=8 * MIB, transcendentals=0),
        name="finish",
    )(pa, pb, xb01, mk, left, sp, xp, s1p, s1q, x2p, xh, sb, d1, s1)


def join_kernel(keep, other, out, sem):
    flip = flip_core()
    a = pltpu.make_async_copy(keep, out.at[pl.ds(jnp.where(flip == 1, H, 0), H)], sem.at[0])
    b = pltpu.make_async_copy(other, out.at[pl.ds(jnp.where(flip == 1, 0, H), H)], sem.at[1])
    a.start()
    b.start()
    a.wait()
    b.wait()


def join(keep, other):
    return pl.pallas_call(
        join_kernel,
        out_shape=jax.ShapeDtypeStruct((R, W, SHARE, B), BF),
        in_specs=[VM, VM],
        out_specs=HBM,
        scratch_shapes=[pltpu.SemaphoreType.DMA((2,))],
        compiler_params=pltpu.CompilerParams(vmem_limit_bytes=2 * MIB),
        name="join",
    )(keep, other)


def chain(layers, grid):
    pairs = []
    for l in range(layers):
        for g in range(grid):
            pairs.append((l * grid + g, l * grid + (g + 1 if l % 2 == 0 else g - 1) % grid))
    return pairs


def per_device(x, ret):
    layers, grid = lax.axis_size("layer"), lax.axis_size("grid")
    cores = [(l, l ^ 1) for l in range(layers)]
    pairs = chain(layers, grid)
    x = pltpu.with_memory_space_constraint(x, pltpu.HBM)
    ret = pltpu.with_memory_space_constraint(ret, pltpu.HBM)
    pa = pack_corner(x, ret)
    pb, xin, mk = pack_deep(x, ret, pa)
    pa = lax.ppermute(pa, ("layer", "grid"), pairs)
    pb = lax.ppermute(pb, ("layer", "grid"), pairs)
    xb01, xh, sb, acc, d1, centre = early(xin, mk)
    centre = lax.ppermute(centre, "layer", cores)
    xh, sb, d1, swap = corner(pa, xb01, acc, mk, xh, sb, d1)
    swapped = lax.ppermute(swap, "layer", cores)
    d1, left, sp, xp, s1p = beside(xb01, mk, xh, sb, d1)
    left, d1, s1, s1q, x2p = use_swapped(centre, swapped, mk, left, d1)
    *_, keep, send = finish(pa, pb, xb01, mk, left, sp, xp, s1p, s1q, x2p, xh, sb, d1, s1)
    other = lax.ppermute(send, "layer", cores)
    return join(keep, other)


def solution(mesh):
    return jax.shard_map(
        per_device,
        mesh=mesh,
        in_specs=(P("grid", None, None, None), P("grid", None)),
        out_specs=P("grid", None, "layer", None),
        check_vma=False,
    )
```

time: 177 us -> 28.7 us (0.16)
  waiting for transfers between devices: 105 us -> 1.62 us
  matrix products: 23.1 us -> 0 us
  Pallas kernels: 0 us -> 14 us
  between operations: 13.5 us -> 0.23 us
  other arithmetic: 12.5 us -> 0 us
  starting transfers between devices: 17.4 us -> 12.7 us
  local copies, waits for them, and re-layouts: 4.53 us -> 0 us
    all_gather x1 -> x0, waiting for transfers between devices: 55.3 us -> none  [per_device(): whole_rows = lax.all_gather(quarter, 'layer', axis=2, tiled=True)]
    ppermute x4 -> x5, waiting for transfers between devices: 50.1 us -> 1.62 us  [the longest x1 1.31 us: per_device(): other = lax.ppermute(send, 'layer', cores)]
    dot_general x36 -> x0, matrix products: 23.1 us -> none  [strip_product(): jnp.einsum('rab,rwbc->rwac', left_rows[:, offset], source, preferred_elem...]
    pallas_call x0 -> x8, Pallas kernels: none -> 14 us  [the longest x1 3.35 us: early(): pl.pallas_call(early_kernel, out_shape=[jax.ShapeDtypeStruct((2, T, 5 * T...]
    concatenate x2 -> x0, other arithmetic: 9.7 us -> none  [extended(): block = jnp.concatenate([low, block, high], axis=dim)]
    ppermute x4 -> x5, starting transfers between devices: 17.4 us -> 12.7 us  [the longest x1 9.9 us: per_device(): pa = lax.ppermute(pa, ('layer', 'grid'), pairs)]
    slice x2 -> x0, local copies, waits for them, and re-layouts: 3.5 us -> none  [extended(): lax.slice_in_dim(block, block.shape[dim] - width, None, axis=dim)]
    select_n x1 -> x0, other arithmetic: 2.1 us -> none  [per_device(): whole_rows = jnp.where(kept, band_blocks, jnp.zeros_like(band_blocks))]
  transfers between devices with their start and end apart: 5 -> 5, of which waited for: 3 -> 2; matrix products, arithmetic and copies ran while one was open for 1% -> 0% of each run, Pallas kernels for 0% -> 32%
where the time goes in v3:
time: 28.7 us; the launch traced here: 28.6 us
  Pallas kernels  14 us (49%)
  starting transfers between devices  12.7 us (44%)
  waiting for transfers between devices  1.62 us (6%)
    ppermute x1, starting transfers between devices, per_device(): pa = lax.ppermute(pa, ('layer', 'grid'), pairs)  9.9 us
    pallas_call x1, Pallas kernels, early(): pl.pallas_call(early_kernel, out_shape=[jax.ShapeDtypeStruct((2, T, 5 * T...  3.35 us
    pallas_call x1, Pallas kernels, finish(): pl.pallas_call(finish_kernel, out_shape=[HROWS, HROWS, D1, LEFT, half, ha...  2.87 us
    pallas_call x1, Pallas kernels, pack_deep(): pl.pallas_call(pack_deep_kernel, out_shape=[jax.ShapeDtypeStruct((B_ROWS,...  1.86 us
    pallas_call x1, Pallas kernels, corner(): pl.pallas_call(corner_kernel, out_shape=[HROWS, HROWS, D1, jax.ShapeDtype...  1.5 us
    ppermute x1, starting transfers between devices, per_device(): other = lax.ppermute(send, 'layer', cores)  1.34 us
    ppermute x1, waiting for transfers between devices, per_device(): other = lax.ppermute(send, 'layer', cores)  1.31 us
    pallas_call x1, Pallas kernels, use_swapped(): pl.pallas_call(swapped_kernel, out_shape=[LEFT, D1, LEFT, jax.ShapeDtypeS...  1.28 us
  transfers between devices with their start and end apart: 5, of which 2 were waited for; matrix products, arithmetic and copies ran while one was open for 0% of the time, Pallas kernels for 32%

profile of v3, /device:TPU:1, one launch (start us, length us, event | category | flops | bytes accessed | tf_op | source)
XLA Modules:
  0.0 28.6 jit_solution(9100823386541197016)
XLA Ops:
  0.0 1.1 %pack_corner.1.first = bf16[1056,128]{1,0:T(8,128)(2,1)S(1)} custom-call(bf16[10,9,128,128]{3,2,1,0:T(8,128)(2,1)} %x.3, s32[10,9]{1,0:T(8,128)} %ret.3), custom_call_target="tpu_custom_call" | custom-call | flops 1000 | bytes 1048576 | tf_op jit(solution)/shard_map/pack_corner/pallas_call | solution.py:151
  1.1 9.9 %collective-permute-start = (bf16[1056,128]{1,0:T(8,128)(2,1)S(1)}, bf16[1056,128]{1,0:T(8,128)(2,1)S(1)}, u32[]{:S(2)}, u32[]{:S(2)}) collective-permute-start(bf16[1056,128]{1,0:T(8,128)(2,1)S(1)} %pack_corner.1.first), channel_id=1, source_target_pairs={{0,1},{1,2},{2,3},{3,4},{4,5},{5,6},{6,7},{7,8},{8,9},{9,10},{10,1... | collective-permute-start | bytes 811016 | tf_op jit(solution)/shard_map/ppermute | solution.py:675
  11.0 1.9 %pack_deep.1 = (bf16[2320,128]{1,0:T(8,128)(2,1)S(1)}, bf16[10,9,128,128]{3,2,1,0:T(8,128)(2,1)S(1)}, f32[96,128]{1,0:T(8,128)S(1)}) custom-call(bf16[10,9,128,128]{3,2,1,0:T(8,128)(2,1)} %x.3, s32[10,9]{1,0:T(8,128)} %ret.3, bf16[1056,128]{1,0:T(8,128)(2,1)S(1)} %pack_corner.1.first), custom_call_target="tpu_custom_call" | custom-call | flops 1000 | bytes 4194304 | tf_op jit(solution)/shard_map/pack_deep/pallas_call | solution.py:200
  12.8 0.6 %collective-permute-start.1 = (bf16[2320,128]{1,0:T(8,128)(2,1)S(1)}, bf16[2320,128]{1,0:T(8,128)(2,1)S(1)}, u32[]{:S(2)}, u32[]{:S(2)}) collective-permute-start(bf16[2320,128]{1,0:T(8,128)(2,1)S(1)} %get-tuple-element.30), channel_id=1, source_target_pairs={{0,1},{1,2},{2,3},{3,4},{4,5},{5,6},{6,7},{7,8},{8,9},{9,10},{10,1... | collective-permute-start | bytes 1781768 | tf_op jit(solution)/shard_map/ppermute | solution.py:676
  13.5 3.3 %early.1 = (bf16[2,256,1280]{2,1,0:T(8,128)(2,1)S(1)}, bf16[4,256,1280]{2,1,0:T(8,128)(2,1)S(1)}, bf16[4,256,1280]{2,1,0:T(8,128)(2,1)S(1)}, f32[4,256,256]{2,1,...) custom-call(bf16[10,9,128,128]{3,2,1,0:T(8,128)(2,1)S(1)} %get-tuple-element.31.xin, ...), custom_call_target="tpu_custom_call" | custom-call | flops 33554432 | bytes 1000 | tf_op jit(solution)/shard_map/early/pallas_call | solution.py:316
  16.8 0.1 collective-permute-start.2
  16.9 0.0 collective-permute-done.pa
  16.9 1.5 %corner.1 = (bf16[4,256,1280]{2,1,0:T(8,128)(2,1)S(1)}, bf16[4,256,1280]{2,1,0:T(8,128)(2,1)S(1)}, bf16[7,1280,256]{2,1,0:T(8,128)(2,1)S(1)}, bf16[9,128,128]{2,1,0:T(8,128)(2,1)S(1)}) custom-call(bf16[1056,128]{1,0:T(8,128)(2,1)S(1)} %collective-permute-done.pa, ...), custom_call_target="tpu_custom_call", output_to_operand_aliasing={{0}: (4, {}), {1}: (5, {}), {2}: (6, {})} | custom-call | flops 1073741824 | bytes 1000 | tf_op jit(solution)/shard_map/corner/pallas_call | solution.py:415
  18.4 0.8 %collective-permute-start.3 = (bf16[9,128,128]{2,1,0:T(8,128)(2,1)S(1)}, bf16[9,128,128]{2,1,0:T(8,128)(2,1)S(1)}, u32[]{:S(2)}, u32[]{:S(2)}) collective-permute-start(bf16[9,128,128]{2,1,0:T(8,128)(2,1)S(1)} %get-tuple-element.39), channel_id=1, source_target_pairs={{0,64},{64,0},{128,192},{192,128},{1,65},{65,1},{129,193},{193,129... | collective-permute-start | bytes 884744 | tf_op jit(solution)/shard_map/ppermute | solution.py:680
  19.2 1.2 %beside.1 = (bf16[7,1280,256]{2,1,0:T(8,128)(2,1)S(1)}, bf16[320,1792]{1,0:T(8,128)(2,1)S(1)}, f32[3,256,256]{2,1,0:T(8,128)S(1)}, f32[7,256,256]{2,1,0:T(8,128)S(1)}, f32[320,768]{1,0:T(8,128)S(1)}) custom-call(bf16[2,256,1280]{2,1,0:T(8,128)(2,1)S(1)} %get-tuple-element.33.xb01, ...), custom_call_target="tpu_custom_call", output_to_operand_aliasing={{0}: (4, {})} | custom-call | flops 1000 | bytes 1000 | tf_op jit(solution)/shard_map/beside/pallas_call | solution.py:486
  20.4 0.0 collective-permute-done.2.centre
  20.4 0.0 collective-permute-done.3.swapped
  20.4 1.3 %use_swapped.1 = (bf16[320,1792]{1,0:T(8,128)(2,1)S(1)}, bf16[7,1280,256]{2,1,0:T(8,128)(2,1)S(1)}, bf16[320,1792]{1,0:T(8,128)(2,1)S(1)}, f32[320,256]{1,0:T(8,128)S(1)}, f32[320,1280]{1,0:T(8,128)S(1)}) custom-call(bf16[15,128,128]{2,1,0:T(8,128)(2,1)S(1)} %collective-permute-done.2.centre, ...), custom_call_target="tpu_custom_call", output_to_operand_aliasing={{0}: (3, {}), {1}: (4, {})} | custom-call | flops 1000 | bytes 1000 | tf_op jit(solution)/shard_map/use_swapped/pallas_call | solution.py:547
  21.7 0.3 %collective-permute-done.1.pb = bf16[2320,128]{1,0:T(8,128)(2,1)S(1)} collective-permute-done((bf16[2320,128]{1,0:T(8,128)(2,1)S(1)}, bf16[2320,128]{1,0:T(8,128)(2,1)S(1)}, u32[]{:S(2)}, u32[]{:S(2)}) %collective-permute-start.1) | collective-permute-done | bytes 593952 | tf_op jit(solution)/shard_map/ppermute | solution.py:676
  22.0 2.9 %finish.1 = (bf16[4,256,1280]{2,1,0:T(8,128)(2,1)S(1)}, bf16[4,256,1280]{2,1,0:T(8,128)(2,1)S(1)}, bf16[7,1280,256]{2,1,0:T(8,128)(2,1)S(1)}, bf16[320,1792]{1,0...) custom-call(bf16[1056,128]{1,0:T(8,128)(2,1)S(1)} %collective-permut, ...), custom_call_target="tpu_custom_call", output_to_operand_aliasing={{0}: (10, {}), {1}: (11, {}), {2}: (12, {}), {3}: (13, {})} | custom-call | flops 2348810240 | bytes 8388608 | tf_op jit(solution)/shard_map/finish/pallas_call | solution.py:625
  24.9 1.3 %collective-permute-start.4 = (bf16[5,9,32,128]{3,2,1,0:T(8,128)(2,1)S(1)}, bf16[5,9,32,128]{3,2,1,0:T(8,128)(2,1)S(1)}, u32[]{:S(2)}, u32[]{:S(2)}) collective-permute-start(bf16[5,9,32,128]{3,2,1,0:T(8,128)(2,1)S(1)} %get-tuple-element.54), channel_id=1, source_target_pairs={{0,64},{64,0},{128,192},{192,128},{1,65},{65,1},{129,193},{193,129... | collective-permute-start | bytes 1105928 | tf_op jit(solution)/shard_map/ppermute | solution.py:684
  26.2 1.3 %collective-permute-done.4.other = bf16[5,9,32,128]{3,2,1,0:T(8,128)(2,1)S(1)} collective-permute-done((bf16[5,9,32,128]{3,2,1,0:T(8,128)(2,1)S(1)}, bf16[5,9,32,128]{3,2,1,0:T(8,128)(2,1)S(1)}, u32[]{:S(2)}, u32[]{:S(2)}) %collective-permute-start.4) | collective-permute-done | bytes 368672 | tf_op jit(solution)/shard_map/ppermute | solution.py:684
  27.5 0.9 %join.1 = bf16[10,9,32,128]{3,2,1,0:T(8,128)(2,1)} custom-call(bf16[5,9,32,128]{3,2,1,0:T(8,128)(2,1)S(1)} %get-tuple-element.53.keep, bf16[5,9,32,128]{3,2,1,0:T(8,128)(2,1)S(1)} %collective-permute-done.4.other), custom_call_target="tpu_custom_call" | custom-call | tf_op jit(solution)/shard_map/join/pallas_call | solution.py:648
Async XLA Ops:
  1.1 15.8 %collective-permute-start = (bf16[1056,128]{1,0:T(8,128)(2,1)S(1)}, bf16[1056,128]{1,0:T(8,128)(2,1)S(1)}, u32[]{:S(2)}, u32[]{:S(2)}) collective-permute-start(bf16[1056,128]{1,0:T(8,128)(2,1)S(1)} %pack_corner.1.first), channel_id=1, source_target_pairs={{0,1},{1,2},{2,3},{3,4},{4,5},{5,6},{6,7},{7,8},{8,9},{9,10},{10,1... | collective-permute-start | bytes 811016 | tf_op jit(solution)/shard_map/ppermute | solution.py:675
  12.8 9.2 %collective-permute-start.1 = (bf16[2320,128]{1,0:T(8,128)(2,1)S(1)}, bf16[2320,128]{1,0:T(8,128)(2,1)S(1)}, u32[]{:S(2)}, u32[]{:S(2)}) collective-permute-start(bf16[2320,128]{1,0:T(8,128)(2,1)S(1)} %get-tuple-element.30), channel_id=1, source_target_pairs={{0,1},{1,2},{2,3},{3,4},{4,5},{5,6},{6,7},{7,8},{8,9},{9,10},{10,1... | collective-permute-start | bytes 1781768 | tf_op jit(solution)/shard_map/ppermute | solution.py:676
  16.8 3.6 %collective-permute-start.2 = (bf16[15,128,128]{2,1,0:T(8,128)(2,1)S(1)}, bf16[15,128,128]{2,1,0:T(8,128)(2,1)S(1)}, u32[]{:S(2)}, u32[]{:S(2)}) collective-permute-start(bf16[15,128,128]{2,1,0:T(8,128)(2,1)S(1)} %get-tuple-element.34), channel_id=1, source_target_pairs={{0,64},{64,0},{128,192},{192,128},{1,65},{65,1},{129,193},{193,129... | collective-permute-start | bytes 1474568 | tf_op jit(solution)/shard_map/ppermute | solution.py:678
  18.4 2.0 %collective-permute-start.3 = (bf16[9,128,128]{2,1,0:T(8,128)(2,1)S(1)}, bf16[9,128,128]{2,1,0:T(8,128)(2,1)S(1)}, u32[]{:S(2)}, u32[]{:S(2)}) collective-permute-start(bf16[9,128,128]{2,1,0:T(8,128)(2,1)S(1)} %get-tuple-element.39), channel_id=1, source_target_pairs={{0,64},{64,0},{128,192},{192,128},{1,65},{65,1},{129,193},{193,129... | collective-permute-start | bytes 884744 | tf_op jit(solution)/shard_map/ppermute | solution.py:680
  24.9 2.7 %collective-permute-start.4 = (bf16[5,9,32,128]{3,2,1,0:T(8,128)(2,1)S(1)}, bf16[5,9,32,128]{3,2,1,0:T(8,128)(2,1)S(1)}, u32[]{:S(2)}, u32[]{:S(2)}) collective-permute-start(bf16[5,9,32,128]{3,2,1,0:T(8,128)(2,1)S(1)} %get-tuple-element.54), channel_id=1, source_target_pairs={{0,64},{64,0},{128,192},{192,128},{1,65},{65,1},{129,193},{193,129... | collective-permute-start | bytes 1105928 | tf_op jit(solution)/shard_map/ppermute | solution.py:684

commit v4 on v3

--- a/solution.py
+++ b/solution.py
@@ -23,9 +23,10 @@
 C_PACK = [(h - 4, c - 4) for h, c in A_PACK]
 MASKS = A_PAIRS + B_OFF
 NA = len(A_OFF) + 2
-NB = len(B_OFF) + len(C_OFF) + 2
+NC = len(C_OFF) + 2
 A_ROWS = NA * B + 32
-B_ROWS = NB * B + 16
+B_ROWS = len(B_OFF) * B
+C_ROWS = NC * B + 16
 
 HBM = pl.BlockSpec(memory_space=pltpu.HBM)
 VM = pl.BlockSpec(memory_space=pltpu.VMEM)
@@ -118,6 +119,8 @@
         out[pl.ds((len(off) + k) * B, B), :] = jnp.where(r <= c, first, second).astype(BF)
         rows.append(jnp.sum(jnp.where(r == c, second, 0.0), axis=0, keepdims=True))
     n_rows = out.shape[0] - aux
+    if not n_rows:
+        return
     rows.append(jnp.zeros((n_rows - len(rows), B), F32))
     out[pl.ds(aux, n_rows), :] = jnp.concatenate(rows, axis=0).astype(BF)
 
@@ -168,8 +171,7 @@
 MK = R * W + 6
 
 
-def pack_deep_kernel(x, ret, first, out, xin, mk, smem, sem, ret_sem):
-    del first
+def pack_deep_body(x, ret, pb, pc, xin, mk, smem, sem, ret_sem):
     flip = flip_core()
     load = pltpu.make_async_copy(ret, smem, ret_sem)
     load.start()
@@ -191,36 +193,33 @@
         m = jnp.full((16, B), smem_mask(smem, flip, h + 2, g + 2), F32).astype(BF)
         return xin[h + 2, slot] * whole(m)
 
-    send_rows(out, B_OFF + C_OFF, C_PACK, [], get, None)
+    send_rows(pb, B_OFF, [], [], get, None)
+    send_rows(pc, C_OFF, C_PACK, [], get, None)
     copies[0].wait()
     copies[1].wait()
 
 
-def pack_deep(x, ret, first):
-    return pl.pallas_call(
-        pack_deep_kernel,
-        out_shape=[
-            jax.ShapeDtypeStruct((B_ROWS, B), BF),
-            jax.ShapeDtypeStruct((R, W, B, B), BF),
-            jax.ShapeDtypeStruct((MK, B), F32),
-        ],
-        in_specs=[HBM, HBM, VM],
-        out_specs=[VM] * 3,
-        scratch_shapes=[
-            pltpu.SMEM((R, W), jnp.int32),
-            pltpu.SemaphoreType.DMA((R,)),
-            pltpu.SemaphoreType.DMA,
-        ],
-        compiler_params=pltpu.CompilerParams(vmem_limit_bytes=8 * MIB),
-        cost_estimate=pl.CostEstimate(flops=1000, bytes_accessed=4 * MIB, transcendentals=0),
-        name="pack_deep",
-    )(x, ret, first)
-
-
-D1_EARLY = [(0, 2), (2, 0), (1, 2), (2, 1), (2, 2), (1, 3)]
+CORNER = [(r, c) for r in range(6, 9) for c in range(6, 9)]
+CUT = 5
+
+
+def put_swap(store, swap_a, swap_b, I, J):
+    def both(a, b, v):
+        store(a, b, v)
+        at = (R - 1 - 2 * I - a, R - 1 - 2 * J - b)
+        if at in CORNER:
+            n = CORNER.index(at)
+            if n < CUT:
+                swap_a[n] = v
+            else:
+                swap_b[n - CUT] = v
+
+    return both
+
+
+D1_EARLY = [(0, 2), (2, 0), (1, 2), (2, 1), (2, 2), (1, 3), (3, 1), (2, 3), (3, 2), (2, 4), (4, 2)]
 D1_CORNER = [(0, 0), (0, 1), (1, 0), (1, 1)]
-S_EARLY = [(0, 0), (0, 1), (0, 2), (1, 1), (1, 2), (1, 3), (2, 2), (2, 3), (2, 4)]
-S_TURNED = [(0, 1), (0, 2), (1, 2)]
+S_EARLY = [(I, J) for I in range(5) for J in range(I, min(I + 3, 5))]
 D1 = jax.ShapeDtypeStruct((7, 5 * T, T), BF)
 HROWS = jax.ShapeDtypeStruct((4, T, 5 * T), BF)
 
@@ -263,7 +262,7 @@
     return mask
 
 
-def early_kernel(xin, mk, xb01, xh, sb, acc, d1, centre, xb, s):
+def early_body(xin, mk, xb01, xh, sb, acc, d1, xb, s):
     flip = flip_core()
     mask = own_masks(mk)
 
@@ -298,7 +297,7 @@
             s[I, pl.ds(a * B, B), pl.ds((J - I + 2) * T + b * B, B)] = v
 
         put_masked(store, nt(xs(I, J - 2, I + 2), xs(J, J - 2, I + 2)), I, J, mask)
-        if (I, J) in S_TURNED:
+        if I < J:
             s[J, :, pl.ds((I - J + 2) * T, T)] = nt(one, ss(I, J, J)).astype(BF)
 
     for n, (I, J) in enumerate(D1_CORNER):
@@ -308,28 +307,97 @@
 
     for I, J in D1_EARLY:
         lo, hi = max(I, J) - 2, min(I, J) + 2
-        store = put_swap(d1_store(d1, I, J), centre, CENTRE, I, J)
-        put_step(store, xs(I, J, J), nt(ss(I, lo, hi), xs(J, lo, hi)), I, J, mask)
-
-
-def early(xin, mk):
+        put_step(d1_store(d1, I, J), xs(I, J, J), nt(ss(I, lo, hi), xs(J, lo, hi)), I, J, mask)
+
+
+PB = jax.ShapeDtypeStruct((B_ROWS, B), BF)
+PC = jax.ShapeDtypeStruct((C_ROWS, B), BF)
+XIN = jax.ShapeDtypeStruct((R, W, B, B), BF)
+MASK_ROWS = jax.ShapeDtypeStruct((MK, B), F32)
+EARLY = [
+    jax.ShapeDtypeStruct((2, T, 5 * T), BF),
+    HROWS,
+    HROWS,
+    jax.ShapeDtypeStruct((4, T, T), F32),
+    D1,
+]
+DEEP_SCRATCH = [
+    pltpu.SMEM((R, W), jnp.int32),
+    pltpu.SemaphoreType.DMA((R,)),
+    pltpu.SemaphoreType.DMA,
+]
+EARLY_SCRATCH = [pltpu.VMEM((5, T, 5 * T), BF), pltpu.VMEM((5, T, 5 * T), BF)]
+
+
+AHEAD = 5
+
+
+def goes_ahead():
+    return jnp.logical_and(lax.axis_index("grid") < AHEAD, flip_core() == 1)
+
+
+def ahead_kernel(x, ret, pa_in, pa, pb, pc, xin, mk, *refs):
+    del pa_in, pa
+    outs, scratch = refs[: len(EARLY)], refs[len(EARLY) :]
+
+    @pl.when(goes_ahead())
+    def _():
+        pack_deep_body(x, ret, pb, pc, xin, mk, *scratch[2:])
+        early_body(xin, mk, *outs, *scratch[:2])
+
+
+def ahead(x, ret, pa):
+    return pl.pallas_call(
+        ahead_kernel,
+        out_shape=[jax.ShapeDtypeStruct((A_ROWS, B), BF), PB, PC, XIN, MASK_ROWS, *EARLY],
+        in_specs=[HBM, HBM, VM],
+        out_specs=[VM] * (5 + len(EARLY)),
+        scratch_shapes=EARLY_SCRATCH + DEEP_SCRATCH,
+        input_output_aliases={2: 0},
+        compiler_params=pltpu.CompilerParams(vmem_limit_bytes=24 * MIB),
+        cost_estimate=pl.CostEstimate(flops=1000, bytes_accessed=1000, transcendentals=0),
+        name="ahead",
+    )(x, ret, pa)
+
+
+def pack_deep_kernel(x, ret, *refs):
+    @pl.when(jnp.logical_not(goes_ahead()))
+    def _():
+        pack_deep_body(x, ret, *refs[4:])
+
+
+def pack_deep(x, ret, pb, pc, xin, mk):
+    return pl.pallas_call(
+        pack_deep_kernel,
+        out_shape=[PB, PC, XIN, MASK_ROWS],
+        in_specs=[HBM, HBM, VM, VM, VM, VM],
+        out_specs=[VM] * 4,
+        scratch_shapes=DEEP_SCRATCH,
+        input_output_aliases={2: 0, 3: 1, 4: 2, 5: 3},
+        compiler_params=pltpu.CompilerParams(vmem_limit_bytes=8 * MIB),
+        cost_estimate=pl.CostEstimate(flops=1000, bytes_accessed=4 * MIB, transcendentals=0),
+        name="pack_deep",
+    )(x, ret, pb, pc, xin, mk)
+
+
+def early_kernel(xin, mk, *refs):
+    @pl.when(jnp.logical_not(goes_ahead()))
+    def _():
+        early_body(xin, mk, *refs[len(EARLY) :])
+
+
+def early(xin, mk, *outs):
     return pl.pallas_call(
         early_kernel,
-        out_shape=[
-            jax.ShapeDtypeStruct((2, T, 5 * T), BF),
-            HROWS,
-            HROWS,
-            jax.ShapeDtypeStruct((4, T, T), F32),
-            D1,
-            jax.ShapeDtypeStruct((len(CENTRE), B, B), BF),
-        ],
-        in_specs=[VM] * 2,
-        out_specs=[VM] * 6,
-        scratch_shapes=[pltpu.VMEM((5, T, 5 * T), BF), pltpu.VMEM((3, T, 5 * T), BF)],
+        out_shape=EARLY,
+        in_specs=[VM] * (2 + len(EARLY)),
+        out_specs=[VM] * len(EARLY),
+        scratch_shapes=EARLY_SCRATCH,
+        input_output_aliases={2 + n: n for n in range(len(EARLY))},
         compiler_params=pltpu.CompilerParams(vmem_limit_bytes=24 * MIB),
         cost_estimate=pl.CostEstimate(flops=2 * T * T * T, bytes_accessed=1000, transcendentals=0),
         name="early",
-    )(xin, mk)
+    )(xin, mk, *outs)
 
 
 def halo_mask(mk, pa):
@@ -376,21 +444,7 @@
 
 
 S_CROSS = [(0, -2), (0, -1), (1, -1)]
-CENTRE = [(r, c) for r in range(4, 9) for c in range(2, 9) if abs(r - c) <= 4 and not (r < 6 and c < 6) and (r < 6 or c < 6)]
-CORNER = [(r, c) for r in range(6, 9) for c in range(6, 9)]
-
-
-def put_swap(store, swap, blocks, I, J):
-    def both(a, b, v):
-        store(a, b, v)
-        at = (R - 1 - 2 * I - a, R - 1 - 2 * J - b)
-        if at in blocks:
-            swap[blocks.index(at)] = v
-
-    return both
-
-
-def corner_kernel(pa, xb01, acc, mk, xh_in, sb_in, d1_in, xh, sb, d1, swap):
+def corner_kernel(pa, xb01, acc, mk, xh_in, sb_in, d1_in, xh, sb, d1, swap_a, swap_b):
     del xh_in, sb_in, d1_in
     mask = halo_mask(mk, pa)
     one = eye()
@@ -404,7 +458,7 @@
     for n, (I, J) in enumerate(D1_CORNER):
         lo = terms[I, J]
         cube = acc[n] + nt(ss(I, lo, -1), xs(J, lo, -1))
-        store = put_swap(d1_store(d1, I, J), swap, CORNER, I, J)
+        store = put_swap(d1_store(d1, I, J), swap_a, swap_b, I, J)
         put_step(store, xs(I, J, J), cube, I, J, mask)
     for I, J in S_CROSS:
         cube = nt(ss(I, I - 2, J + 2), xs(J, I - 2, J + 2))
@@ -414,9 +468,15 @@
 def corner(pa, xb01, acc, mk, xh, sb, d1):
     return pl.pallas_call(
         corner_kernel,
-        out_shape=[HROWS, HROWS, D1, jax.ShapeDtypeStruct((len(CORNER), B, B), BF)],
+        out_shape=[
+            HROWS,
+            HROWS,
+            D1,
+            jax.ShapeDtypeStruct((CUT, B, B), BF),
+            jax.ShapeDtypeStruct((len(CORNER) - CUT, B, B), BF),
+        ],
         in_specs=[VM] * 7,
-        out_specs=[VM] * 4,
+        out_specs=[VM] * 5,
         input_output_aliases={4: 0, 5: 1, 6: 2},
         compiler_params=pltpu.CompilerParams(vmem_limit_bytes=16 * MIB),
         cost_estimate=pl.CostEstimate(flops=2 * 32 * T * T * T, bytes_accessed=1000, transcendentals=0),
@@ -475,8 +535,7 @@
         xp[n] = total
     for i in range(H):
         for J in range(-2, 5):
-            if not (i == 4 and J >= 3):
-                put_left(left, d1, i, J, chip_rows)
+            put_left(left, d1, i, J, chip_rows)
     for J, k1 in [(-2, 0), (-1, 1), (0, 2)]:
         i0, i1 = in_rows(J)
         s1p[pl.ds(i0 * Q, (i1 - i0 + 1) * Q), pl.ds((J + 2) * T, T)] = product(left, d1, J, i0, i1, 0, k1)
@@ -515,24 +574,19 @@
                 s1[dst] = jnp.zeros((Q, B), BF)
 
 
-def swapped_kernel(centre, swapped, mk, left_in, d1_in, left, d1, s1, s1q, x2p):
-    del left_in, d1_in
-    _, chip_rows = chip_share()
+def swapped_kernel(swap_a, swap_b, mk, left, d1_in, d1, s1, s1q, x2p):
+    del d1_in
     mask = own_masks(mk)
 
     def put(r, c, v):
         d1_store(d1, r // 2, c // 2)(r % 2, c % 2, v)
 
-    for ref, blocks in ((centre, CENTRE), (swapped, CORNER)):
-        for n, (r, c) in enumerate(blocks):
-            put(r, c, ref[n])
-    for k in range(4, R):
+    for n, (r, c) in enumerate(CORNER):
+        put(r, c, swap_a[n] if n < CUT else swap_b[n - CUT])
+    for k in range(6, R):
         put(k, R - 1, jnp.zeros((B, B), BF))
         if k < R - 1:
             put(R - 1, k, jnp.zeros((B, B), BF))
-    put(7, 2, jnp.zeros((B, B), BF))
-    for J in (3, 4):
-        put_left(left, d1, 4, J, chip_rows)
     for J in (2, 3, 4):
         i0, i1 = in_rows(J)
         put_square(s1, product(left, d1, J, i0, i1, max(J - 2, 0), 4), J, i0, mask)
@@ -543,31 +597,58 @@
         x2p[pl.ds(i0 * Q, (i1 - i0 + 1) * Q), pl.ds(J * T, T)] = part
 
 
-def use_swapped(centre, swapped, mk, left, d1):
+def use_swapped(swap_a, swap_b, mk, left, d1):
     return pl.pallas_call(
         swapped_kernel,
-        out_shape=[
-            LEFT,
-            D1,
-            LEFT,
-            jax.ShapeDtypeStruct((M, T), F32),
-            jax.ShapeDtypeStruct((M, 5 * T), F32),
-        ],
+        out_shape=[D1, LEFT, jax.ShapeDtypeStruct((M, T), F32), jax.ShapeDtypeStruct((M, 5 * T), F32)],
         in_specs=[VM] * 5,
-        out_specs=[VM] * 5,
-        input_output_aliases={3: 0, 4: 1},
+        out_specs=[VM] * 4,
+        input_output_aliases={4: 0},
         compiler_params=pltpu.CompilerParams(vmem_limit_bytes=16 * MIB),
         cost_estimate=pl.CostEstimate(flops=1000, bytes_accessed=1000, transcendentals=0),
         name="use_swapped",
-    )(centre, swapped, mk, left, d1)
-
-
-def finish_kernel(pa, pb, xb01, mk, left, sp, xp, s1p, s1q, x2p, xh_in, sb_in, d1_in, s1_in, xh, sb, d1, s1, keep, send):
+    )(swap_a, swap_b, mk, left, d1)
+
+
+S_DEEP = [(-1, -3), (-2, -3), (-2, -4)]
+D1_DEEP = [(-1, -1), (-1, -2), (-2, -1), (-2, -2)]
+HALF = jax.ShapeDtypeStruct((H, W, SHARE, B), BF)
+X2C = jax.ShapeDtypeStruct((M, 4 * T), F32)
+
+
+def emit(keep, send, flip, left, mask, J, i0, cube):
+    for i in range(i0, i0 + cube.shape[0] // Q):
+        for b in range(2):
+            j = 2 * J + b
+            if abs(i - j) > 4:
+                continue
+            q = cube[(i - i0) * Q : (i - i0 + 1) * Q, b * B : (b + 1) * B] * mask(i, j)
+            x = left[pl.ds(i * Q, Q), pl.ds((J + 2) * T + b * B, B)].astype(F32)
+            v = (3.0 * x - q * SCALE) * 0.5
+            w = j - i + 4
+            near = jnp.where(flip == 1, H - 1 - i, i)
+            slot = jnp.where(flip == 1, W - 1 - w, w)
+            lo, hi = v[:SHARE].astype(BF), v[SHARE:].astype(BF)
+            keep[near, slot] = jnp.where(flip == 1, hi, lo)
+            send[near, slot] = jnp.where(flip == 1, lo, hi)
+
+
+def plus(part, i0, whole_ref, cols, j0, j1):
+    n = part.shape[0] // Q
+    assert j0 == i0
+    total = part + whole_ref[pl.ds(i0 * Q, n * Q), cols]
+    if j1 >= i0 + n:
+        total = jnp.concatenate([total, whole_ref[pl.ds((i0 + n) * Q, (j1 - i0 - n + 1) * Q), cols]], axis=0)
+    return total
+
+
+def middle_kernel(pa, pb, xb01, mk, left, sp, xp, s1p, s1q, x2p, xh_in, sb_in, d1_in, s1_in, *outs):
     del xh_in, sb_in, d1_in, s1_in
+    xh, sb, d1, s1, sdp, xc, x2c, keep, send = outs
     flip, _ = chip_share()
     mask = halo_mask(mk, pa)
     one = eye()
-    unpack(pb, B_OFF + C_OFF, C_PACK, NB - 2, NB * B, xh, one)
+    unpack(pb, B_OFF, [], 0, 0, xh, one)
     xs = rows_of(xb01, xh)
     ss = square_rows(sb)
 
@@ -575,85 +656,141 @@
         lo = max(I, J) - 2
         put_masked(sb_store(sb, I, J), sp[n] + nt(xs(I, lo, -3), xs(J, lo, -3)), I, J, mask)
     sb[sb_at(-2, -1)] = nt(one, ss(-1, -2, -2)).astype(BF)
-    for I, J in [(-1, -3), (-2, -3), (-2, -4)]:
-        put_masked(sb_store(sb, I, J), nt(xs(I, I - 2, J + 2), xs(J, I - 2, J + 2)), I, J, mask)
-
+    for n, (I, J) in enumerate(S_DEEP):
+        sdp[n] = nt(xs(I, -2, J + 2), xs(J, -2, J + 2))
     for n, (I, J) in enumerate(D1_HALO):
         lo = max(I, J) - 2
-        put_step(d1_store(d1, I, J), xs(I, J, J), xp[n] + nt(ss(I, lo, -1), xs(J, lo, -1)), I, J, mask)
-
-    for J in (1, 0, -1, -2):
-        i0, i1 = in_rows(J)
-        near = min(i1, 3)
-        part = product(left, d1, J, i0, near, max(J - 2, -2), -1)
-        rows = pl.ds(i0 * Q, (near - i0 + 1) * Q)
-        rest = s1q if J == 1 else s1p
-        cols = pl.ds(0, T) if J == 1 else pl.ds((J + 2) * T, T)
-        total = part + rest[rows, cols]
-        if i1 > near:
-            total = jnp.concatenate([total, rest[pl.ds((near + 1) * Q, (i1 - near) * Q), cols]], axis=0)
-        put_square(s1, total, J, i0, mask)
+        total = xp[n] + nt(ss(I, max(lo, -2), -1), xs(J, max(lo, -2), -1))
+        if (I, J) in D1_DEEP:
+            xc[D1_DEEP.index((I, J))] = total
+        else:
+            put_step(d1_store(d1, I, J), xs(I, J, J), total, I, J, mask)
+
+    part = product(left, d1, 1, 0, 3, -1, -1)
+    put_square(s1, plus(part, 0, s1q, pl.ds(0, T), 0, 4), 1, 0, mask)
+    part = product(left, d1, 0, 0, 3, -2, -1)
+    put_square(s1, plus(part, 0, s1p, pl.ds(2 * T, T), 0, 4), 0, 0, mask)
 
     for J in range(4, -3, -1):
         i0, i1 = in_rows(J)
         rows = pl.ds(i0 * Q, (i1 - i0 + 1) * Q)
-        k0 = max(J - 2, -2)
         if J == 4:
-            cube = x2p[rows, pl.ds(J * T, T)]
+            total = x2p[rows, pl.ds(J * T, T)]
         else:
-            cube = product(s1, d1, J, i0, i1, k0, min(J + 2, 1))
+            total = product(s1, d1, J, i0, i1, max(J - 2, 0), min(J + 2, 1))
             if J >= 0:
-                cube = cube + x2p[rows, pl.ds(J * T, T)]
-        for i in range(i0, i1 + 1):
-            for b in range(2):
-                j = 2 * J + b
-                if abs(i - j) > 4:
-                    continue
-                q = cube[(i - i0) * Q : (i - i0 + 1) * Q, b * B : (b + 1) * B] * mask(i, j)
-                x = left[pl.ds(i * Q, Q), pl.ds((J + 2) * T + b * B, B)].astype(F32)
-                v = (3.0 * x - q * SCALE) * 0.5
-                w = j - i + 4
-                near = jnp.where(flip == 1, H - 1 - i, i)
-                slot = jnp.where(flip == 1, W - 1 - w, w)
-                lo, hi = v[:SHARE].astype(BF), v[SHARE:].astype(BF)
-                keep[near, slot] = jnp.where(flip == 1, hi, lo)
-                send[near, slot] = jnp.where(flip == 1, lo, hi)
-
-
-def finish(pa, pb, xb01, mk, left, sp, xp, s1p, s1q, x2p, xh, sb, d1, s1):
-    half = jax.ShapeDtypeStruct((H, W, SHARE, B), BF)
-    return pl.pallas_call(
-        finish_kernel,
-        out_shape=[HROWS, HROWS, D1, LEFT, half, half],
+                total = total + x2p[rows, pl.ds(J * T, T)]
+        if J >= 2:
+            emit(keep, send, flip, left, mask, J, i0, total)
+        else:
+            x2c[rows, pl.ds((J + 2) * T, T)] = total
+
+
+def middle(pa, pb, xb01, mk, left, sp, xp, s1p, s1q, x2p, xh, sb, d1, s1):
+    return pl.pallas_call(
+        middle_kernel,
+        out_shape=[
+            HROWS,
+            HROWS,
+            D1,
+            LEFT,
+            jax.ShapeDtypeStruct((len(S_DEEP), T, T), F32),
+            jax.ShapeDtypeStruct((len(D1_DEEP), T, T), F32),
+            X2C,
+            HALF,
+            HALF,
+        ],
         in_specs=[VM] * 14,
-        out_specs=[VM] * 6,
+        out_specs=[VM] * 9,
         input_output_aliases={10: 0, 11: 1, 12: 2, 13: 3},
         compiler_params=pltpu.CompilerParams(vmem_limit_bytes=16 * MIB),
-        cost_estimate=pl.CostEstimate(flops=2 * 70 * T * T * T, bytes_accessed=8 * MIB, transcendentals=0),
+        cost_estimate=pl.CostEstimate(flops=1000, bytes_accessed=1000, transcendentals=0),
+        name="middle",
+    )(pa, pb, xb01, mk, left, sp, xp, s1p, s1q, x2p, xh, sb, d1, s1)
+
+
+def finish_kernel(pa, pc, xb01, mk, left, s1p, sdp, xc, x2c, *refs):
+    xh, sb, d1, s1, keep, send = refs[6:]
+    flip, _ = chip_share()
+    mask = halo_mask(mk, pa)
+    unpack(pc, C_OFF, C_PACK, len(C_OFF), NC * B, xh, eye())
+    xs = rows_of(xb01, xh)
+    ss = square_rows(sb)
+
+    for n, (I, J) in enumerate(S_DEEP):
+        lo = I - 2
+        put_masked(sb_store(sb, I, J), sdp[n] + nt(xs(I, lo, -3), xs(J, lo, -3)), I, J, mask)
+    for n, (I, J) in enumerate(D1_DEEP):
+        lo = max(I, J) - 2
+        put_step(d1_store(d1, I, J), xs(I, J, J), xc[n] + nt(ss(I, lo, -3), xs(J, lo, -3)), I, J, mask)
+    for J in (-1, -2):
+        i0, i1 = in_rows(J)
+        part = product(left, d1, J, i0, i1, -2, -1)
+        put_square(s1, part + s1p[pl.ds(i0 * Q, (i1 - i0 + 1) * Q), pl.ds((J + 2) * T, T)], J, i0, mask)
+    for J in (1, 0, -1, -2):
+        i0, i1 = in_rows(J)
+        part = product(s1, d1, J, i0, min(i1, 3), max(J - 2, -2), -1)
+        emit(keep, send, flip, left, mask, J, i0, plus(part, i0, x2c, pl.ds((J + 2) * T, T), i0, i1))
+
+
+def finish(pa, pc, xb01, mk, left, s1p, sdp, xc, x2c, xh, sb, d1, s1, keep, send):
+    return pl.pallas_call(
+        finish_kernel,
+        out_shape=[HROWS, HROWS, D1, LEFT, HALF, HALF],
+        in_specs=[VM] * 15,
+        out_specs=[VM] * 6,
+        input_output_aliases={9 + n: n for n in range(6)},
+        compiler_params=pltpu.CompilerParams(vmem_limit_bytes=16 * MIB),
+        cost_estimate=pl.CostEstimate(flops=2 * 30 * T * T * T, bytes_accessed=4 * MIB, transcendentals=0),
         name="finish",
-    )(pa, pb, xb01, mk, left, sp, xp, s1p, s1q, x2p, xh, sb, d1, s1)
-
-
-def join_kernel(keep, other, out, sem):
-    flip = flip_core()
-    a = pltpu.make_async_copy(keep, out.at[pl.ds(jnp.where(flip == 1, H, 0), H)], sem.at[0])
-    b = pltpu.make_async_copy(other, out.at[pl.ds(jnp.where(flip == 1, 0, H), H)], sem.at[1])
-    a.start()
-    b.start()
-    a.wait()
-    b.wait()
-
-
-def join(keep, other):
+    )(pa, pc, xb01, mk, left, s1p, sdp, xc, x2c, xh, sb, d1, s1, keep, send)
+
+
+def half_out(src, out, sem, first):
+    copies = []
+    for n in range(H):
+        copies.append(pltpu.make_async_copy(src.at[n], out.at[first + n], sem.at[n]))
+        copies[-1].start()
+    for copy in copies:
+        copy.wait()
+
+
+def keep_kernel(keep, out, sem):
+    half_out(keep, out, sem, jnp.where(flip_core() == 1, H, 0))
+
+
+def join_kernel(other, out_in, out, sem):
+    del out_in
+    half_out(other, out, sem, jnp.where(flip_core() == 1, 0, H))
+
+
+OUT = jax.ShapeDtypeStruct((R, W, SHARE, B), BF)
+
+
+def put_keep(keep):
+    return pl.pallas_call(
+        keep_kernel,
+        out_shape=OUT,
+        in_specs=[VM],
+        out_specs=HBM,
+        scratch_shapes=[pltpu.SemaphoreType.DMA((H,))],
+        compiler_params=pltpu.CompilerParams(vmem_limit_bytes=2 * MIB),
+        cost_estimate=pl.CostEstimate(flops=1000, bytes_accessed=1000, transcendentals=0),
+        name="put_keep",
+    )(keep)
+
+
+def join(other, out):
     return pl.pallas_call(
         join_kernel,
-        out_shape=jax.ShapeDtypeStruct((R, W, SHARE, B), BF),
-        in_specs=[VM, VM],
+        out_shape=OUT,
+        in_specs=[VM, HBM],
         out_specs=HBM,
-        scratch_shapes=[pltpu.SemaphoreType.DMA((2,))],
+        scratch_shapes=[pltpu.SemaphoreType.DMA((H,))],
+        input_output_aliases={1: 0},
         compiler_params=pltpu.CompilerParams(vmem_limit_bytes=2 * MIB),
         name="join",
-    )(keep, other)
+    )(other, out)
 
 
 def chain(layers, grid):
@@ -670,19 +807,23 @@
     pairs = chain(layers, grid)
     x = pltpu.with_memory_space_constraint(x, pltpu.HBM)
     ret = pltpu.with_memory_space_constraint(ret, pltpu.HBM)
-    pa = pack_corner(x, ret)
-    pb, xin, mk = pack_deep(x, ret, pa)
+    pa, pb, pc, xin, mk, *outs = ahead(x, ret, pack_corner(x, ret))
     pa = lax.ppermute(pa, ("layer", "grid"), pairs)
+    pb, pc, xin, mk = pack_deep(x, ret, pb, pc, xin, mk)
     pb = lax.ppermute(pb, ("layer", "grid"), pairs)
-    xb01, xh, sb, acc, d1, centre = early(xin, mk)
-    centre = lax.ppermute(centre, "layer", cores)
-    xh, sb, d1, swap = corner(pa, xb01, acc, mk, xh, sb, d1)
-    swapped = lax.ppermute(swap, "layer", cores)
+    pc = lax.ppermute(pc, ("layer", "grid"), pairs)
+    xb01, xh, sb, acc, d1 = early(xin, mk, *outs)
+    xh, sb, d1, swap_a, swap_b = corner(pa, xb01, acc, mk, xh, sb, d1)
+    swap_a = lax.ppermute(swap_a, "layer", cores)
+    swap_b = lax.ppermute(swap_b, "layer", cores)
     d1, left, sp, xp, s1p = beside(xb01, mk, xh, sb, d1)
-    left, d1, s1, s1q, x2p = use_swapped(centre, swapped, mk, left, d1)
-    *_, keep, send = finish(pa, pb, xb01, mk, left, sp, xp, s1p, s1q, x2p, xh, sb, d1, s1)
+    d1, s1, s1q, x2p = use_swapped(swap_a, swap_b, mk, left, d1)
+    xh, sb, d1, s1, sdp, xc, x2c, keep, send = middle(
+        pa, pb, xb01, mk, left, sp, xp, s1p, s1q, x2p, xh, sb, d1, s1
+    )
+    *_, keep, send = finish(pa, pc, xb01, mk, left, s1p, sdp, xc, x2c, xh, sb, d1, s1, keep, send)
     other = lax.ppermute(send, "layer", cores)
-    return join(keep, other)
+    return join(other, put_keep(keep))
 
 
 def solution(mesh):

time: 28.7 us -> 27.5 us (0.958)
  starting transfers between devices: 12.7 us -> 9.42 us
  Pallas kernels: 14 us -> 16.5 us
  waiting for transfers between devices: 1.62 us -> 1.23 us
    ppermute x1, starting transfers between devices: 9.9 us -> 3.6 us  [per_device(): pa = lax.ppermute(pa, ('layer', 'grid'), pairs)]
    pallas_call x5 -> x8, Pallas kernels: 10.2 us -> 12.7 us  [the longest x1 6.41 us: ahead(): pl.pallas_call(ahead_kernel, out_shape=[jax.ShapeDtypeStruct((A_ROWS, B),...]
    ppermute x2 -> x3, starting transfers between devices: 0.85 us -> 2.93 us  [the longest x1 2.58 us: per_device(): swap_a = lax.ppermute(swap_a, 'layer', cores)]
    ppermute x1, starting transfers between devices: 0.62 us -> 2.38 us  [per_device(): pb = lax.ppermute(pb, ('layer', 'grid'), pairs)]
    ppermute x1, starting transfers between devices: 1.34 us -> 0.5 us  [per_device(): other = lax.ppermute(send, 'layer', cores)]
    ppermute x1, waiting for transfers between devices: 1.31 us -> 0.53 us  [per_device(): other = lax.ppermute(send, 'layer', cores)]
    ppermute x1, waiting for transfers between devices: 0.01 us -> 0.66 us  [per_device(): pa = lax.ppermute(pa, ('layer', 'grid'), pairs)]
    ppermute x1, waiting for transfers between devices: 0.3 us -> 0.01 us  [per_device(): pb = lax.ppermute(pb, ('layer', 'grid'), pairs)]
  transfers between devices with their start and end apart: 5 -> 6, of which waited for: 2 -> 2; matrix products, arithmetic and copies ran while one was open for 0% -> 0% of each run, Pallas kernels for 32% -> 24%
where the time goes in v4:
time: 27.5 us; the launch traced here: 27.4 us
  Pallas kernels  16.5 us (60%)
  starting transfers between devices  9.42 us (34%)
  waiting for transfers between devices  1.23 us (4%)
    pallas_call x1, Pallas kernels, ahead(): pl.pallas_call(ahead_kernel, out_shape=[jax.ShapeDtypeStruct((A_ROWS, B),...  6.41 us
    ppermute x1, starting transfers between devices, per_device(): pa = lax.ppermute(pa, ('layer', 'grid'), pairs)  3.6 us
    ppermute x1, starting transfers between devices, per_device(): swap_a = lax.ppermute(swap_a, 'layer', cores)  2.58 us
    ppermute x1, starting transfers between devices, per_device(): pb = lax.ppermute(pb, ('layer', 'grid'), pairs)  2.38 us
    pallas_call x1, Pallas kernels, middle(): pl.pallas_call(middle_kernel, out_shape=[HROWS, HROWS, D1, LEFT, jax.Shap...  1.91 us
    pallas_call x1, Pallas kernels, finish(): pl.pallas_call(finish_kernel, out_shape=[HROWS, HROWS, D1, LEFT, HALF, HA...  1.52 us
    pallas_call x1, Pallas kernels, corner(): pl.pallas_call(corner_kernel, out_shape=[HROWS, HROWS, D1, jax.ShapeDtype...  1.5 us
    pallas_call x1, Pallas kernels, beside(): pl.pallas_call(beside_kernel, out_shape=[D1, LEFT, jax.ShapeDtypeStruct((...  1.21 us
  transfers between devices with their start and end apart: 6, of which 2 were waited for; matrix products, arithmetic and copies ran while one was open for 0% of the time, Pallas kernels for 24%

profile of v4, /device:TPU:1, one launch (start us, length us, event | category | flops | bytes accessed | tf_op | source)
XLA Modules:
  0.0 27.4 jit_solution(10590661337683701277)
XLA Ops:
  0.0 1.1 %pack_corner.1.pa_in = bf16[1056,128]{1,0:T(8,128)(2,1)S(1)} custom-call(bf16[10,9,128,128]{3,2,1,0:T(8,128)(2,1)} %x.5, s32[10,9]{1,0:T(8,128)} %ret.5), custom_call_target="tpu_custom_call" | custom-call | flops 1000 | bytes 1048576 | tf_op jit(solution)/shard_map/pack_corner/pallas_call | solution.py:154
  1.1 6.4 %ahead.1 = (bf16[1056,128]{1,0:T(8,128)(2,1)S(1)}, bf16[1280,128]{1,0:T(8,128)(2,1)S(1)}, bf16[1040,128]{1,0:T(8,128)(2,1)S(1)}, bf16[10,9,128,128]{3,2,1,0:T(8,...) custom-call(bf16[10,9,128,128]{3,2,1,0:T(8,128)(2,1)} %x.5, ...), custom_call_target="tpu_custom_call", output_to_operand_aliasing={{0}: (2, {})} | custom-call | flops 1000 | bytes 1000 | tf_op jit(solution)/shard_map/ahead/pallas_call | solution.py:350
  7.5 3.6 %collective-permute-start = (bf16[1056,128]{1,0:T(8,128)(2,1)S(1)}, bf16[1056,128]{1,0:T(8,128)(2,1)S(1)}, u32[]{:S(2)}, u32[]{:S(2)}) collective-permute-start(bf16[1056,128]{1,0:T(8,128)(2,1)S(1)} %get-tuple-element.49), channel_id=1, source_target_pairs={{0,1},{1,2},{2,3},{3,4},{4,5},{5,6},{6,7},{7,8},{8,9},{9,10},{10,1... | collective-permute-start | bytes 811016 | tf_op jit(solution)/shard_map/ppermute | solution.py:811
  11.1 0.1 pack_deep.1
  11.2 2.4 %collective-permute-start.2 = (bf16[1280,128]{1,0:T(8,128)(2,1)S(1)}, bf16[1280,128]{1,0:T(8,128)(2,1)S(1)}, u32[]{:S(2)}, u32[]{:S(2)}) collective-permute-start(bf16[1280,128]{1,0:T(8,128)(2,1)S(1)} %get-tuple-element.72), channel_id=1, source_target_pairs={{0,1},{1,2},{2,3},{3,4},{4,5},{5,6},{6,7},{7,8},{8,9},{9,10},{10,1... | collective-permute-start | bytes 983048 | tf_op jit(solution)/shard_map/ppermute | solution.py:813
  13.6 0.3 collective-permute-start.1
  13.9 0.7 %collective-permute-done.pa = bf16[1056,128]{1,0:T(8,128)(2,1)S(1)} collective-permute-done((bf16[1056,128]{1,0:T(8,128)(2,1)S(1)}, bf16[1056,128]{1,0:T(8,128)(2,1)S(1)}, u32[]{:S(2)}, u32[]{:S(2)}) %collective-permute-start) | collective-permute-done | bytes 270368 | tf_op jit(solution)/shard_map/ppermute | solution.py:811
  14.5 1.5 %corner.1 = (bf16[4,256,1280]{2,1,0:T(8,128)(2,1)S(1)}, bf16[4,256,1280]{2,1,0:T(8,128)(2,1)S(1)}, bf16[7,1280,256]{2,1,0:T(8,128)(2,1)S(1)}, bf16[5,128,128]{2,1,0:T(8,128)(2,1)S(1)}, bf16[4,128,128]{2,1,0:T(8,128)(2,1)S(1)}) custom-call(bf16[1056,128]{1,0:T(8,128)(2,1)S(1)} %collective-permute-done.pa, ...), custom_call_target="tpu_custom_call", output_to_operand_aliasing={{0}: (4, {}), {1}: (5, {}), {2}: (6, {})} | custom-call | flops 1073741824 | bytes 1000 | tf_op jit(solution)/shard_map/corner/pallas_call | solution.py:469
  16.0 2.6 %collective-permute-start.3 = (bf16[5,128,128]{2,1,0:T(8,128)(2,1)S(1)}, bf16[5,128,128]{2,1,0:T(8,128)(2,1)S(1)}, u32[]{:S(2)}, u32[]{:S(2)}) collective-permute-start(bf16[5,128,128]{2,1,0:T(8,128)(2,1)S(1)} %get-tuple-element.75), channel_id=1, source_target_pairs={{0,64},{64,0},{128,192},{192,128},{1,65},{65,1},{129,193},{193,129... | collective-permute-start | bytes 491528 | tf_op jit(solution)/shard_map/ppermute | solution.py:817
  18.6 0.1 collective-permute-start.4
  18.7 1.2 %beside.1 = (bf16[7,1280,256]{2,1,0:T(8,128)(2,1)S(1)}, bf16[320,1792]{1,0:T(8,128)(2,1)S(1)}, f32[3,256,256]{2,1,0:T(8,128)S(1)}, f32[7,256,256]{2,1,0:T(8,128)S(1)}, f32[320,768]{1,0:T(8,128)S(1)}) custom-call(bf16[2,256,1280]{2,1,0:T(8,128)(2,1)S(1)} %get-tuple-element.62.xb01, ...), custom_call_target="tpu_custom_call", output_to_operand_aliasing={{0}: (4, {})} | custom-call | flops 1000 | bytes 1000 | tf_op jit(solution)/shard_map/beside/pallas_call | solution.py:545
  19.9 0.0 collective-permute-done.4.swap_b
  20.0 0.0 collective-permute-done.3.swap_a
  20.0 1.2 %use_swapped.1 = (bf16[7,1280,256]{2,1,0:T(8,128)(2,1)S(1)}, bf16[320,1792]{1,0:T(8,128)(2,1)S(1)}, f32[320,256]{1,0:T(8,128)S(1)}, f32[320,1280]{1,0:T(8,128)S(1)}) custom-call(bf16[5,128,128]{2,1,0:T(8,128)(2,1)S(1)} %collective-permute-done.3.swap_a, bf16[4,128,128]{2,1,0:T(8,128)(2,1)S(1)} %collective-permute-done.4.swap_b, ...), custom_call_target="tpu_custom_call", output_to_operand_aliasing={{0}: (4, {})} | custom-call | flops 1000 | bytes 1000 | tf_op jit(solution)/shard_map/use_swapped/pallas_call | solution.py:601
  21.1 0.0 collective-permute-done.2.pb
  21.2 1.9 %middle.1 = (bf16[4,256,1280]{2,1,0:T(8,128)(2,1)S(1)}, bf16[4,256,1280]{2,1,0:T(8,128)(2,1)S(1)}, bf16[7,1280,256]{2,1,0:T(8,128)(2,1)S(1)}, bf16[320,1792]{1,0...) custom-call(bf16[1056,128]{1,0:T(8,128)(2,1)S(1)} %collective-permut, ...), custom_call_target="tpu_custom_call", output_to_operand_aliasing={{0}: (10, {}), {1}: (11, {}), {2}: (12, {}), {3}: (13, {})} | custom-call | flops 1000 | bytes 1000 | tf_op jit(solution)/shard_map/middle/pallas_call | solution.py:690
  23.1 0.0 collective-permute-done.1.pc
  23.1 1.5 %finish.1 = (bf16[4,256,1280]{2,1,0:T(8,128)(2,1)S(1)}, bf16[4,256,1280]{2,1,0:T(8,128)(2,1)S(1)}, bf16[7,1280,256]{2,1,0:T(8,128)(2,1)S(1)}, bf16[320,1792]{1,0...) custom-call(bf16[1056,128]{1,0:T(8,128)(2,1)S(1)} %collective-permut, ...), custom_call_target="tpu_custom_call", output_to_operand_aliasing={{0}: (9, {}), {1}: (10, {}), {2}: (11, {}), {3}: (12, {}), ... | custom-call | flops 1006632960 | bytes 4194304 | tf_op jit(solution)/shard_map/finish/pallas_call | solution.py:737
  24.6 0.5 %collective-permute-start.5 = (bf16[5,9,32,128]{3,2,1,0:T(8,128)(2,1)S(1)}, bf16[5,9,32,128]{3,2,1,0:T(8,128)(2,1)S(1)}, u32[]{:S(2)}, u32[]{:S(2)}) collective-permute-start(bf16[5,9,32,128]{3,2,1,0:T(8,128)(2,1)S(1)} %get-tuple-element.91), channel_id=1, source_target_pairs={{0,64},{64,0},{128,192},{192,128},{1,65},{65,1},{129,193},{193,129... | collective-permute-start | bytes 1105928 | tf_op jit(solution)/shard_map/ppermute | solution.py:825
  25.1 0.8 %put_keep.1.out_in = bf16[10,9,32,128]{3,2,1,0:T(8,128)(2,1)} custom-call(bf16[5,9,32,128]{3,2,1,0:T(8,128)(2,1)S(1)} %get-tuple-element.92.keep), custom_call_target="tpu_custom_call" | custom-call | flops 1000 | bytes 1000 | tf_op jit(solution)/shard_map/put_keep/pallas_call | solution.py:771
  25.9 0.5 %collective-permute-done.5.other = bf16[5,9,32,128]{3,2,1,0:T(8,128)(2,1)S(1)} collective-permute-done((bf16[5,9,32,128]{3,2,1,0:T(8,128)(2,1)S(1)}, bf16[5,9,32,128]{3,2,1,0:T(8,128)(2,1)S(1)}, u32[]{:S(2)}, u32[]{:S(2)}) %collective-permute-start.5) | collective-permute-done | bytes 368672 | tf_op jit(solution)/shard_map/ppermute | solution.py:825
  26.4 0.8 %join.1 = bf16[10,9,32,128]{3,2,1,0:T(8,128)(2,1)} custom-call(bf16[5,9,32,128]{3,2,1,0:T(8,128)(2,1)S(1)} %collective-permute-done.5.other, bf16[10,9,32,128]{3,2,1,0:T(8,128)(2,1)} %put_keep.1.out_in), custom_call_target="tpu_custom_call", output_to_operand_aliasing={{}: (1, {})} | custom-call | tf_op jit(solution)/shard_map/join/pallas_call | solution.py:784
  (1 shorter events, 0.0 us)
Async XLA Ops:
  7.5 7.0 %collective-permute-start = (bf16[1056,128]{1,0:T(8,128)(2,1)S(1)}, bf16[1056,128]{1,0:T(8,128)(2,1)S(1)}, u32[]{:S(2)}, u32[]{:S(2)}) collective-permute-start(bf16[1056,128]{1,0:T(8,128)(2,1)S(1)} %get-tuple-element.49), channel_id=1, source_target_pairs={{0,1},{1,2},{2,3},{3,4},{4,5},{5,6},{6,7},{7,8},{8,9},{9,10},{10,1... | collective-permute-start | bytes 811016 | tf_op jit(solution)/shard_map/ppermute | solution.py:811
  11.2 9.9 %collective-permute-start.2 = (bf16[1280,128]{1,0:T(8,128)(2,1)S(1)}, bf16[1280,128]{1,0:T(8,128)(2,1)S(1)}, u32[]{:S(2)}, u32[]{:S(2)}) collective-permute-start(bf16[1280,128]{1,0:T(8,128)(2,1)S(1)} %get-tuple-element.72), channel_id=1, source_target_pairs={{0,1},{1,2},{2,3},{3,4},{4,5},{5,6},{6,7},{7,8},{8,9},{9,10},{10,1... | collective-permute-start | bytes 983048 | tf_op jit(solution)/shard_map/ppermute | solution.py:813
  13.6 9.5 %collective-permute-start.1 = (bf16[1040,128]{1,0:T(8,128)(2,1)S(1)}, bf16[1040,128]{1,0:T(8,128)(2,1)S(1)}, u32[]{:S(2)}, u32[]{:S(2)}) collective-permute-start(bf16[1040,128]{1,0:T(8,128)(2,1)S(1)} %get-tuple-element.54), channel_id=1, source_target_pairs={{0,1},{1,2},{2,3},{3,4},{4,5},{5,6},{6,7},{7,8},{8,9},{9,10},{10,1... | collective-permute-start | bytes 798728 | tf_op jit(solution)/shard_map/ppermute | solution.py:814
  16.0 3.9 %collective-permute-start.3 = (bf16[5,128,128]{2,1,0:T(8,128)(2,1)S(1)}, bf16[5,128,128]{2,1,0:T(8,128)(2,1)S(1)}, u32[]{:S(2)}, u32[]{:S(2)}) collective-permute-start(bf16[5,128,128]{2,1,0:T(8,128)(2,1)S(1)} %get-tuple-element.75), channel_id=1, source_target_pairs={{0,64},{64,0},{128,192},{192,128},{1,65},{65,1},{129,193},{193,129... | collective-permute-start | bytes 491528 | tf_op jit(solution)/shard_map/ppermute | solution.py:817
  18.6 1.3 %collective-permute-start.4 = (bf16[4,128,128]{2,1,0:T(8,128)(2,1)S(1)}, bf16[4,128,128]{2,1,0:T(8,128)(2,1)S(1)}, u32[]{:S(2)}, u32[]{:S(2)}) collective-permute-start(bf16[4,128,128]{2,1,0:T(8,128)(2,1)S(1)} %get-tuple-element.76), channel_id=1, source_target_pairs={{0,64},{64,0},{128,192},{192,128},{1,65},{65,1},{129,193},{193,129... | collective-permute-start | bytes 393224 | tf_op jit(solution)/shard_map/ppermute | solution.py:818
  24.6 1.8 %collective-permute-start.5 = (bf16[5,9,32,128]{3,2,1,0:T(8,128)(2,1)S(1)}, bf16[5,9,32,128]{3,2,1,0:T(8,128)(2,1)S(1)}, u32[]{:S(2)}, u32[]{:S(2)}) collective-permute-start(bf16[5,9,32,128]{3,2,1,0:T(8,128)(2,1)S(1)} %get-tuple-element.91), channel_id=1, source_target_pairs={{0,64},{64,0},{128,192},{192,128},{1,65},{65,1},{129,193},{193,129... | collective-permute-start | bytes 1105928 | tf_op jit(solution)/shard_map/ppermute | solution.py:825

commit v5 on v4

--- a/solution.py
+++ b/solution.py
@@ -709,8 +709,48 @@
     )(pa, pb, xb01, mk, left, sp, xp, s1p, s1q, x2p, xh, sb, d1, s1)
 
 
+def one_share(off, flip, mask, left, d1, s1p, x2c, sh, target):
+    def rows(ref, i1, cols):
+        at = [pl.multiple_of(i * Q + off, SHARE) for i in range(i1 + 1)]
+        return jnp.concatenate([ref[pl.ds(a, SHARE), cols] for a in at], axis=0)
+
+    for J in (-1, -2):
+        _, i1 = in_rows(J)
+        total = nn(rows(left, i1, pl.ds(0, 2 * T)), d1[J + 2, pl.ds(-J * T, 2 * T), :])
+        total = total + rows(s1p, i1, pl.ds((J + 2) * T, T))
+        for i in range(4):
+            for b in range(2):
+                j = 2 * J + b
+                dst = (pl.ds(i * SHARE, SHARE), pl.ds((J + 2) * T + b * B, B))
+                if abs(i - j) <= 4:
+                    q = total[i * SHARE : (i + 1) * SHARE, b * B : (b + 1) * B]
+                    sh[dst] = (q * mask(i, j)).astype(BF)
+                else:
+                    sh[dst] = jnp.zeros((SHARE, B), BF)
+    for J in (1, 0, -1, -2):
+        _, i1 = in_rows(J)
+        last = min(i1, 3)
+        k0 = max(J - 2, -2)
+        a = sh[pl.ds(0, (last + 1) * SHARE), pl.ds((k0 + 2) * T, -k0 * T)]
+        part = nn(a, d1[J + 2, pl.ds((k0 - J + 2) * T, -k0 * T), :])
+        for i in range(i1 + 1):
+            at = pl.multiple_of(i * Q + off, SHARE)
+            for b in range(2):
+                j = 2 * J + b
+                if abs(i - j) > 4:
+                    continue
+                q = x2c[pl.ds(at, SHARE), pl.ds((J + 2) * T + b * B, B)]
+                if i <= last:
+                    q = q + part[i * SHARE : (i + 1) * SHARE, b * B : (b + 1) * B]
+                x = left[pl.ds(at, SHARE), pl.ds((J + 2) * T + b * B, B)].astype(F32)
+                v = (3.0 * x - q * mask(i, j) * SCALE) * 0.5
+                near = jnp.where(flip == 1, H - 1 - i, i)
+                slot = jnp.where(flip == 1, W - 1 - (j - i + 4), j - i + 4)
+                target[near, slot] = v.astype(BF)
+
+
 def finish_kernel(pa, pc, xb01, mk, left, s1p, sdp, xc, x2c, *refs):
-    xh, sb, d1, s1, keep, send = refs[6:]
+    xh, sb, d1, send, sh = refs[4:]
     flip, _ = chip_share()
     mask = halo_mask(mk, pa)
     unpack(pc, C_OFF, C_PACK, len(C_OFF), NC * B, xh, eye())
@@ -723,27 +763,24 @@
     for n, (I, J) in enumerate(D1_DEEP):
         lo = max(I, J) - 2
         put_step(d1_store(d1, I, J), xs(I, J, J), xc[n] + nt(ss(I, lo, -3), xs(J, lo, -3)), I, J, mask)
-    for J in (-1, -2):
-        i0, i1 = in_rows(J)
-        part = product(left, d1, J, i0, i1, -2, -1)
-        put_square(s1, part + s1p[pl.ds(i0 * Q, (i1 - i0 + 1) * Q), pl.ds((J + 2) * T, T)], J, i0, mask)
-    for J in (1, 0, -1, -2):
-        i0, i1 = in_rows(J)
-        part = product(s1, d1, J, i0, min(i1, 3), max(J - 2, -2), -1)
-        emit(keep, send, flip, left, mask, J, i0, plus(part, i0, x2c, pl.ds((J + 2) * T, T), i0, i1))
-
-
-def finish(pa, pc, xb01, mk, left, s1p, sdp, xc, x2c, xh, sb, d1, s1, keep, send):
+    one_share((1 - flip) * SHARE, flip, mask, left, d1, s1p, x2c, sh, send)
+
+
+SH = pltpu.VMEM((4 * SHARE, 2 * T), BF)
+
+
+def finish(pa, pc, xb01, mk, left, s1p, sdp, xc, x2c, xh, sb, d1, send):
     return pl.pallas_call(
         finish_kernel,
-        out_shape=[HROWS, HROWS, D1, LEFT, HALF, HALF],
-        in_specs=[VM] * 15,
-        out_specs=[VM] * 6,
-        input_output_aliases={9 + n: n for n in range(6)},
+        out_shape=[HROWS, HROWS, D1, HALF],
+        in_specs=[VM] * 13,
+        out_specs=[VM] * 4,
+        scratch_shapes=[SH],
+        input_output_aliases={9 + n: n for n in range(4)},
         compiler_params=pltpu.CompilerParams(vmem_limit_bytes=16 * MIB),
         cost_estimate=pl.CostEstimate(flops=2 * 30 * T * T * T, bytes_accessed=4 * MIB, transcendentals=0),
         name="finish",
-    )(pa, pc, xb01, mk, left, s1p, sdp, xc, x2c, xh, sb, d1, s1, keep, send)
+    )(pa, pc, xb01, mk, left, s1p, sdp, xc, x2c, xh, sb, d1, send)
 
 
 def half_out(src, out, sem, first):
@@ -755,7 +792,10 @@
         copy.wait()
 
 
-def keep_kernel(keep, out, sem):
+def keep_kernel(mk, left, s1p, x2c, d1, keep_in, out, keep, sh, sem):
+    del keep_in
+    flip = flip_core()
+    one_share(flip * SHARE, flip, own_masks(mk), left, d1, s1p, x2c, sh, keep)
     half_out(keep, out, sem, jnp.where(flip_core() == 1, H, 0))
 
 
@@ -767,17 +807,18 @@
 OUT = jax.ShapeDtypeStruct((R, W, SHARE, B), BF)
 
 
-def put_keep(keep):
+def put_keep(mk, left, s1p, x2c, d1, keep):
     return pl.pallas_call(
         keep_kernel,
-        out_shape=OUT,
-        in_specs=[VM],
-        out_specs=HBM,
-        scratch_shapes=[pltpu.SemaphoreType.DMA((H,))],
-        compiler_params=pltpu.CompilerParams(vmem_limit_bytes=2 * MIB),
+        out_shape=[OUT, HALF],
+        in_specs=[VM] * 6,
+        out_specs=[HBM, VM],
+        scratch_shapes=[SH, pltpu.SemaphoreType.DMA((H,))],
+        input_output_aliases={5: 1},
+        compiler_params=pltpu.CompilerParams(vmem_limit_bytes=8 * MIB),
         cost_estimate=pl.CostEstimate(flops=1000, bytes_accessed=1000, transcendentals=0),
         name="put_keep",
-    )(keep)
+    )(mk, left, s1p, x2c, d1, keep)
 
 
 def join(other, out):
@@ -821,9 +862,10 @@
     xh, sb, d1, s1, sdp, xc, x2c, keep, send = middle(
         pa, pb, xb01, mk, left, sp, xp, s1p, s1q, x2p, xh, sb, d1, s1
     )
-    *_, keep, send = finish(pa, pc, xb01, mk, left, s1p, sdp, xc, x2c, xh, sb, d1, s1, keep, send)
+    _, _, d1, send = finish(pa, pc, xb01, mk, left, s1p, sdp, xc, x2c, xh, sb, d1, send)
     other = lax.ppermute(send, "layer", cores)
-    return join(other, put_keep(keep))
+    out, _ = put_keep(mk, left, s1p, x2c, d1, keep)
+    return join(other, out)
 
 
 def solution(mesh):

time: 27.5 us -> 27.4 us (level)
  waiting for transfers between devices: 1.23 us -> 0.75 us
  Pallas kernels: 16.5 us -> 16.8 us
    ppermute x1, waiting for transfers between devices: 0.53 us -> 0.06 us  [per_device(): other = lax.ppermute(send, 'layer', cores)]
    pallas_call x2, Pallas kernels: 2.29 us -> 2.58 us  [the longest x1 1.34 us: finish(): pl.pallas_call(finish_kernel, out_shape=[HROWS, HROWS, D1, HALF], in_spec...]
  transfers between devices with their start and end apart: 6 -> 6, of which waited for: 2 -> 2; matrix products, arithmetic and copies ran while one was open for 0% -> 0% of each run, Pallas kernels for 24% -> 26%
where the time goes in v5:
time: 27.4 us; the launch traced here: 27.2 us
  Pallas kernels  16.8 us (61%)
  starting transfers between devices  9.4 us (34%)
  waiting for transfers between devices  0.75 us (3%)
    pallas_call x1, Pallas kernels, ahead(): pl.pallas_call(ahead_kernel, out_shape=[jax.ShapeDtypeStruct((A_ROWS, B),...  6.42 us
    ppermute x1, starting transfers between devices, per_device(): pa = lax.ppermute(pa, ('layer', 'grid'), pairs)  3.59 us
    ppermute x1, starting transfers between devices, per_device(): swap_a = lax.ppermute(swap_a, 'layer', cores)  2.58 us
    ppermute x1, starting transfers between devices, per_device(): pb = lax.ppermute(pb, ('layer', 'grid'), pairs)  2.38 us
    pallas_call x1, Pallas kernels, middle(): pl.pallas_call(middle_kernel, out_shape=[HROWS, HROWS, D1, LEFT, jax.Shap...  1.93 us
    pallas_call x1, Pallas kernels, corner(): pl.pallas_call(corner_kernel, out_shape=[HROWS, HROWS, D1, jax.ShapeDtype...  1.5 us
    pallas_call x1, Pallas kernels, finish(): pl.pallas_call(finish_kernel, out_shape=[HROWS, HROWS, D1, HALF], in_spec...  1.34 us
    pallas_call x1, Pallas kernels, put_keep(): pl.pallas_call(keep_kernel, out_shape=[OUT, HALF], in_specs=[VM] * 6, out...  1.25 us
  transfers between devices with their start and end apart: 6, of which 2 were waited for; matrix products, arithmetic and copies ran while one was open for 0% of the time, Pallas kernels for 26%

profile of v5, /device:TPU:1, one launch (start us, length us, event | category | flops | bytes accessed | tf_op | source)
XLA Modules:
  0.0 27.2 jit_solution(653152322772636638)
XLA Ops:
  0.0 1.1 %pack_corner.1.pa_in = bf16[1056,128]{1,0:T(8,128)(2,1)S(1)} custom-call(bf16[10,9,128,128]{3,2,1,0:T(8,128)(2,1)} %x.5, s32[10,9]{1,0:T(8,128)} %ret.5), custom_call_target="tpu_custom_call" | custom-call | flops 1000 | bytes 1048576 | tf_op jit(solution)/shard_map/pack_corner/pallas_call | solution.py:154
  1.1 6.4 %ahead.1 = (bf16[1056,128]{1,0:T(8,128)(2,1)S(1)}, bf16[1280,128]{1,0:T(8,128)(2,1)S(1)}, bf16[1040,128]{1,0:T(8,128)(2,1)S(1)}, bf16[10,9,128,128]{3,2,1,0:T(8,...) custom-call(bf16[10,9,128,128]{3,2,1,0:T(8,128)(2,1)} %x.5, ...), custom_call_target="tpu_custom_call", output_to_operand_aliasing={{0}: (2, {})} | custom-call | flops 1000 | bytes 1000 | tf_op jit(solution)/shard_map/ahead/pallas_call | solution.py:350
  7.5 3.6 %collective-permute-start = (bf16[1056,128]{1,0:T(8,128)(2,1)S(1)}, bf16[1056,128]{1,0:T(8,128)(2,1)S(1)}, u32[]{:S(2)}, u32[]{:S(2)}) collective-permute-start(bf16[1056,128]{1,0:T(8,128)(2,1)S(1)} %get-tuple-element.49), channel_id=1, source_target_pairs={{0,1},{1,2},{2,3},{3,4},{4,5},{5,6},{6,7},{7,8},{8,9},{9,10},{10,1... | collective-permute-start | bytes 811016 | tf_op jit(solution)/shard_map/ppermute | solution.py:852
  11.1 0.1 pack_deep.1
  11.2 2.4 %collective-permute-start.2 = (bf16[1280,128]{1,0:T(8,128)(2,1)S(1)}, bf16[1280,128]{1,0:T(8,128)(2,1)S(1)}, u32[]{:S(2)}, u32[]{:S(2)}) collective-permute-start(bf16[1280,128]{1,0:T(8,128)(2,1)S(1)} %get-tuple-element.72), channel_id=1, source_target_pairs={{0,1},{1,2},{2,3},{3,4},{4,5},{5,6},{6,7},{7,8},{8,9},{9,10},{10,1... | collective-permute-start | bytes 983048 | tf_op jit(solution)/shard_map/ppermute | solution.py:854
  13.6 0.3 collective-permute-start.1
  13.9 0.7 %collective-permute-done.pa = bf16[1056,128]{1,0:T(8,128)(2,1)S(1)} collective-permute-done((bf16[1056,128]{1,0:T(8,128)(2,1)S(1)}, bf16[1056,128]{1,0:T(8,128)(2,1)S(1)}, u32[]{:S(2)}, u32[]{:S(2)}) %collective-permute-start) | collective-permute-done | bytes 270368 | tf_op jit(solution)/shard_map/ppermute | solution.py:852
  14.5 1.5 %corner.1 = (bf16[4,256,1280]{2,1,0:T(8,128)(2,1)S(1)}, bf16[4,256,1280]{2,1,0:T(8,128)(2,1)S(1)}, bf16[7,1280,256]{2,1,0:T(8,128)(2,1)S(1)}, bf16[5,128,128]{2,1,0:T(8,128)(2,1)S(1)}, bf16[4,128,128]{2,1,0:T(8,128)(2,1)S(1)}) custom-call(bf16[1056,128]{1,0:T(8,128)(2,1)S(1)} %collective-permute-done.pa, ...), custom_call_target="tpu_custom_call", output_to_operand_aliasing={{0}: (4, {}), {1}: (5, {}), {2}: (6, {})} | custom-call | flops 1073741824 | bytes 1000 | tf_op jit(solution)/shard_map/corner/pallas_call | solution.py:469
  16.0 2.6 %collective-permute-start.3 = (bf16[5,128,128]{2,1,0:T(8,128)(2,1)S(1)}, bf16[5,128,128]{2,1,0:T(8,128)(2,1)S(1)}, u32[]{:S(2)}, u32[]{:S(2)}) collective-permute-start(bf16[5,128,128]{2,1,0:T(8,128)(2,1)S(1)} %get-tuple-element.75), channel_id=1, source_target_pairs={{0,64},{64,0},{128,192},{192,128},{1,65},{65,1},{129,193},{193,129... | collective-permute-start | bytes 491528 | tf_op jit(solution)/shard_map/ppermute | solution.py:858
  18.6 0.1 collective-permute-start.4
  18.7 1.2 %beside.1 = (bf16[7,1280,256]{2,1,0:T(8,128)(2,1)S(1)}, bf16[320,1792]{1,0:T(8,128)(2,1)S(1)}, f32[3,256,256]{2,1,0:T(8,128)S(1)}, f32[7,256,256]{2,1,0:T(8,128)S(1)}, f32[320,768]{1,0:T(8,128)S(1)}) custom-call(bf16[2,256,1280]{2,1,0:T(8,128)(2,1)S(1)} %get-tuple-element.62.xb01, ...), custom_call_target="tpu_custom_call", output_to_operand_aliasing={{0}: (4, {})} | custom-call | flops 1000 | bytes 1000 | tf_op jit(solution)/shard_map/beside/pallas_call | solution.py:545
  19.9 0.0 collective-permute-done.4.swap_b
  19.9 0.0 collective-permute-done.3.swap_a
  20.0 1.2 %use_swapped.1 = (bf16[7,1280,256]{2,1,0:T(8,128)(2,1)S(1)}, bf16[320,1792]{1,0:T(8,128)(2,1)S(1)}, f32[320,256]{1,0:T(8,128)S(1)}, f32[320,1280]{1,0:T(8,128)S(1)}) custom-call(bf16[5,128,128]{2,1,0:T(8,128)(2,1)S(1)} %collective-permute-done.3.swap_a, bf16[4,128,128]{2,1,0:T(8,128)(2,1)S(1)} %collective-permute-done.4.swap_b, ...), custom_call_target="tpu_custom_call", output_to_operand_aliasing={{0}: (4, {})} | custom-call | flops 1000 | bytes 1000 | tf_op jit(solution)/shard_map/use_swapped/pallas_call | solution.py:601
  21.1 0.0 collective-permute-done.2.pb
  21.1 1.9 %middle.1 = (bf16[4,256,1280]{2,1,0:T(8,128)(2,1)S(1)}, bf16[4,256,1280]{2,1,0:T(8,128)(2,1)S(1)}, bf16[7,1280,256]{2,1,0:T(8,128)(2,1)S(1)}, bf16[320,1792]{1,0...) custom-call(bf16[1056,128]{1,0:T(8,128)(2,1)S(1)} %collective-permut, ...), custom_call_target="tpu_custom_call", output_to_operand_aliasing={{0}: (10, {}), {1}: (11, {}), {2}: (12, {}), {3}: (13, {})} | custom-call | flops 1000 | bytes 1000 | tf_op jit(solution)/shard_map/middle/pallas_call | solution.py:690
  23.1 0.0 collective-permute-done.1.pc
  23.1 1.3 %finish.1 = (bf16[4,256,1280]{2,1,0:T(8,128)(2,1)S(1)}, bf16[4,256,1280]{2,1,0:T(8,128)(2,1)S(1)}, bf16[7,1280,256]{2,1,0:T(8,128)(2,1)S(1)}, bf16[5,9,32,128]{3,2,1,0:T(8,128)(2,1)S(1)}) custom-call(bf16[1056,128]{1,0:T(8,128)(2,1)S(1)} %collective-permute-done.pa, ...), custom_call_target="tpu_custom_call", output_to_operand_aliasing={{0}: (9, {}), {1}: (10, {}), {2}: (11, {}), {3}: (12, {})} | custom-call | flops 1006632960 | bytes 4194304 | tf_op jit(solution)/shard_map/finish/pallas_call | solution.py:773
  24.4 0.5 %collective-permute-start.5 = (bf16[5,9,32,128]{3,2,1,0:T(8,128)(2,1)S(1)}, bf16[5,9,32,128]{3,2,1,0:T(8,128)(2,1)S(1)}, u32[]{:S(2)}, u32[]{:S(2)}) collective-permute-start(bf16[5,9,32,128]{3,2,1,0:T(8,128)(2,1)S(1)} %get-tuple-element.89), channel_id=1, source_target_pairs={{0,64},{64,0},{128,192},{192,128},{1,65},{65,1},{129,193},{193,129... | collective-permute-start | bytes 1105928 | tf_op jit(solution)/shard_map/ppermute | solution.py:866
  24.9 1.2 %put_keep.1 = (bf16[10,9,32,128]{3,2,1,0:T(8,128)(2,1)}, bf16[5,9,32,128]{3,2,1,0:T(8,128)(2,1)S(1)}) custom-call(f32[96,128]{1,0:T(8,128)S(1)} %get-tuple-element.56.mk, bf16[320,1792]{1,0:T(8,128)(2,1)S(1)} %get-tuple-element.70.left, f32[320,768]{1,0:T(8,128)S(1)} %get-tuple-element.71.s1p, ...), custom_call_target="tpu_custom_call", output_to_operand_aliasing={{1}: (5, {})} | custom-call | flops 1000 | bytes 1000 | tf_op jit(solution)/shard_map/put_keep/pallas_call | solution.py:811
  26.2 0.1 collective-permute-done.5.other
  26.2 0.8 %join.1 = bf16[10,9,32,128]{3,2,1,0:T(8,128)(2,1)} custom-call(bf16[5,9,32,128]{3,2,1,0:T(8,128)(2,1)S(1)} %collective-permute-done.5.other, bf16[10,9,32,128]{3,2,1,0:T(8,128)(2,1)} %get-tuple-element.92.out_in), custom_call_target="tpu_custom_call", output_to_operand_aliasing={{}: (1, {})} | custom-call | tf_op jit(solution)/shard_map/join/pallas_call | solution.py:825
  (1 shorter events, 0.0 us)
Async XLA Ops:
  7.5 7.0 %collective-permute-start = (bf16[1056,128]{1,0:T(8,128)(2,1)S(1)}, bf16[1056,128]{1,0:T(8,128)(2,1)S(1)}, u32[]{:S(2)}, u32[]{:S(2)}) collective-permute-start(bf16[1056,128]{1,0:T(8,128)(2,1)S(1)} %get-tuple-element.49), channel_id=1, source_target_pairs={{0,1},{1,2},{2,3},{3,4},{4,5},{5,6},{6,7},{7,8},{8,9},{9,10},{10,1... | collective-permute-start | bytes 811016 | tf_op jit(solution)/shard_map/ppermute | solution.py:852
  11.2 9.9 %collective-permute-start.2 = (bf16[1280,128]{1,0:T(8,128)(2,1)S(1)}, bf16[1280,128]{1,0:T(8,128)(2,1)S(1)}, u32[]{:S(2)}, u32[]{:S(2)}) collective-permute-start(bf16[1280,128]{1,0:T(8,128)(2,1)S(1)} %get-tuple-element.72), channel_id=1, source_target_pairs={{0,1},{1,2},{2,3},{3,4},{4,5},{5,6},{6,7},{7,8},{8,9},{9,10},{10,1... | collective-permute-start | bytes 983048 | tf_op jit(solution)/shard_map/ppermute | solution.py:854
  13.6 9.5 %collective-permute-start.1 = (bf16[1040,128]{1,0:T(8,128)(2,1)S(1)}, bf16[1040,128]{1,0:T(8,128)(2,1)S(1)}, u32[]{:S(2)}, u32[]{:S(2)}) collective-permute-start(bf16[1040,128]{1,0:T(8,128)(2,1)S(1)} %get-tuple-element.54), channel_id=1, source_target_pairs={{0,1},{1,2},{2,3},{3,4},{4,5},{5,6},{6,7},{7,8},{8,9},{9,10},{10,1... | collective-permute-start | bytes 798728 | tf_op jit(solution)/shard_map/ppermute | solution.py:855
  16.0 3.9 %collective-permute-start.3 = (bf16[5,128,128]{2,1,0:T(8,128)(2,1)S(1)}, bf16[5,128,128]{2,1,0:T(8,128)(2,1)S(1)}, u32[]{:S(2)}, u32[]{:S(2)}) collective-permute-start(bf16[5,128,128]{2,1,0:T(8,128)(2,1)S(1)} %get-tuple-element.75), channel_id=1, source_target_pairs={{0,64},{64,0},{128,192},{192,128},{1,65},{65,1},{129,193},{193,129... | collective-permute-start | bytes 491528 | tf_op jit(solution)/shard_map/ppermute | solution.py:858
  18.6 1.3 %collective-permute-start.4 = (bf16[4,128,128]{2,1,0:T(8,128)(2,1)S(1)}, bf16[4,128,128]{2,1,0:T(8,128)(2,1)S(1)}, u32[]{:S(2)}, u32[]{:S(2)}) collective-permute-start(bf16[4,128,128]{2,1,0:T(8,128)(2,1)S(1)} %get-tuple-element.76), channel_id=1, source_target_pairs={{0,64},{64,0},{128,192},{192,128},{1,65},{65,1},{129,193},{193,129... | collective-permute-start | bytes 393224 | tf_op jit(solution)/shard_map/ppermute | solution.py:859
  24.4 1.8 %collective-permute-start.5 = (bf16[5,9,32,128]{3,2,1,0:T(8,128)(2,1)S(1)}, bf16[5,9,32,128]{3,2,1,0:T(8,128)(2,1)S(1)}, u32[]{:S(2)}, u32[]{:S(2)}) collective-permute-start(bf16[5,9,32,128]{3,2,1,0:T(8,128)(2,1)S(1)} %get-tuple-element.89), channel_id=1, source_target_pairs={{0,64},{64,0},{128,192},{192,128},{1,65},{65,1},{129,193},{193,129... | collective-permute-start | bytes 1105928 | tf_op jit(solution)/shard_map/ppermute | solution.py:866
